TPU v7x, 32 devices: a whole 2x2x4 slice. The times are simulated.
32 devices in a mesh: section: 4 (over y, x), rows: 8 (over z, core).
Axes of the slice: x: 2, y: 2, z: 4, core: 2. Of those that a mesh axis runs over, the one named last changes fastest.
Arguments:
- inputs: bfloat16 [4, 2, 512, 2000], P('section', None, 'rows'), may hold values from -6 to 6
- resets: int32 [4, 2, 512], P(None, None, 'rows'), may hold values from 0 to 1, as said below
- valid_mask: int32 [4, 2, 512], P(None, None, 'rows'), may hold values from 0 to 1, as said below
- weights: bfloat16 [4, 2000, 2000], P('section'), may hold values from -0.125 to 0.125
- recurrence: float32 [4, 2000], P('section'), may hold values from 0.7 to 0.99
- state_bias: float32 [4, 2000], P('section'), may hold values from -3 to 3
- norm_gain: float32 [4, 2000], P('section'), may hold values from 0.2 to 0.8
- norm_shift: float32 [4, 2000], P('section'), may hold values from -3 to 3
- cotangent: bfloat16 [4, 2, 512, 2000], P('section', None, 'rows'), may hold values from -6 to 6
Outputs:
- outputs: bfloat16 [4, 2, 512, 2000], P('section', None, 'rows')
- grad_inputs: bfloat16 [4, 2, 512, 2000], P('section', None, 'rows')
- grad_weights: float32 [4, 2000, 2000], P('section')
- grad_recurrence: float32 [4, 2000], P('section')
- grad_bias: float32 [4, 2000], P('section')
- grad_gain: float32 [4, 2000], P('section')
- grad_shift: float32 [4, 2000], P('section')
Inputs may be any that keep to these rules, and one draw needn't show every extreme that they name: `resets`: 1 marks the first frame of a clip, where the state restarts from zero; frame 0 of every sequence is 1, and in every micro-batch one sequence has no other 1. `valid_mask`: 1 marks a valid frame; frame 0 of every sequence is valid.
All inputs are finite; a program needn't handle non-finite values.
Results may differ from a plain program's by a relative error of at most 0.011.
Values may be sent and summed in bfloat16 or wider, within the bound.
A program may use at most 320 MiB of HBM per device.

v0:
```python
import jax
import jax.numpy as jnp
from jax import lax
from jax.sharding import PartitionSpec as P

norm_eps = 1e-05
block_frames = 8


def carried_in(value, axis, join, neutral, backward):
    count, mine = (lax.axis_size(axis), lax.axis_index(axis))
    pieces = jax.tree.map(lambda part: lax.all_gather(part, axis), value)
    if backward:
        pieces = jax.tree.map(lambda part: part[::-1], pieces)
        mine = count - 1 - mine
    subtotal = jax.tree.map(
        lambda part, zero: jnp.full_like(part, 0) + jnp.asarray(zero, part.dtype), value, neutral
    )

    def hop(position, subtotal):
        longer = join(subtotal, jax.tree.map(lambda part: part[position], pieces))
        return jax.tree.map(lambda new, old: jnp.where(position < mine, new, old), longer, subtotal)

    return lax.fori_loop(0, count - 1, hop, subtotal)


def from_behind(block, axis, distance):
    devices = range(lax.axis_size(axis))
    route = [(i - distance, i) for i in devices if i - distance in devices]
    return lax.ppermute(block, axis, route)


def decay_combine(earlier, latter):
    return (earlier[0] * latter[0], latter[0] * earlier[1] + latter[1])


def block_recur(decays, drives, reverse):
    seq_count, frame_count, width = drives.shape
    block_count = frame_count // block_frames
    decay_blocks = jnp.swapaxes(decays.reshape(seq_count, block_count, block_frames, width), 0, 1)
    drive_blocks = jnp.swapaxes(drives.reshape(seq_count, block_count, block_frames, width), 0, 1)

    def advance(carry, blocks):
        factor, value = carry
        block_decay, block_drive = blocks
        factor_list = [None] * block_frames
        value_list = [None] * block_frames
        order = range(block_frames - 1, -1, -1) if reverse else range(block_frames)
        for inner in order:
            factor = block_decay[:, inner] * factor
            value = block_decay[:, inner] * value + block_drive[:, inner]
            factor_list[inner] = factor
            value_list[inner] = value
        return ((factor, value), (jnp.stack(factor_list, 1), jnp.stack(value_list, 1)))

    start = (jnp.ones((seq_count, width), jnp.float32), jnp.zeros((seq_count, width), jnp.float32))
    unused_carry, (factor_all, value_all) = lax.scan(
        advance, start, (decay_blocks, drive_blocks), reverse=reverse
    )
    factor_all = jnp.swapaxes(factor_all, 0, 1).reshape(seq_count, frame_count, width)
    value_all = jnp.swapaxes(value_all, 0, 1).reshape(seq_count, frame_count, width)
    return (factor_all, value_all)


def silu_slope(value):
    sigma = jax.nn.sigmoid(value)
    return sigma * (1.0 + value * (1.0 - sigma))


def place_slot(buffer, value, slot_index, active):
    previous = lax.dynamic_index_in_dim(buffer, slot_index, 0, keepdims=False)
    chosen = jnp.where(active, value.astype(buffer.dtype), previous)
    return lax.dynamic_update_index_in_dim(buffer, chosen, slot_index, 0)


def take_slot(buffer, slot_index):
    return lax.dynamic_index_in_dim(buffer, slot_index, 0, keepdims=False)


def row_moments(projected, valid_rows):
    total_sum, frame_count = lax.psum(
        (jnp.sum(projected * valid_rows, axis=(0, 1)), jnp.sum(valid_rows)), "rows"
    )
    row_mean = total_sum / frame_count
    centred = projected - row_mean
    spread = lax.psum(jnp.sum(centred * centred * valid_rows, axis=(0, 1)), "rows") / frame_count
    return (row_mean, lax.rsqrt(spread + norm_eps), frame_count)


def layer_forward(
    layer_input, weight, rate_vec, bias_vec, gain_vec, shift_vec, reset_rows, valid_rows
):
    projected = jnp.einsum("sfh,hk->sfk", layer_input, weight, preferred_element_type=jnp.float32)
    row_mean, inv_spread, frame_count = row_moments(projected, valid_rows)
    normed = (projected - row_mean) * inv_spread
    drive_term = gain_vec * normed + shift_vec
    decay_rate = rate_vec * (1 - reset_rows).astype(jnp.float32)[..., None]
    local_a, local_b = block_recur(decay_rate, drive_term, False)
    identity_pair = (jnp.ones_like(local_a[:, 0]), jnp.zeros_like(local_b[:, 0]))
    before_a, before_b = carried_in(
        (local_a[:, -1], local_b[:, -1]), "rows", decay_combine, identity_pair, False
    )
    states = local_a * before_b[:, None] + local_b
    hidden = valid_rows * jax.nn.silu(states + bias_vec)
    return (hidden, (normed, states, before_b, inv_spread, frame_count))


def layer_backward(
    grad_hidden,
    layer_input,
    weight,
    rate_vec,
    bias_vec,
    gain_vec,
    reset_rows,
    valid_rows,
    kept_vals,
):
    normed, states, carried, inv_spread, frame_count = kept_vals
    keep_state = (1 - reset_rows).astype(jnp.float32)[..., None]
    decay_rate = rate_vec * keep_state
    grad_pre = grad_hidden * valid_rows * silu_slope(states + bias_vec)
    back_a, back_b = block_recur(decay_rate, decay_rate * grad_pre, True)
    identity_pair = (jnp.ones_like(back_a[:, 0]), jnp.zeros_like(back_b[:, 0]))
    after_a, after_b = carried_in(
        (back_a[:, 0], back_b[:, 0]), "rows", decay_combine, identity_pair, True
    )
    passed = back_a * after_b[:, None] + back_b
    next_passed = jnp.concatenate([passed[:, 1:], after_b[:, None]], axis=1)
    grad_state = grad_pre + next_passed
    previous = jnp.concatenate([carried[:, None], states[:, :-1]], axis=1)
    grad_rate = jnp.sum(grad_state * keep_state * previous, axis=(0, 1))
    grad_bias = jnp.sum(grad_pre, axis=(0, 1))
    sum_shift, sum_gain = lax.psum(
        (jnp.sum(grad_state, axis=(0, 1)), jnp.sum(grad_state * normed, axis=(0, 1))), "rows"
    )
    grad_proj = (
        gain_vec
        * inv_spread
        * (grad_state - valid_rows / frame_count * (sum_shift + normed * sum_gain))
    )
    grad_low = grad_proj.astype(jnp.bfloat16)
    grad_weight = jnp.einsum(
        "sfh,sfk->hk", layer_input, grad_low, preferred_element_type=jnp.float32
    )
    grad_input = jnp.einsum("sfk,hk->sfh", grad_low, weight, preferred_element_type=jnp.float32)
    return (grad_input, grad_weight, grad_rate, grad_bias, sum_shift, sum_gain)


def local(
    inputs, resets, valid_mask, weights, recurrence, state_bias, norm_gain, norm_shift, cotangent
):
    section_count = lax.axis_size("section")
    section_index = lax.axis_index("section")
    is_even = section_index % 2 == 0
    is_first = section_index == 0
    is_last = section_index == section_count - 1
    all_inputs, all_cotangent = (
        lax.all_gather(inputs, "section", axis=0, tiled=True),
        lax.all_gather(cotangent, "section", axis=0, tiled=True),
    )
    batches = all_inputs.shape[0]
    rounds = batches + section_count - 1
    weight = weights[0]
    rate_vec = recurrence[0]
    bias_vec = state_bias[0]
    gain_vec = norm_gain[0]
    shift_vec = norm_shift[0]
    valid_all = valid_mask.astype(jnp.float32)[..., None]
    blank = jnp.zeros(all_inputs.shape[1:], jnp.bfloat16)
    stash = jnp.zeros_like(all_inputs)
    out_store = jnp.zeros_like(all_inputs)
    normed_store = jnp.zeros(all_inputs.shape, jnp.float32)
    states_store = jnp.zeros(all_inputs.shape, jnp.float32)
    carry_store = jnp.zeros((batches, all_inputs.shape[1], all_inputs.shape[3]), jnp.float32)
    scale_store = jnp.zeros((batches, all_inputs.shape[3]), jnp.float32)
    count_store = jnp.zeros((batches,), jnp.float32)
    recv_main, recv_side = (blank, blank)
    for step_number in range(rounds):
        micro_index = step_number - section_index
        active = (micro_index >= 0) & (micro_index < batches)
        slot_index = jnp.clip(micro_index, 0, batches - 1)
        own_input = take_slot(all_inputs, slot_index)
        layer_input = jnp.where(is_first, own_input, recv_main)
        reset_rows = take_slot(resets, slot_index)
        valid_rows = take_slot(valid_all, slot_index)
        hidden, kept_vals = layer_forward(
            layer_input, weight, rate_vec, bias_vec, gain_vec, shift_vec, reset_rows, valid_rows
        )
        merged = (recv_side.astype(jnp.float32) + hidden).astype(jnp.bfloat16)
        send_main = jnp.where(is_even, hidden.astype(jnp.bfloat16), merged)
        send_side = jnp.where(is_even, layer_input, blank)
        stash = place_slot(stash, layer_input, slot_index, active)
        out_store = place_slot(out_store, merged, slot_index, active & is_last)
        normed_store = place_slot(normed_store, kept_vals[0], slot_index, active)
        states_store = place_slot(states_store, kept_vals[1], slot_index, active)
        carry_store = place_slot(carry_store, kept_vals[2], slot_index, active)
        scale_store = place_slot(scale_store, kept_vals[3], slot_index, active)
        count_store = place_slot(count_store, kept_vals[4], slot_index, active)
        if step_number + 1 < rounds:
            recv_main, recv_side = from_behind((send_main, send_side), "section", 1)
    grad_weight_sum = jnp.zeros(weight.shape, jnp.float32)
    grad_rate_sum = jnp.zeros(rate_vec.shape, jnp.float32)
    grad_bias_sum = jnp.zeros(rate_vec.shape, jnp.float32)
    gain_sum = jnp.zeros(rate_vec.shape, jnp.float32)
    shift_sum = jnp.zeros(rate_vec.shape, jnp.float32)
    grad_store = jnp.zeros_like(all_inputs)
    back_main, back_side = (blank, blank)
    for step_number in range(rounds):
        micro_index = step_number - (section_count - 1 - section_index)
        active = (micro_index >= 0) & (micro_index < batches)
        slot_index = jnp.clip(micro_index, 0, batches - 1)
        layer_input = take_slot(stash, slot_index)
        reset_rows = take_slot(resets, slot_index)
        valid_rows = take_slot(valid_all, slot_index)
        kept_vals = (
            take_slot(normed_store, slot_index),
            take_slot(states_store, slot_index),
            take_slot(carry_store, slot_index),
            take_slot(scale_store, slot_index),
            take_slot(count_store, slot_index),
        )
        top_grad = take_slot(all_cotangent, slot_index)
        grad_hidden = jnp.where(is_last, top_grad, back_main).astype(jnp.float32)
        grad_hidden = jnp.where(active, grad_hidden, 0.0)
        grad_input, grad_weight, grad_rate, grad_bias, sum_shift, sum_gain = layer_backward(
            grad_hidden,
            layer_input,
            weight,
            rate_vec,
            bias_vec,
            gain_vec,
            reset_rows,
            valid_rows,
            kept_vals,
        )
        grad_weight_sum = grad_weight_sum + grad_weight
        grad_rate_sum = grad_rate_sum + grad_rate
        grad_bias_sum = grad_bias_sum + grad_bias
        gain_sum = gain_sum + sum_gain
        shift_sum = shift_sum + sum_shift
        total_grad = grad_input + jnp.where(is_even, back_side.astype(jnp.float32), 0.0)
        send_main = total_grad.astype(jnp.bfloat16)
        send_side = jnp.where(is_even, blank, grad_hidden.astype(jnp.bfloat16))
        grad_store = place_slot(grad_store, send_main, slot_index, active & is_first)
        if step_number + 1 < rounds:
            back_main, back_side = from_behind((send_main, send_side), "section", -1)
    grad_weight_sum, grad_bias_sum, grad_rate_sum = lax.psum(
        (grad_weight_sum, grad_bias_sum, grad_rate_sum), "rows"
    )
    out_total, grad_total = (
        lax.psum_scatter(
            out_store.astype(jnp.float32).astype(jnp.bfloat16),
            "section",
            scatter_dimension=0,
            tiled=True,
        ).astype(jnp.float32),
        lax.psum_scatter(
            grad_store.astype(jnp.float32).astype(jnp.bfloat16),
            "section",
            scatter_dimension=0,
            tiled=True,
        ).astype(jnp.float32),
    )
    return (
        out_total.astype(jnp.bfloat16),
        grad_total.astype(jnp.bfloat16),
        grad_weight_sum[None],
        grad_rate_sum[None],
        grad_bias_sum[None],
        gain_sum[None],
        shift_sum[None],
    )


def solution(mesh):
    return jax.shard_map(
        local,
        mesh=mesh,
        in_specs=(
            P("section", None, "rows", None),
            P(None, None, "rows"),
            P(None, None, "rows"),
            P("section", None, None),
            P("section", None),
            P("section", None),
            P("section", None),
            P("section", None),
            P("section", None, "rows", None),
        ),
        out_specs=(
            P("section", None, "rows", None),
            P("section", None, "rows", None),
            P("section", None, None),
            P("section", None),
            P("section", None),
            P("section", None),
            P("section", None),
        ),
        check_vma=False,
    )
```

profile of v0, /device:TPU:0, one launch (start us, length us, event | category | flops | bytes accessed | tf_op | source)
XLA Modules:
  0.0 2266.1 jit_solution(8346779562956341166)
XLA Ops:
  22.9 25.0 %all-gather.31.cloned.1.call-done = bf16[4,2,64,2000]{3,2,1,0:T(8,128)(2,1)} async-done(((bf16[1,2,64,2000]{3,2,1,0:T(8,128)(2,1)}), bf16[4,2,64,2000]{3,2,1,0:T(8,128)(2,1)}) %all-gather.31.cloned.1.call-update) | async-done | bytes 2048016 | tf_op jit(solution)/shard_map/all_gather | solution.py:159
  52.7 17.5 all-reduce.15
  98.0 23.5 %while.462 = (s32[]{:T(128)}, f32[2,2000]{1,0:T(2,128)S(1)}, f32[2,2000]{1,0:T(2,128)S(1)}, f32[8,2,8,2000]{3,1,2,0:T(2,128)}, f32[8,2,8,2000]{3,1,2,0:T(2,128)S...) while((s32[]{:T(128)}, f32[2,2000]{1,0:T(2,128)S(1)}, ...), condition=%wide.region_7.8_spmd.clone, body=%wide.region_6.7_spmd.clone.sunk | while | flops 148001 | bytes 2280444 | solution.py:57
  140.6 14.2 all-gather.1
  189.7 14.7 all-reduce.14
  230.8 23.5 %while.464 = (s32[]{:T(128)}, f32[2,2000]{1,0:T(2,128)S(1)}, f32[2,2000]{1,0:T(2,128)S(1)}, f32[8,2,8,2000]{3,1,2,0:T(2,128)}, f32[8,2,8,2000]{3,1,2,0:T(2,128)S...) while((s32[]{:T(128)}, f32[2,2000]{1,0:T(2,128)S(1)}, ...), condition=%wide.region_17.18_spmd.clone, body=%wide.region_16.17_spmd.clone.sunk | while | flops 148001 | bytes 2280444 | solution.py:57
  266.3 14.4 all-gather.2
  283.9 14.0 all-gather.3
  331.8 14.8 all-reduce.13
  374.3 23.6 %while.466 = (s32[]{:T(128)}, f32[2,2000]{1,0:T(2,128)S(1)}, f32[2,2000]{1,0:T(2,128)S(1)}, f32[8,2,8,2000]{3,1,2,0:T(2,128)}, f32[8,2,8,2000]{3,1,2,0:T(2,128)S...) while((s32[]{:T(128)}, f32[2,2000]{1,0:T(2,128)S(1)}, ...), condition=%wide.region_27.28_spmd.clone, body=%wide.region_26.27_spmd.clone.sunk | while | flops 148001 | bytes 2280444 | solution.py:57
  399.7 14.0 all-gather.4
  416.9 14.0 all-gather.5
  464.6 14.8 all-reduce.12
  507.2 23.5 %while.468 = (s32[]{:T(128)}, f32[2,2000]{1,0:T(2,128)S(1)}, f32[2,2000]{1,0:T(2,128)S(1)}, f32[8,2,8,2000]{3,1,2,0:T(2,128)}, f32[8,2,8,2000]{3,1,2,0:T(2,128)S...) while((s32[]{:T(128)}, f32[2,2000]{1,0:T(2,128)S(1)}, ...), condition=%wide.region_37.38_spmd.clone, body=%wide.region_36.37_spmd.clone.sunk | while | flops 148001 | bytes 2280444 | solution.py:57
  549.8 14.0 all-gather.7
  597.9 14.8 all-reduce.11
  639.6 23.6 %while.470 = (s32[]{:T(128)}, f32[2,2000]{1,0:T(2,128)S(1)}, f32[2,2000]{1,0:T(2,128)S(1)}, f32[8,2,8,2000]{3,1,2,0:T(2,128)}, f32[8,2,8,2000]{3,1,2,0:T(2,128)S...) while((s32[]{:T(128)}, f32[2,2000]{1,0:T(2,128)S(1)}, ...), condition=%wide.region_47.48_spmd.clone, body=%wide.region_46.47_spmd.clone.sunk | while | flops 148001 | bytes 2280444 | solution.py:57
  665.0 14.0 all-gather.8
  682.2 14.0 all-gather.9
  730.4 14.8 all-reduce.10
  772.6 23.5 %while.472 = (s32[]{:T(128)}, f32[2,2000]{1,0:T(2,128)S(1)}, f32[2,2000]{1,0:T(2,128)S(1)}, f32[8,2,8,2000]{3,1,2,0:T(2,128)}, f32[8,2,8,2000]{3,1,2,0:T(2,128)S...) while((s32[]{:T(128)}, f32[2,2000]{1,0:T(2,128)S(1)}, ...), condition=%wide.region_57.58_spmd.clone, body=%wide.region_56.57_spmd.clone.sunk | while | flops 148001 | bytes 2280444 | solution.py:57
  815.1 14.2 all-gather.11
  863.0 14.7 all-reduce.9
  906.5 23.9 %while.474 = (s32[]{:T(128)}, f32[2,2000]{1,0:T(2,128)S(1)}, f32[2,2000]{1,0:T(2,128)S(1)}, f32[8,2,8,2000]{3,1,2,0:T(2,128)}, f32[8,2,8,2000]{3,1,2,0:T(2,128)}...) while((s32[]{:T(128)}, f32[2,2000]{1,0:T(2,128)S(1)}, ...), condition=%wide.region_67.68_spmd.clone, body=%wide.region_66.67_spmd.clone.sunk | while | flops 148001 | bytes 2274300 | solution.py:57
  932.3 14.4 all-gather.12
  951.2 14.0 all-gather.13
  982.3 23.9 %while.476 = (s32[]{:T(128)}, f32[2,2000]{1,0:T(2,128)S(1)}, f32[2,2000]{1,0:T(2,128)S(1)}, f32[8,2,8,2000]{3,1,2,0:T(2,128)}, f32[8,2,8,2000]{3,1,2,0:T(2,128)S...) while((s32[]{:T(128)}, f32[2,2000]{1,0:T(2,128)S(1)}, ...), condition=%wide.region_72.73_spmd.clone, body=%wide.region_71.72_spmd.clone.sunk | while | flops 148002 | bytes 2478480 | solution.py:57
  1024.4 14.0 all-gather.14
  1060.3 26.1 %all-reduce.8 = (f32[2000]{0:T(1024)S(1)}, f32[2000]{0:T(1024)S(1)}) all-reduce(f32[2000]{0:T(1024)S(1)} %get-tuple-element.3231, f32[2000]{0:T(1024)S(1)} %get-tuple-element.3232), channel_id=1, replica_groups=mesh['section'=4,'rows'=8] {'rows'}, use_global_device_ids=true, to_apply=%region_78.79 | all-reduce | flops 4000 | bytes 32000 | tf_op jit(solution)/shard_map/psum | solution.py:134
  1117.6 23.4 %while.478 = (s32[]{:T(128)}, f32[2,2000]{1,0:T(2,128)S(1)}, f32[2,2000]{1,0:T(2,128)S(1)}, f32[8,2,8,2000]{3,1,2,0:T(2,128)}, f32[8,2,8,2000]{3,1,2,0:T(2,128)}...) while((s32[]{:T(128)}, f32[2,2000]{1,0:T(2,128)S(1)}, ...), condition=%wide.region_80.81_spmd.clone, body=%wide.region_79.80_spmd.clone.sunk | while | flops 148002 | bytes 2216336 | solution.py:57
  1190.1 28.2 %all-reduce.7 = (f32[2000]{0:T(1024)S(1)}, f32[2000]{0:T(1024)S(1)}) all-reduce(f32[2000]{0:T(1024)S(1)} %get-tuple-element.3228, f32[2000]{0:T(1024)S(1)} %get-tuple-element.3229), channel_id=1, replica_groups=mesh['section'=4,'rows'=8] {'rows'}, use_global_device_ids=true, to_apply=%region_86.87 | all-reduce | flops 4000 | bytes 32000 | tf_op jit(solution)/shard_map/psum | solution.py:134
  1250.5 23.4 %while.480 = (s32[]{:T(128)}, f32[2,2000]{1,0:T(2,128)S(1)}, f32[2,2000]{1,0:T(2,128)S(1)}, f32[8,2,8,2000]{3,1,2,0:T(2,128)}, f32[8,2,8,2000]{3,1,2,0:T(2,128)}...) while((s32[]{:T(128)}, f32[2,2000]{1,0:T(2,128)S(1)}, ...), condition=%wide.region_88.89_spmd.clone, body=%wide.region_87.88_spmd.clone.sunk | while | flops 148002 | bytes 2216336 | solution.py:57
  1294.0 14.4 all-gather.18
  1319.5 26.9 %all-reduce.6 = (f32[2000]{0:T(1024)S(1)}, f32[2000]{0:T(1024)S(1)}) all-reduce(f32[2000]{0:T(1024)S(1)} %get-tuple-element.3234, f32[2000]{0:T(1024)S(1)} %get-tuple-element.3235), channel_id=1, replica_groups=mesh['section'=4,'rows'=8] {'rows'}, use_global_device_ids=true, to_apply=%region_94.95 | all-reduce | flops 4000 | bytes 32000 | tf_op jit(solution)/shard_map/psum | solution.py:134
  1378.9 23.5 %while.482 = (s32[]{:T(128)}, f32[2,2000]{1,0:T(2,128)S(1)}, f32[2,2000]{1,0:T(2,128)S(1)}, f32[8,2,8,2000]{3,1,2,0:T(2,128)}, f32[8,2,8,2000]{3,1,2,0:T(2,128)}...) while((s32[]{:T(128)}, f32[2,2000]{1,0:T(2,128)S(1)}, ...), condition=%wide.region_96.97_spmd.clone, body=%wide.region_95.96_spmd.clone.sunk | while | flops 148002 | bytes 2216336 | solution.py:57
  1422.5 14.1 all-gather.20
  1451.9 26.9 %all-reduce.5 = (f32[2000]{0:T(1024)S(1)}, f32[2000]{0:T(1024)S(1)}) all-reduce(f32[2000]{0:T(1024)S(1)} %get-tuple-element.3237, f32[2000]{0:T(1024)S(1)} %get-tuple-element.3238), channel_id=1, replica_groups=mesh['section'=4,'rows'=8] {'rows'}, use_global_device_ids=true, to_apply=%region_102.103 | all-reduce | flops 4000 | bytes 32000 | tf_op jit(solution)/shard_map/psum | solution.py:134
  1511.8 23.3 %while.484 = (s32[]{:T(128)}, f32[2,2000]{1,0:T(2,128)S(1)}, f32[2,2000]{1,0:T(2,128)S(1)}, f32[8,2,8,2000]{3,1,2,0:T(2,128)}, f32[8,2,8,2000]{3,1,2,0:T(2,128)}...) while((s32[]{:T(128)}, f32[2,2000]{1,0:T(2,128)S(1)}, ...), condition=%wide.region_104.105_spmd.clone, body=%wide.region_103.104_spmd.clone.sunk | while | flops 148002 | bytes 2216336 | solution.py:57
  1540.2 14.2 all-gather.23
  1580.6 26.1 %all-reduce.4 = (f32[2000]{0:T(1024)S(1)}, f32[2000]{0:T(1024)S(1)}) all-reduce(f32[2000]{0:T(1024)S(1)} %get-tuple-element.3240, f32[2000]{0:T(1024)S(1)} %get-tuple-element.3241), channel_id=1, replica_groups=mesh['section'=4,'rows'=8] {'rows'}, use_global_device_ids=true, to_apply=%region_110.111 | all-reduce | flops 4000 | bytes 32000 | tf_op jit(solution)/shard_map/psum | solution.py:134
  1638.2 23.4 %while.486 = (s32[]{:T(128)}, f32[2,2000]{1,0:T(2,128)S(1)}, f32[2,2000]{1,0:T(2,128)S(1)}, f32[8,2,8,2000]{3,1,2,0:T(2,128)}, f32[8,2,8,2000]{3,1,2,0:T(2,128)}...) while((s32[]{:T(128)}, f32[2,2000]{1,0:T(2,128)S(1)}, ...), condition=%wide.region_112.113_spmd.clone, body=%wide.region_111.112_spmd.clone.sunk | while | flops 148002 | bytes 2216336 | solution.py:57
  1666.7 14.4 all-gather.25
  1711.3 27.0 %all-reduce.3 = (f32[2000]{0:T(1024)S(1)}, f32[2000]{0:T(1024)S(1)}) all-reduce(f32[2000]{0:T(1024)S(1)} %get-tuple-element.3243, f32[2000]{0:T(1024)S(1)} %get-tuple-element.3244), channel_id=1, replica_groups=mesh['section'=4,'rows'=8] {'rows'}, use_global_device_ids=true, to_apply=%region_118.119 | all-reduce | flops 4000 | bytes 32000 | tf_op jit(solution)/shard_map/psum | solution.py:134
  1771.7 23.4 %while.488 = (s32[]{:T(128)}, f32[2,2000]{1,0:T(2,128)S(1)}, f32[2,2000]{1,0:T(2,128)S(1)}, f32[8,2,8,2000]{3,1,2,0:T(2,128)}, f32[8,2,8,2000]{3,1,2,0:T(2,128)}...) while((s32[]{:T(128)}, f32[2,2000]{1,0:T(2,128)S(1)}, ...), condition=%wide.region_120.121_spmd.clone, body=%wide.region_119.120_spmd.clone.sunk | while | flops 148002 | bytes 2216336 | solution.py:57
  1814.6 14.2 all-gather.26
  1835.3 26.7 %all-reduce.2 = (f32[2000]{0:T(1024)S(1)}, f32[2000]{0:T(1024)S(1)}, f32[1,2000]{1,0:T(1,128)}, f32[1,2000]{1,0:T(1,128)}) all-reduce(f32[2000]{0:T(1024)S(1)} %get-tuple-element.3246, f32[2000]{0:T(1024)S(1)} %get-tuple-element.3247, f32[1,2000]{1,0:T(1,128)S(1)} %bitcast.4745, ...), channel_id=1, replica_groups=mesh['section'=4,'rows'=8] {'rows'}, use_global_device_ids=true, to_apply=%region_126.127 | all-reduce | flops 8000 | bytes 64000 | tf_op jit(solution)/shard_map/psum | solution.py:134
  1880.7 38.5 %fusion.224 = f32[1,2000,2000]{2,1,0:T(8,128)} fusion(f32[2000,2000,1]{1,0,2:T(8,128)} %fusion.341, f32[2000,2000,1]{1,0,2:T(8,128)} %fusion.343, f32[2000,2000,1]{1,0,2:T(8,128)} %fusion.345, f32[2000,2000,1]{1,0,2:T(8,128)} %fusion.347, f32[2000,2000,1]{1,0,2:T(8,128)} %fusion.349, f32[2000,2000,1]{1,0,2:T(8,128)} %fusion.338, ...), kind=kOutput, calls=%fused_computation.786 | convolution fusion | flops 1048000000 | bytes 113048576 | tf_op jit(solution)/shard_map/sfh,sfk->hk/dot_general | solution.py:143
  1921.3 326.2 %all-reduce.18.cloned.1.call-done = f32[1,2000,2000]{2,1,0:T(8,128)} async-done(((f32[1,2000,2000]{2,1,0:T(8,128)}), f32[1,2000,2000]{2,1,0:T(8,128)}) %all-reduce.18.cloned.1.call-update) | async-done | bytes 16000016 | tf_op jit(solution)/shard_map/psum | solution.py:248
  (3048 shorter events, 1374.1 us)
Async XLA Ops:
  7.2 40.7 %all-gather.31.cloned.1.call-start = ((), (), s32[]{:S(2)}) async-start(), calls=%async_computation.2 | async-start | bytes 2621440 | tf_op jit(solution)/shard_map/all_gather | solution.py:159
  7.9 969.4 %all-gather.33.cloned.1.call-start = ((), (), s32[]{:S(2)}) async-start(), calls=%async_computation.3 | async-start | bytes 2621440 | tf_op jit(solution)/shard_map/all_gather | solution.py:160
  8.6 1912.6 %reduce-scatter.7.cloned.1.call-start = ((), (), s32[]{:S(2)}) async-start(), calls=%async_computation.5 | async-start | bytes 2621440
  11.3 61.0 %copy-start.172 = (f32[2,64]{1,0:T(2,128)}, f32[2,64]{1,0:T(2,128)S(1)}, u32[]{:S(2)}) copy-start(f32[2,64]{1,0:T(2,128)S(1)} %get-tuple-element.4058) | copy-start | bytes 1540
  121.5 40.6 %copy-start.51 = (f32[1,2000]{1,0:T(1,128)S(1)}, f32[1,2000]{1,0:T(1,128)}, u32[]{:S(2)}) copy-start(f32[1,2000]{1,0:T(1,128)} %param.70) | copy-start | bytes 24004
  121.5 40.6 %copy-start.173 = (f32[2,64]{1,0:T(2,128)S(1)}, f32[2,64]{1,0:T(2,128)}, u32[]{:S(2)}) copy-start(f32[2,64]{1,0:T(2,128)} %copy-done.172) | copy-start | bytes 1540
  170.2 15.3 collective-permute-start.1
  254.3 50.8 %copy-start.119 = (f32[1,2,2000]{2,0,1:T(1,128)S(1)}, f32[1,2,2000]{2,0,1:T(1,128)}, u32[]{:S(2)}) copy-start(f32[1,2,2000]{2,0,1:T(1,128)} %constant_dynamic-slice_fusion.7) | copy-start | bytes 48004
  255.0 184.2 %collective-permute-start.2 = (bf16[2,64,2000]{2,1,0:T(8,128)(2,1)}, bf16[2,64,2000]{2,1,0:T(8,128)(2,1)}, u32[]{:S(2)}, u32[]{:S(2)}) collective-permute-start(bf16[2,64,2000]{2,1,0:T(8,128)(2,1)} %broadcast_select_fusion.4), channel_id=1, source_target_pairs={{0,8},{8,16},{16,24},{1,9},{9,17},{17,25},{2,10},{10,18},{18,26},{... | collective-permute-start | bytes 1536008 | tf_op jit(solution)/shard_map/ppermute | solution.py:30
  260.1 52.1 %collective-permute-start = (bf16[2,64,2000]{2,1,0:T(8,128)(2,1)}, bf16[2,64,2000]{2,1,0:T(8,128)(2,1)}, u32[]{:S(2)}, u32[]{:S(2)}) collective-permute-start(bf16[2,64,2000]{2,1,0:T(8,128)(2,1)} %get-tuple-element.3990), channel_id=1, source_target_pairs={{0,8},{8,16},{16,24},{1,9},{9,17},{17,25},{2,10},{10,18},{18,26},{... | collective-permute-start | bytes 1536008 | tf_op jit(solution)/shard_map/ppermute | solution.py:30
  314.7 13.5 collective-permute-start.3
  331.8 40.5 %copy-start.8 = (f32[2,64,2000]{2,1,0:T(8,128)}, f32[2,64,2000]{2,1,0:T(8,128)S(1)}, u32[]{:S(2)}) copy-start(f32[2,64,2000]{2,1,0:T(8,128)S(1)} %get-tuple-element.4071) | copy-start | bytes 3072004
  331.8 42.5 %copy-start.98 = (f32[2,2000]{1,0:T(2,128)S(1)}, f32[2,2000]{1,0:T(2,128)}, u32[]{:S(2)}) copy-start(f32[2,2000]{1,0:T(2,128)} %custom-call.7) | copy-start | bytes 48004
  331.8 42.5 %copy-start.99 = (f32[2,2000]{1,0:T(2,128)S(1)}, f32[2,2000]{1,0:T(2,128)}, u32[]{:S(2)}) copy-start(f32[2,2000]{1,0:T(2,128)} %custom-call.6) | copy-start | bytes 48004
  364.9 207.1 %collective-permute-start.4 = (bf16[2,64,2000]{2,1,0:T(8,128)(2,1)}, bf16[2,64,2000]{2,1,0:T(8,128)(2,1)}, u32[]{:S(2)}, u32[]{:S(2)}) collective-permute-start(bf16[2,64,2000]{2,1,0:T(8,128)(2,1)} %broadcast_select_fusion.3), channel_id=1, source_target_pairs={{0,8},{8,16},{16,24},{1,9},{9,17},{17,25},{2,10},{10,18},{18,26},{... | collective-permute-start | bytes 1536008 | tf_op jit(solution)/shard_map/ppermute | solution.py:30
  447.5 13.5 collective-permute-start.5
  464.6 42.6 %copy-start.96 = (f32[2,2000]{1,0:T(2,128)S(1)}, f32[2,2000]{1,0:T(2,128)}, u32[]{:S(2)}) copy-start(f32[2,2000]{1,0:T(2,128)} %custom-call.10) | copy-start | bytes 48004
  464.6 42.6 %copy-start.97 = (f32[2,2000]{1,0:T(2,128)S(1)}, f32[2,2000]{1,0:T(2,128)}, u32[]{:S(2)}) copy-start(f32[2,2000]{1,0:T(2,128)} %custom-call.9) | copy-start | bytes 48004
  497.9 206.7 %collective-permute-start.6 = (bf16[2,64,2000]{2,1,0:T(8,128)(2,1)}, bf16[2,64,2000]{2,1,0:T(8,128)(2,1)}, u32[]{:S(2)}, u32[]{:S(2)}) collective-permute-start(bf16[2,64,2000]{2,1,0:T(8,128)(2,1)} %broadcast_select_fusion.2), channel_id=1, source_target_pairs={{0,8},{8,16},{16,24},{1,9},{9,17},{17,25},{2,10},{10,18},{18,26},{... | collective-permute-start | bytes 1536008 | tf_op jit(solution)/shard_map/ppermute | solution.py:30
  580.4 13.9 collective-permute-start.7
  597.8 41.7 %copy-start.94 = (f32[2,2000]{1,0:T(2,128)S(1)}, f32[2,2000]{1,0:T(2,128)}, u32[]{:S(2)}) copy-start(f32[2,2000]{1,0:T(2,128)} %custom-call.13) | copy-start | bytes 48004
  597.8 41.7 %copy-start.95 = (f32[2,2000]{1,0:T(2,128)S(1)}, f32[2,2000]{1,0:T(2,128)}, u32[]{:S(2)}) copy-start(f32[2,2000]{1,0:T(2,128)} %custom-call.12) | copy-start | bytes 48004
  630.3 207.5 %collective-permute-start.8 = (bf16[2,64,2000]{2,1,0:T(8,128)(2,1)}, bf16[2,64,2000]{2,1,0:T(8,128)(2,1)}, u32[]{:S(2)}, u32[]{:S(2)}) collective-permute-start(bf16[2,64,2000]{2,1,0:T(8,128)(2,1)} %broadcast_select_fusion.1), channel_id=1, source_target_pairs={{0,8},{8,16},{16,24},{1,9},{9,17},{17,25},{2,10},{10,18},{18,26},{... | collective-permute-start | bytes 1536008 | tf_op jit(solution)/shard_map/ppermute | solution.py:30
  712.9 13.9 collective-permute-start.9
  730.4 42.2 %copy-start.92 = (f32[2,2000]{1,0:T(2,128)S(1)}, f32[2,2000]{1,0:T(2,128)}, u32[]{:S(2)}) copy-start(f32[2,2000]{1,0:T(2,128)} %custom-call.16) | copy-start | bytes 48004
  730.4 42.2 %copy-start.93 = (f32[2,2000]{1,0:T(2,128)S(1)}, f32[2,2000]{1,0:T(2,128)}, u32[]{:S(2)}) copy-start(f32[2,2000]{1,0:T(2,128)} %custom-call.15) | copy-start | bytes 48004
  763.4 285.9 %collective-permute-start.10 = (bf16[2,64,2000]{2,1,0:T(8,128)(2,1)}, bf16[2,64,2000]{2,1,0:T(8,128)(2,1)}, u32[]{:S(2)}, u32[]{:S(2)}) collective-permute-start(bf16[2,64,2000]{2,1,0:T(8,128)(2,1)} %broadcast_select_fusion), channel_id=1, source_target_pairs={{0,8},{8,16},{16,24},{1,9},{9,17},{17,25},{2,10},{10,18},{18,26},{... | collective-permute-start | bytes 1536008 | tf_op jit(solution)/shard_map/ppermute | solution.py:30
  796.1 40.6 %copy-start.118 = (f32[1,2,2000]{2,0,1:T(1,128)S(1)}, f32[1,2,2000]{2,0,1:T(1,128)}, u32[]{:S(2)}) copy-start(f32[1,2,2000]{2,0,1:T(1,128)} %constant_dynamic-slice_fusion.3) | copy-start | bytes 48004
  796.1 41.7 %copy-start.166 = (f32[2,64]{1,0:T(2,128)S(1)}, f32[2,64]{1,0:T(2,128)}, u32[]{:S(2)}) copy-start(f32[2,64]{1,0:T(2,128)} %get-tuple-element.4053) | copy-start | bytes 1540
  846.0 14.2 collective-permute-start.11
  863.0 43.6 %copy-start.90 = (f32[2,2000]{1,0:T(2,128)S(1)}, f32[2,2000]{1,0:T(2,128)}, u32[]{:S(2)}) copy-start(f32[2,2000]{1,0:T(2,128)} %custom-call.19) | copy-start | bytes 48004
  863.0 43.6 %copy-start.91 = (f32[2,2000]{1,0:T(2,128)S(1)}, f32[2,2000]{1,0:T(2,128)}, u32[]{:S(2)}) copy-start(f32[2,2000]{1,0:T(2,128)} %custom-call.18) | copy-start | bytes 48004
  1053.2 868.1 %reduce-scatter.9.cloned.1.call-start = ((), (), s32[]{:S(2)}) async-start(), calls=%async_computation.6 | async-start | bytes 2621440
  1086.4 143.4 %copy-start.121 = (f32[2000]{0:T(1024)}, f32[2000]{0:T(1024)S(1)}, u32[]{:S(2)}) copy-start(f32[2000]{0:T(1024)S(1)} %get-tuple-element.3605) | copy-start | bytes 24004
  1086.4 143.4 %copy-start.123 = (f32[2000]{0:T(1024)}, f32[2000]{0:T(1024)S(1)}, u32[]{:S(2)}) copy-start(f32[2000]{0:T(1024)S(1)} %get-tuple-element.3606) | copy-start | bytes 24004
  1096.7 13.1 collective-permute-start.12
  1185.5 40.9 %collective-permute-start.13 = (bf16[2,64,2000]{2,1,0:T(8,128)(2,1)}, bf16[2,64,2000]{2,1,0:T(8,128)(2,1)}, u32[]{:S(2)}, u32[]{:S(2)}) collective-permute-start(bf16[2,64,2000]{2,1,0:T(8,128)(2,1)} %get-tuple-element.3989), channel_id=1, source_target_pairs={{8,0},{16,8},{24,16},{9,1},{17,9},{25,17},{10,2},{18,10},{26,18},{... | collective-permute-start | bytes 1536008 | tf_op jit(solution)/shard_map/ppermute | solution.py:30
  1228.5 14.2 collective-permute-start.14
  1239.2 115.3 %collective-permute-start.15 = (bf16[2,64,2000]{2,1,0:T(8,128)(2,1)}, bf16[2,64,2000]{2,1,0:T(8,128)(2,1)}, u32[]{:S(2)}, u32[]{:S(2)}) collective-permute-start(bf16[2,64,2000]{2,1,0:T(8,128)(2,1)} %get-tuple-element.3988), channel_id=1, source_target_pairs={{8,0},{16,8},{24,16},{9,1},{17,9},{25,17},{10,2},{18,10},{26,18},{... | collective-permute-start | bytes 1536008 | tf_op jit(solution)/shard_map/ppermute | solution.py:30
  1356.7 14.5 collective-permute-start.16
  1447.3 39.6 %collective-permute-start.17 = (bf16[2,64,2000]{2,1,0:T(8,128)(2,1)}, bf16[2,64,2000]{2,1,0:T(8,128)(2,1)}, u32[]{:S(2)}, u32[]{:S(2)}) collective-permute-start(bf16[2,64,2000]{2,1,0:T(8,128)(2,1)} %get-tuple-element.3987), channel_id=1, source_target_pairs={{8,0},{16,8},{24,16},{9,1},{17,9},{25,17},{10,2},{18,10},{26,18},{... | collective-permute-start | bytes 1536008 | tf_op jit(solution)/shard_map/ppermute | solution.py:30
  1489.1 15.0 collective-permute-start.18
  1498.5 116.3 %collective-permute-start.19 = (bf16[2,64,2000]{2,1,0:T(8,128)(2,1)}, bf16[2,64,2000]{2,1,0:T(8,128)(2,1)}, u32[]{:S(2)}, u32[]{:S(2)}) collective-permute-start(bf16[2,64,2000]{2,1,0:T(8,128)(2,1)} %get-tuple-element.3986), channel_id=1, source_target_pairs={{8,0},{16,8},{24,16},{9,1},{17,9},{25,17},{10,2},{18,10},{26,18},{... | collective-permute-start | bytes 1536008 | tf_op jit(solution)/shard_map/ppermute | solution.py:30
  1616.9 13.6 collective-permute-start.20
  1706.7 40.3 %collective-permute-start.21 = (bf16[2,64,2000]{2,1,0:T(8,128)(2,1)}, bf16[2,64,2000]{2,1,0:T(8,128)(2,1)}, u32[]{:S(2)}, u32[]{:S(2)}) collective-permute-start(bf16[2,64,2000]{2,1,0:T(8,128)(2,1)} %get-tuple-element.3985), channel_id=1, source_target_pairs={{8,0},{16,8},{24,16},{9,1},{17,9},{25,17},{10,2},{18,10},{26,18},{... | collective-permute-start | bytes 1536008 | tf_op jit(solution)/shard_map/ppermute | solution.py:30
  1749.1 15.1 collective-permute-start.22
  1758.6 111.3 %collective-permute-start.23 = (bf16[2,64,2000]{2,1,0:T(8,128)(2,1)}, bf16[2,64,2000]{2,1,0:T(8,128)(2,1)}, u32[]{:S(2)}, u32[]{:S(2)}) collective-permute-start(bf16[2,64,2000]{2,1,0:T(8,128)(2,1)} %get-tuple-element.3984), channel_id=1, source_target_pairs={{8,0},{16,8},{24,16},{9,1},{17,9},{25,17},{10,2},{18,10},{26,18},{... | collective-permute-start | bytes 1536008 | tf_op jit(solution)/shard_map/ppermute | solution.py:30
  1872.1 375.4 %all-reduce.18.cloned.1.call-start = ((), (), s32[]{:S(2)}) async-start(), calls=%async_computation.4 | async-start | bytes 32768000 | tf_op jit(solution)/shard_map/psum | solution.py:248
  (213 other events, 2682.7 us)
Sparse Core Ops, SparseCore 0:
  9.8 38.0 all-gather.30
  49.7 35.2 all-gather.32
  1053.3 33.3 reduce-scatter.6
  1872.2 37.5 reduce-scatter.8
  1919.5 327.9 all-reduce.17
where the time goes:
time: 2290 us; the launch traced here: 2270 us
  blocking collectives  785 us (34%)
  local copies, waits for them, and re-layouts  508 us (22%)
  waiting for transfers between devices  403 us (18%)
  other arithmetic  327 us (14%)
  matrix products  147 us (6%)
  starting transfers between devices  62.3 us (3%)
  between operations  26.7 us (1%)
    all_gather x28, blocking collectives, carried_in(): pieces = jax.tree.map(lambda part: lax.all_gather(part, axis), value)  394 us
    psum x1, waiting for transfers between devices, local(): lax.psum((grad_weight_sum, grad_bias_sum, grad_rate_sum), 'rows')  326 us
    squeeze x216, local copies, waits for them, and re-layouts, block_recur(): lax.scan(advance, start, (decay_blocks, drive_blocks), reverse=reverse)  198 us
    psum x7, blocking collectives, layer_backward(): lax.psum((jnp.sum(grad_state, axis=(0, 1)), jnp.sum(grad_state * normed,...  188 us
    psum x7, blocking collectives, row_moments(): lax.psum((jnp.sum(projected * valid_rows, axis=(0, 1)), jnp.sum(valid_row...  106 us
    psum x7, blocking collectives, row_moments(): lax.psum(jnp.sum(centred * centred * valid_rows, axis=(0, 1)), 'rows')  97.4 us
    dot_general x7, matrix products, layer_backward(): jnp.einsum('sfh,sfk->hk', layer_input, grad_low, preferred_element_type=j...  88.2 us
    dynamic_update_slice x33, other arithmetic, place_slot(): return lax.dynamic_update_index_in_dim(buffer, chosen, slot_index, 0)  78.7 us
  transfers between devices with their start and end apart: 29, of which 14 were waited for; matrix products, arithmetic and copies ran while one was open for 42% of the time, Pallas kernels for 0%

commit v1 on v0

v1 whole, which is shorter than its diff:
```python
import functools

import jax
import jax.numpy as jnp
from jax import lax
from jax.experimental import pallas as pl
from jax.experimental.pallas import tpu as pltpu
from jax.sharding import PartitionSpec as P

MESH = pl.DeviceIdType.MESH
norm_eps = 1e-05
F32, BF16 = jnp.float32, jnp.bfloat16
SECTIONS = 4
GROUP = 8


class Sizes:
    def __init__(self, nz, seqs, frames, hidden):
        self.nz, self.seqs, self.frames = nz, seqs, frames
        self.pieces = GROUP // seqs
        self.steps = frames // self.pieces
        self.half = seqs * frames
        self.rows = 2 * self.half
        self.groups = self.rows // GROUP
        self.bw = -(-hidden // 1024) * 128
        self.padded = 8 * self.bw
        self.part = 4 * self.bw // nz
        self.items = 4 * SECTIONS


def wait_bytes(ref, sem):
    pltpu.make_async_copy(ref, ref, sem).wait()


def remote(src, dst, send, recv, device):
    return pltpu.make_async_remote_copy(
        src_ref=src, dst_ref=dst, send_sem=send, recv_sem=recv, device_id=device, device_id_type=MESH
    )


def kernel(
    sz, inp, cot, par_in, mask_in, w_in,
    outg, ging, gout, smallg,
    mainbuf, wbuf, ysend, yrecv, own, xbuf, states, carry_in, chunk_a, chunk_aex, chunk_s0,
    keepf, validf, maskbuf, par, pre_send, pre_recv, ex_send, ex_recv, e1_send, e1_recv, e2_send, e2_recv,
    scal, s1ex, dbuf, dabuf, cex, aexr, dpbuf, pkeep, sibsend, sibrecv, xsend, xrecv, gw, gsend, grecv, gpiece,
    small, outbuf,
    in_ss, in_fs, in_rs, cot_ss, cot_rs, par_ss, par_rs, mask_ss, mask_rs, w_ls, w_ss, w_rs, w_up, w_dn,
    pre_ss, pre_rs, mx_ss, mx_rs, ms_ss, ms_rs, mf_ss, mf_rs, y_ss, y_rs, ex_ss, ex_rs,
    o_ss, o_rs, e1_ss, e1_rs, e2_ss, e2_rs, dp_ss, dp_rs, sb_ss, sb_rs, xp_ss, xp_rs,
    gi_ss, gi_rs, gr_ss, gr_rs, gx_ss, gx_rs, gz_rs, gz_up, gz_dn, gz_sb, gs_rs, sm_ss, sm_rs,
):
    nz, bw, items, groups, steps = sz.nz, sz.bw, sz.items, sz.groups, sz.steps
    pieces, seqs = sz.pieces, sz.seqs
    s, r = lax.axis_index("section"), lax.axis_index("rows")
    y, x, z, c = s // 2, s % 2, r // 2, r % 2
    s_x, s_y, s_d = s + 1 - 2 * x, s + 2 - 4 * y, 3 - s
    r_c = r + 1 - 2 * c
    to_x, to_y, to_d, to_c = (s_x, r), (s_y, r), (s_d, r), (s, r_c)
    j_own, j_x, j_c, j_xc = 2 * x + c, 2 * (1 - x) + c, 2 * x + 1 - c, 2 * (1 - x) + 1 - c
    me = 2 * s + c
    part = sz.part
    sub = lax.broadcasted_iota(jnp.int32, (GROUP, bw), 0)
    place = sub % pieces

    def z_peer(distance):
        return (s, 2 * ((z + distance) % nz) + c)

    def z_slot(p):
        return (z - p + nz - 1) % nz

    def by_seq(rows):
        value = jnp.broadcast_to(rows[seqs - 1], (GROUP, bw))
        for q in range(seqs - 2, -1, -1):
            value = jnp.where(sub < (q + 1) * pieces, jnp.broadcast_to(rows[q], (GROUP, bw)), value)
        return value

    def last_of(value, q):
        return value[(q + 1) * pieces - 1 : (q + 1) * pieces]

    def first_of(value, q):
        return value[q * pieces : q * pieces + 1]

    def entering(a, b, reverse):
        out_a, out_b = [None, None], [None, None]
        t_a = t_b = None
        for h in (1, 0) if reverse else (0, 1):
            ia, ib = a[h], b[h]
            hop = 1
            while hop < pieces:
                if reverse:
                    ok, shift = place < pieces - hop, GROUP - hop
                else:
                    ok, shift = place >= hop, hop
                pa = jnp.where(ok, pltpu.roll(ia, shift, 0), 1.0)
                pb = jnp.where(ok, pltpu.roll(ib, shift, 0), 0.0)
                ib = ia * pb + ib
                ia = ia * pa
                hop *= 2
            if reverse:
                ok, shift, edge = place < pieces - 1, GROUP - 1, first_of
            else:
                ok, shift, edge = place >= 1, 1, last_of
            xa = jnp.where(ok, pltpu.roll(ia, shift, 0), 1.0)
            xb = jnp.where(ok, pltpu.roll(ib, shift, 0), 0.0)
            na = [edge(ia, q) for q in range(seqs)]
            nb = [edge(ib, q) for q in range(seqs)]
            if t_a is not None:
                ea, eb = by_seq(t_a), by_seq(t_b)
                xb = xa * eb + xb
                xa = xa * ea
                nb = [na[q] * t_b[q] + nb[q] for q in range(seqs)]
                na = [na[q] * t_a[q] for q in range(seqs)]
            t_a, t_b = na, nb
            out_a[h], out_b[h] = xa, xb
        return out_a, out_b, t_a, t_b

    def pack(rows):
        rows = rows + [jnp.zeros((1, bw), F32)] * (8 - len(rows))
        value = jnp.zeros((8, bw), F32)
        for q, row in enumerate(rows):
            value = jnp.where(sub == q, jnp.broadcast_to(row, (8, bw)), value)
        return value

    def total(value):
        return jnp.sum(value, axis=0, keepdims=True)

    def over_z(body, start):
        return lax.fori_loop(0, nz, body, start, unroll=nz <= 8)

    def send_z(src, dst_of, send_sem, recv_sem):
        def one(k, _):
            remote(src, dst_of(k - 1), send_sem, recv_sem, z_peer(k)).start()
            return 0

        lax.fori_loop(1, nz, one, 0, unroll=nz <= 8)

    def not_me(t, h):
        return jnp.logical_or(t != s, h != c)

    barrier = pltpu.get_barrier_semaphore()
    for t in (s, s_x, s_y, s_d):
        for q in (r, r_c):
            if not (t is s and q is r):
                pl.semaphore_signal(barrier, inc=1, device_id=(t, q), device_id_type=MESH)

    def greet(k, _):
        pl.semaphore_signal(barrier, inc=1, device_id=z_peer(k), device_id_type=MESH)
        return 0

    lax.fori_loop(1, nz, greet, 0)
    pl.semaphore_wait(barrier, 7 + nz - 1)

    pltpu.make_async_copy(par_in.at[me], par.at[s], par_rs.at[s]).start()
    for n, t in enumerate((s_x, s_y, s_d)):
        remote(par_in.at[2 * t + c], par.at[s], par_ss.at[n], par_rs.at[s], (t, r)).start()
    pltpu.make_async_copy(mask_in, maskbuf.at[c], mask_rs.at[c]).start()
    remote(mask_in, maskbuf.at[c], mask_ss.at[0], mask_rs.at[c], to_c).start()
    pltpu.make_async_copy(w_in.at[y, j_own], wbuf.at[s], w_ls).start()

    def w_cross():
        for n, t in enumerate((s_x, s_y, s_d)):
            src = w_in.at[t // 2, 2 * (t % 2) + c, pl.ds(z * part, part)]
            remote(src, wbuf.at[s, pl.ds(z * part, part)], w_ss.at[n], w_rs.at[s, z], (t, r)).start()

    @pl.when(s == 0)
    def _():
        w_cross()

    in_dst = mainbuf.at[s, :, c]
    pltpu.make_async_copy(inp.at[pl.ds(4 * y, 4)], in_dst, in_rs.at[s, c]).start()
    remote(inp.at[pl.ds(4 * y, 4)], in_dst, in_ss.at[0], in_rs.at[s, c], to_x).start()
    remote(inp.at[pl.ds(4 - 4 * y, 4)], in_dst, in_ss.at[1], in_rs.at[s, c], to_y).start()
    remote(inp.at[pl.ds(4 - 4 * y, 4)], in_dst, in_ss.at[2], in_rs.at[s, c], to_d).start()
    remote(inp.at[pl.ds(4 * y, 4)], in_dst, in_ss.at[3], in_rs.at[s, c], to_c).start()

    wait_bytes(maskbuf.at[0], mask_rs.at[0])
    wait_bytes(maskbuf.at[1], mask_rs.at[1])

    def masks_of(m, _):
        for h in range(2):
            lo, hi = h * steps, (h + 1) * steps
            keepf[m, lo:hi] = maskbuf[h, 0, m].astype(F32).reshape(steps, GROUP, bw)
            validf[m, lo:hi] = maskbuf[h, 1, m].astype(F32).reshape(steps, GROUP, bw)
        return 0

    lax.fori_loop(0, 4, masks_of, 0)
    for t in range(SECTIONS):
        wait_bytes(par.at[t], par_rs.at[t])

    def decays_of(i, _):
        l, m = i // 4, i % 4
        u = jnp.broadcast_to(par[l, 0:1], (GROUP, bw))
        a_h, v_h = [], []
        for h in range(2):
            a = jnp.ones((GROUP, bw), F32)
            v = jnp.zeros((GROUP, bw), F32)
            for t in range(steps):
                d = u * keepf[m, h * steps + t]
                a = d * a
                v = d * v + 1.0
            a_h.append(a)
            v_h.append(v)
        xa, xb, ta, tb = entering(a_h, v_h, False)
        for h in range(2):
            chunk_a[i, h] = a_h[h]
            chunk_aex[i, h] = xa[h]
            chunk_s0[i, h] = xb[h]
        valid_count = total(jnp.sum(validf[m], axis=0))
        value = pack(ta + tb + [valid_count])
        pre_send[i] = value
        pre_recv[nz - 1, i] = value
        return 0

    lax.fori_loop(0, items, decays_of, 0)
    send_z(pre_send, lambda k: pre_recv.at[k], pre_ss, pre_rs)

    for n, t in enumerate((s_x, s_y, s_d)):
        wait_bytes(mainbuf.at[t, :, c], in_rs.at[t, c])
        remote(mainbuf.at[t, :, c], mainbuf.at[t, :, c], in_fs.at[n], in_rs.at[t, c], to_c).start()
    wait_bytes(in_dst, in_rs.at[s, c])

    def w_hop(l, d, finish):
        def piece(p):
            return wbuf.at[l, pl.ds(p * part, part)]

        def move(p, up, down):
            @pl.when(jnp.logical_and(p >= 0, p < nz))
            def _():
                if not finish:
                    wait_bytes(piece(p), w_rs.at[l, p])
                if up:
                    @pl.when(z + 1 < nz)
                    def _():
                        copy = remote(piece(p), piece(p), w_up.at[l, p], w_rs.at[l, p], (s, r + 2))
                        copy.wait_send() if finish else copy.start()
                if down:
                    @pl.when(z >= 1)
                    def _():
                        copy = remote(piece(p), piece(p), w_dn.at[l, p], w_rs.at[l, p], (s, r - 2))
                        copy.wait_send() if finish else copy.start()

        @pl.when(jnp.logical_and(l != s, jnp.logical_and(l < SECTIONS, d < nz)))
        def _():
            @pl.when(d == 0)
            def _():
                move(z, True, True)

            @pl.when(d > 0)
            def _():
                move(z - d, True, False)
                move(z + d, False, True)

    def w_hops(l, first, count, finish=False):
        def one(d, _):
            w_hop(l, d, finish)
            return 0

        lax.fori_loop(first, first + count, one, 0)

    w_hops(0, 0, nz)
    wait_bytes(wbuf.at[s], w_ls)

    @pl.when(s != 0)
    def _():
        w_cross()

    for t in range(SECTIONS):
        for h in range(2):
            src = cot.at[2 * t + h]

            @pl.when(not_me(t, h))
            def _(src=src, t=t, h=h):
                remote(src, dbuf.at[s, c], cot_ss.at[t, h], cot_rs.at[s, c], (t, 2 * z + h)).start()

            @pl.when(jnp.logical_not(not_me(t, h)))
            def _(src=src):
                pltpu.make_async_copy(src, dbuf.at[s, c], cot_rs.at[s, c]).start()

    wait_bytes(pre_recv.at[pl.ds(0, nz - 1)], pre_rs)

    def arrived(i):
        block = mainbuf.at[i, j_x]
        wait_bytes(block, mx_rs.at[i])
        remote(block, block, mf_ss.at[i], mf_rs.at[i], to_c).start()

    def project(i):
        l, m = i // 4, i % 4

        @pl.when(l == 0)
        def _():
            wait_bytes(mainbuf.at[i, :, 1 - c], in_rs.at[m, 1 - c])

        @pl.when(l > 0)
        def _():
            wait_bytes(mainbuf.at[i, j_c], ms_rs.at[i])
            wait_bytes(mainbuf.at[i, j_xc], mf_rs.at[i])
            wait_bytes(ysend.at[m], y_ss.at[m])

        acc = jnp.zeros((sz.rows, 2 * bw), F32)
        for j in range(4):
            acc = acc + jnp.dot(
                mainbuf[i, j].reshape(sz.rows, bw), wbuf[l, j * bw : (j + 1) * bw], preferred_element_type=F32
            )
        ysend[m] = acc[:, bw:].astype(BF16)
        remote(ysend.at[m], yrecv.at[i % 8], y_ss.at[m], y_rs.at[i % 8], to_y).start()
        own[m] = acc[:, :bw].reshape(groups, GROUP, bw)

    def moments(i):
        l, m = i // 4, i % 4
        wait_bytes(yrecv.at[i % 8], y_rs.at[i % 8])
        pre = own[m] + yrecv[i % 8].astype(F32).reshape(groups, GROUP, bw)
        valid = validf[m]
        pre_sum = total(jnp.sum(pre * valid, axis=0))
        local_count = pre_send[i, 2 * seqs : 2 * seqs + 1]
        pivot = pre_sum / jnp.maximum(local_count, 1.0)
        shifted = pre - pivot
        xbuf[i] = shifted
        square = total(jnp.sum(shifted * shifted * valid, axis=0))
        u = jnp.broadcast_to(par[l, 0:1], (GROUP, bw))
        ends = []
        for h in range(2):
            v = jnp.zeros((GROUP, bw), F32)
            for t in range(steps):
                v = (u * keepf[m, h * steps + t]) * v + shifted[h * steps + t]
            ends.append(v)
        unused_a, xb, unused_t, tb = entering([chunk_a[i, 0], chunk_a[i, 1]], ends, False)
        for h in range(2):
            s1ex[m, h] = xb[h]
        value = pack([pre_sum, square] + tb)

        @pl.when(l > 0)
        def _():
            wait_bytes(ex_recv.at[i % 8, pl.ds(0, nz - 1)], ex_ss.at[m])

        ex_send[m] = value
        ex_recv[i % 8, nz - 1] = value
        send_z(ex_send.at[m], lambda k: ex_recv.at[i % 8, k], ex_ss.at[m], ex_rs.at[i % 8])

    def finish_layer(i):
        l, m = i // 4, i % 4
        wait_bytes(ex_recv.at[i % 8, pl.ds(0, nz - 1)], ex_rs.at[i % 8])
        u, bias = par[l, 0:1], par[l, 1:2]
        gain, shift = par[l, 2:3], par[l, 3:4]

        def add_sum(p, carry):
            slot = z_slot(p)
            return (
                carry[0] + ex_recv[i % 8, slot, 0:1],
                carry[1] + pre_recv[slot, i, 2 * seqs : 2 * seqs + 1],
            )

        zero = jnp.zeros((1, bw), F32)
        sum_all, count_all = over_z(add_sum, (zero, zero))
        mean = sum_all / count_all

        def pivot_of(slot):
            count = pre_recv[slot, i, 2 * seqs : 2 * seqs + 1]
            return ex_recv[i % 8, slot, 0:1] / jnp.maximum(count, 1.0), count

        def add_square(p, carry):
            slot = z_slot(p)
            pivot, count = pivot_of(slot)
            return carry + ex_recv[i % 8, slot, 1:2] + count * (pivot - mean) * (pivot - mean)

        var = over_z(add_square, zero) / count_all
        inv = lax.rsqrt(var + norm_eps)
        alpha = gain * inv

        def hop_in(p, carry):
            slot = z_slot(p)
            pivot, unused = pivot_of(slot)
            beta = shift + alpha * (pivot - mean)
            after = []
            for q in range(seqs):
                value = (
                    alpha * ex_recv[i % 8, slot, 2 + q : 3 + q]
                    + beta * pre_recv[slot, i, seqs + q : seqs + q + 1]
                    + pre_recv[slot, i, q : q + 1] * carry[q]
                )
                after.append(jnp.where(p < z, value, carry[q]))
            return tuple(after)

        enter = by_seq(list(over_z(hop_in, (zero,) * seqs)))
        pivot, unused = pivot_of(nz - 1)
        beta = shift + alpha * (pivot - mean)
        offset = (pivot - mean) * inv
        scal[i] = pack([alpha, 1.0 / count_all])
        wide = [jnp.broadcast_to(v, (GROUP, bw)) for v in (u, bias, alpha, beta, inv, offset)]
        u, bias, alpha, beta, inv, offset = wide
        side = mainbuf.at[jnp.maximum(i - 4, 0), j_own]
        odd = (l % 2).astype(F32)
        to_next = l < SECTIONS - 1
        target = jnp.minimum(i + 4, items - 1)
        for h in range(2):
            v = alpha * s1ex[m, h] + beta * chunk_s0[i, h] + chunk_aex[i, h] * enter
            carry_in[i, h] = v
            hidden = []
            for t in range(steps):
                g = h * steps + t
                shifted = xbuf[i, g]
                v = (u * keepf[m, g]) * v + (alpha * shifted + beta)
                states[i, g] = v
                xbuf[i, g] = shifted * inv + offset
                w = v + bias
                hidden.append(validf[m, g] * (w * jax.nn.sigmoid(w)))
            value = jnp.concatenate(hidden, axis=0) + odd * side[h].astype(F32)
            outbuf[m, h] = value.astype(BF16)

        @pl.when(to_next)
        def _():
            block = mainbuf.at[target, j_own]
            block[...] = outbuf[m]
            remote(block, block, mx_ss.at[target], mx_rs.at[target], to_x).start()
            remote(block, block, ms_ss.at[target], ms_rs.at[target], to_c).start()

        @pl.when(jnp.logical_not(to_next))
        def _():
            for h in range(2):
                @pl.when(not_me(m, h))
                def _(h=h):
                    remote(outbuf.at[m, h], outg.at[me], o_ss.at[m, h], o_rs.at[me], (m, 2 * z + h)).start()

                @pl.when(jnp.logical_not(not_me(m, h)))
                def _(h=h):
                    pltpu.make_async_copy(outbuf.at[m, h], outg.at[me], o_rs.at[me]).start()

    hop_count = -(-nz // 4)

    def forward_tick(k, _):
        @pl.when(k < items)
        def _():
            project(k)

        @pl.when(k >= 2)
        def _():
            finish_layer(k - 2)

        @pl.when(jnp.logical_and(k >= 1, k < items + 1))
        def _():
            moments(k - 1)

        @pl.when(jnp.logical_and(k + 1 >= 4, k + 1 < items))
        def _():
            arrived(k + 1)

        @pl.when(k < 12)
        def _():
            w_hops(k // 4 + 1, (k % 4) * hop_count, hop_count)

        return 0

    lax.fori_loop(0, items + 2, forward_tick, 0)

    def back_index(b):
        l, m = SECTIONS - 1 - b // 4, b % 4
        return l, m, l * 4 + m

    def act_back(b):
        l, m, i = back_index(b)

        @pl.when(b < 4)
        def _():
            for h in range(2):
                wait_bytes(dbuf.at[m, h], cot_rs.at[m, h])

        u = jnp.broadcast_to(par[l, 0:1], (GROUP, bw))
        bias = jnp.broadcast_to(par[l, 1:2], (GROUP, bw))
        ends = [None, None]
        sum_act = jnp.zeros((GROUP, bw), F32)
        for h in (1, 0):
            grad = dbuf[b, h].astype(F32).reshape(steps, GROUP, bw)
            v = jnp.zeros((GROUP, bw), F32)
            for t in range(steps - 1, -1, -1):
                g = h * steps + t
                w = states[i, g] + bias
                sg = jax.nn.sigmoid(w)
                da = grad[t] * validf[m, g] * (sg * (1.0 + w * (1.0 - sg)))
                dabuf[m, g] = da
                sum_act = sum_act + da
                v = (u * keepf[m, g]) * (da + v)
            ends[h] = v
        xa, xb, unused, tb = entering([chunk_a[i, 0], chunk_a[i, 1]], ends, True)
        for h in range(2):
            aexr[m, h] = xa[h]
            cex[m, h] = xb[h]
        value = pack(tb + [total(sum_act)])

        @pl.when(b >= 4)
        def _():
            wait_bytes(e1_recv.at[b % 8, pl.ds(0, nz - 1)], e1_ss.at[m])

        e1_send[m] = value
        e1_recv[b % 8, nz - 1] = value
        send_z(e1_send.at[m], lambda k: e1_recv.at[b % 8, k], e1_ss.at[m], e1_rs.at[b % 8])

    def state_back(b):
        l, m, i = back_index(b)
        wait_bytes(e1_recv.at[b % 8, pl.ds(0, nz - 1)], e1_rs.at[b % 8])
        zero = jnp.zeros((1, bw), F32)

        def hop_in(n, carry):
            p = nz - 1 - n
            slot = z_slot(p)
            after = []
            for q in range(seqs):
                value = e1_recv[b % 8, slot, q : q + 1] + pre_recv[slot, i, q : q + 1] * carry[q]
                after.append(jnp.where(p > z, value, carry[q]))
            return tuple(after) + (carry[seqs] + e1_recv[b % 8, slot, seqs : seqs + 1],)

        *enter, sum_act = over_z(hop_in, (zero,) * (seqs + 1))
        enter = by_seq(enter)
        u = jnp.broadcast_to(par[l, 0:1], (GROUP, bw))
        sum_shift = jnp.zeros((GROUP, bw), F32)
        sum_gain = jnp.zeros((GROUP, bw), F32)
        sum_rate = jnp.zeros((GROUP, bw), F32)
        for h in (1, 0):
            v = cex[m, h] + aexr[m, h] * enter
            for t in range(steps - 1, -1, -1):
                g = h * steps + t
                keep = keepf[m, g]
                ds = dabuf[m, g] + v
                dabuf[m, g] = ds
                sum_shift = sum_shift + ds
                sum_gain = sum_gain + ds * xbuf[i, g]
                before = carry_in[i, h] if t == 0 else states[i, g - 1]
                sum_rate = sum_rate + (ds * keep) * before
                v = (u * keep) * ds
        value = pack([total(sum_gain), total(sum_shift), total(sum_rate)])

        @pl.when(b >= 4)
        def _():
            wait_bytes(e2_recv.at[b % 8, pl.ds(0, nz - 1)], e2_ss.at[m])

        e2_send[m] = value
        e2_recv[b % 8, nz - 1] = value
        send_z(e2_send.at[m], lambda k: e2_recv.at[b % 8, k], e2_ss.at[m], e2_rs.at[b % 8])
        added = pack([zero, zero, zero, sum_act])

        @pl.when(m == 0)
        def _():
            small[l] = added

        @pl.when(m > 0)
        def _():
            small[l] = small[l] + added

    def norm_back(b):
        l, m, i = back_index(b)
        wait_bytes(e2_recv.at[b % 8, pl.ds(0, nz - 1)], e2_rs.at[b % 8])

        def add(p, carry):
            return carry + e2_recv[b % 8, z_slot(p)]

        sums = over_z(add, jnp.zeros((8, bw), F32))
        small[l] = small[l] + sums
        alpha = jnp.broadcast_to(scal[i, 0:1], (GROUP, bw))
        per_count = scal[i, 1:2]
        gain_part = jnp.broadcast_to(sums[0:1] * per_count, (GROUP, bw))
        shift_part = jnp.broadcast_to(sums[1:2] * per_count, (GROUP, bw))
        rows = []
        for g in range(groups):
            rows.append(alpha * (dabuf[m, g] - validf[m, g] * (shift_part + xbuf[i, g] * gain_part)))
        dpbuf[i, 0] = jnp.concatenate(rows, axis=0).astype(BF16)
        remote(dpbuf.at[i, 0], dpbuf.at[i, 1], dp_ss.at[i], dp_rs.at[i], to_y).start()

    nt = (((1,), (1,)), ((), ()))
    tn = (((0,), (0,)), ((), ()))

    def input_back(b):
        l, m, i = back_index(b)
        wait_bytes(dpbuf.at[i, 1], dp_rs.at[i])
        dp = jnp.concatenate([dpbuf[i, 0], dpbuf[i, 1]], axis=1)

        def toward(j):
            w = wbuf[l, pl.ds(pl.multiple_of(j * bw, bw), bw), :]
            return lax.dot_general(dp, w, nt, preferred_element_type=F32)

        @pl.when(b >= 4)
        def _():
            wait_bytes(sibsend.at[m], sb_ss.at[m])

        sibsend[m, 0] = toward(j_c).astype(BF16)
        sibsend[m, 1] = toward(j_xc).astype(BF16)
        remote(sibsend.at[m], sibrecv.at[b % 8], sb_ss.at[m], sb_rs.at[b % 8], to_c).start()
        pkeep[m, 0] = toward(j_own)
        pkeep[m, 1] = toward(j_x)

    def weight_back(b):
        l, m, i = back_index(b)
        dp = jnp.concatenate([dpbuf[i, 0], dpbuf[i, 1]], axis=1)
        for j in range(4):
            rows = pl.ds(j * bw, bw)
            new = lax.dot_general(mainbuf[i, j].reshape(sz.rows, bw), dp, tn, preferred_element_type=F32)

            @pl.when(m == 0)
            def _(new=new, rows=rows):
                gw[rows] = new

            @pl.when(jnp.logical_and(m > 0, m < 3))
            def _(new=new, rows=rows):
                gw[rows] = gw[rows] + new

            @pl.when(m == 3)
            def _(new=new, rows=rows):
                gsend[l, rows] = (gw[rows] + new).astype(BF16)

        @pl.when(m == 3)
        def _():
            def one(k, _):
                p = (z + k) % nz
                src = gsend.at[l, pl.ds(p * part, part)]
                remote(src, grecv.at[l, k - 1], gr_ss.at[l], gr_rs.at[l], z_peer(k)).start()
                return 0

            lax.fori_loop(1, nz, one, 0)

    def cross_back(b):
        m = b % 4
        wait_bytes(sibrecv.at[b % 8], sb_rs.at[b % 8])

        @pl.when(b >= 4)
        def _():
            wait_bytes(xsend.at[m], xp_ss.at[m])

        xsend[m] = (pkeep[m, 1] + sibrecv[b % 8, 1].astype(F32)).astype(BF16)
        remote(xsend.at[m], xrecv.at[b % 8], xp_ss.at[m], xp_rs.at[b % 8], to_x).start()
        pkeep[m, 0] = pkeep[m, 0] + sibrecv[b % 8, 0].astype(F32)

    def join_back(b):
        l, m, i = back_index(b)
        wait_bytes(xrecv.at[b % 8], xp_rs.at[b % 8])
        even = (1 - l % 2).astype(F32)
        side = dbuf[jnp.maximum(b - 4, 0)].astype(F32).reshape(sz.rows, bw)
        value = pkeep[m, 0] + xrecv[b % 8].astype(F32) + even * side
        dbuf[b + 4] = value.astype(BF16).reshape(2, sz.half, bw)

        @pl.when(l == 0)
        def _():
            for h in range(2):
                src = dbuf.at[b + 4, h]

                @pl.when(not_me(m, h))
                def _(src=src, h=h):
                    remote(src, ging.at[me], gi_ss.at[m, h], gi_rs.at[me], (m, 2 * z + h)).start()

                @pl.when(jnp.logical_not(not_me(m, h)))
                def _(src=src):
                    pltpu.make_async_copy(src, ging.at[me], gi_rs.at[me]).start()

    def gather_weights(l):
        wait_bytes(grecv.at[l], gr_rs.at[l])

        def add(k, carry):
            return carry + grecv[l, k].astype(F32)

        start = gsend[l, pl.ds(pl.multiple_of(z * part, part), part), :].astype(F32)
        gpiece[l] = lax.fori_loop(0, nz - 1, add, start).astype(BF16)

        @pl.when(l != s)
        def _():
            remote(gpiece.at[l], gout.at[c, z, s], gx_ss.at[l], gx_rs.at[s], (l, r)).start()

        @pl.when(l == s)
        def _():
            pltpu.make_async_copy(gpiece.at[l], gout.at[c, z, s], gx_rs.at[s]).start()

    def backward_tick(k, _):
        @pl.when(k >= 4)
        def _():
            join_back(k - 4)

        @pl.when(k < items)
        def _():
            act_back(k)

        @pl.when(jnp.logical_and(k >= 3, k < items + 3))
        def _():
            input_back(k - 3)

        @pl.when(jnp.logical_and(k >= 1, k < items + 1))
        def _():
            state_back(k - 1)

        @pl.when(jnp.logical_and(k >= 3, k < items + 3))
        def _():
            cross_back(k - 3)

        @pl.when(jnp.logical_and(k >= 2, k < items + 2))
        def _():
            norm_back(k - 2)

        @pl.when(jnp.logical_and(k >= 3, k < items + 3))
        def _():
            weight_back(k - 3)

        @pl.when(jnp.logical_and(k >= 10, k % 4 == 2))
        def _():
            gather_weights(SECTIONS - 1 - (k - 10) // 4)

        return 0

    lax.fori_loop(0, items + 4, backward_tick, 0)

    for t in range(SECTIONS):
        for h in range(2):
            @pl.when(not_me(t, h))
            def _(t=t, h=h):
                remote(small.at[t], smallg.at[me], sm_ss.at[t, h], sm_rs.at[me], (t, 2 * z + h)).start()

            @pl.when(jnp.logical_not(not_me(t, h)))
            def _(t=t):
                pltpu.make_async_copy(small.at[t], smallg.at[me], sm_rs.at[me]).start()

    gather_weights(0)
    for t in range(SECTIONS):
        wait_bytes(gout.at[c, z, t], gx_rs.at[t])

    def g_move(p, up, down, finish):
        @pl.when(jnp.logical_and(p >= 0, p < nz))
        def _():
            block = gout.at[c, p]
            if not finish:
                @pl.when(p != z)
                def _():
                    wait_bytes(block, gz_rs.at[p])
            if up:
                @pl.when(z + 1 < nz)
                def _():
                    copy = remote(block, block, gz_up.at[p], gz_rs.at[p], (s, r + 2))
                    copy.wait_send() if finish else copy.start()
            if down:
                @pl.when(z >= 1)
                def _():
                    copy = remote(block, block, gz_dn.at[p], gz_rs.at[p], (s, r - 2))
                    copy.wait_send() if finish else copy.start()
            copy = remote(block, block, gz_sb.at[p], gs_rs.at[p], to_c)
            copy.wait_send() if finish else copy.start()

    def g_hops(finish):
        g_move(z, True, True, finish)

        def one(d, _):
            g_move(z - d, True, False, finish)
            g_move(z + d, False, True, finish)
            return 0

        lax.fori_loop(1, nz, one, 0)

    g_hops(False)

    def drain_z(p, _):
        wait_bytes(gout.at[1 - c, p], gs_rs.at[p])
        return 0

    lax.fori_loop(0, nz, drain_z, 0)
    for e in range(8):
        wait_bytes(outg.at[e], o_rs.at[e])
        wait_bytes(ging.at[e], gi_rs.at[e])
        wait_bytes(smallg.at[e], sm_rs.at[e])
    g_hops(True)
    for l in range(SECTIONS):
        w_hops(l, 0, nz, True)
        wait_bytes(grecv.at[l], gr_ss.at[l])

        @pl.when(l != s)
        def _(l=l):
            wait_bytes(gpiece.at[l], gx_ss.at[l])

        wait_bytes(ysend.at[l], y_ss.at[l])
        wait_bytes(ex_recv.at[l, pl.ds(0, nz - 1)], ex_ss.at[l])
        wait_bytes(e1_recv.at[l, pl.ds(0, nz - 1)], e1_ss.at[l])
        wait_bytes(e2_recv.at[l, pl.ds(0, nz - 1)], e2_ss.at[l])
        wait_bytes(sibsend.at[l], sb_ss.at[l])
        wait_bytes(xsend.at[l], xp_ss.at[l])
        for h in range(2):
            @pl.when(not_me(l, h))
            def _(l=l, h=h):
                wait_bytes(dbuf.at[s, c], cot_ss.at[l, h])
                wait_bytes(outbuf.at[l, h], o_ss.at[l, h])
                wait_bytes(dbuf.at[items + l, h], gi_ss.at[l, h])
                wait_bytes(small.at[l], sm_ss.at[l, h])

    def drain(i, _):
        wait_bytes(dpbuf.at[i, 0], dp_ss.at[i])

        @pl.when(i >= 4)
        def _():
            wait_bytes(mainbuf.at[i, j_own], mx_ss.at[i])
            wait_bytes(mainbuf.at[i, j_own], ms_ss.at[i])
            wait_bytes(mainbuf.at[i, j_x], mf_ss.at[i])

        return 0

    lax.fori_loop(0, items, drain, 0)
    for n in range(4):
        wait_bytes(in_dst, in_ss.at[n])
    for n, t in enumerate((s_x, s_y, s_d)):
        wait_bytes(mainbuf.at[t, :, c], in_fs.at[n])
        wait_bytes(par.at[s], par_ss.at[n])
        wait_bytes(wbuf.at[s, pl.ds(z * part, part)], w_ss.at[n])
    wait_bytes(maskbuf.at[c], mask_ss.at[0])
    wait_bytes(pre_recv.at[pl.ds(0, nz - 1)], pre_ss)


def run_kernel(sz, inp, cot, par, masks, weights):
    nz, bw, items, groups = sz.nz, sz.bw, sz.items, sz.groups
    half, rows, part = sz.half, sz.rows, sz.part
    dma = pltpu.SemaphoreType.DMA
    vm = pltpu.VMEM
    step = (GROUP, bw)
    scratch = [
        vm((items, 4, 2, half, bw), BF16),
        vm((SECTIONS, 4 * bw, 2 * bw), BF16),
        vm((4, rows, bw), BF16),
        vm((8, rows, bw), BF16),
        vm((4, groups) + step, F32),
        vm((items, groups) + step, F32),
        vm((items, groups) + step, F32),
        vm((items, 2) + step, F32),
        vm((items, 2) + step, F32),
        vm((items, 2) + step, F32),
        vm((items, 2) + step, F32),
        vm((4, groups) + step, F32),
        vm((4, groups) + step, F32),
        vm((2, 2, 4, half, bw), BF16),
        vm((SECTIONS,) + step, F32),
        vm((items,) + step, F32),
        vm((nz, items) + step, F32),
        vm((4,) + step, F32),
        vm((8, nz) + step, F32),
        vm((4,) + step, F32),
        vm((8, nz) + step, F32),
        vm((4,) + step, F32),
        vm((8, nz) + step, F32),
        vm((items,) + step, F32),
        vm((4, 2) + step, F32),
        vm((items + 4, 2, half, bw), BF16),
        vm((4, groups) + step, F32),
        vm((4, 2) + step, F32),
        vm((4, 2) + step, F32),
        vm((items, 2, rows, bw), BF16),
        vm((4, 2, rows, bw), F32),
        vm((4, 2, rows, bw), BF16),
        vm((8, 2, rows, bw), BF16),
        vm((4, rows, bw), BF16),
        vm((8, rows, bw), BF16),
        vm((4 * bw, 2 * bw), F32),
        vm((SECTIONS, 4 * bw, 2 * bw), BF16),
        vm((SECTIONS, nz - 1, part, 2 * bw), BF16),
        vm((SECTIONS, part, 2 * bw), BF16),
        vm((SECTIONS,) + step, F32),
        vm((4, 2, half, bw), BF16),
    ]
    sems = [
        dma((4,)), dma((3,)), dma((4, 2)), dma((4, 2)), dma((4, 2)), dma((3,)), dma((4,)),
        dma((1,)), dma((2,)), dma, dma((3,)), dma((4, nz)), dma((4, nz)), dma((4, nz)),
        dma, dma, dma((items,)), dma((items,)), dma((items,)), dma((items,)), dma((items,)), dma((items,)),
        dma((4,)), dma((8,)), dma((4,)), dma((8,)),
        dma((4, 2)), dma((8,)), dma((4,)), dma((8,)), dma((4,)), dma((8,)),
        dma((items,)), dma((items,)), dma((4,)), dma((8,)), dma((4,)), dma((8,)),
        dma((4, 2)), dma((8,)), dma((4,)), dma((4,)), dma((4,)), dma((4,)),
        dma((nz,)), dma((nz,)), dma((nz,)), dma((nz,)), dma((nz,)), dma((4, 2)), dma((8,)),
    ]
    anywhere = pl.BlockSpec(memory_space=pl.ANY)
    return pl.pallas_call(
        functools.partial(kernel, sz),
        out_shape=(
            jax.ShapeDtypeStruct((8, half, bw), BF16),
            jax.ShapeDtypeStruct((8, half, bw), BF16),
            jax.ShapeDtypeStruct((2, nz, 4, part, 2 * bw), BF16),
            jax.ShapeDtypeStruct((8, 8, bw), F32),
        ),
        in_specs=[anywhere] * 5,
        out_specs=(anywhere,) * 4,
        scratch_shapes=scratch + sems,
        compiler_params=pltpu.CompilerParams(
            collective_id=0, has_side_effects=True, vmem_limit_bytes=63 * 2**20
        ),
    )(inp, cot, par, masks, weights)


def local(sz, inputs, resets, valid_mask, weights, recurrence, state_bias, norm_gain, norm_shift, cotangent):
    hidden = inputs.shape[-1]
    bw, padded, seqs, pieces, steps = sz.bw, sz.padded, sz.seqs, sz.pieces, sz.steps
    spare = padded - hidden

    def to_blocks(a):
        a = a[0].reshape(seqs, pieces, steps, hidden).transpose(2, 0, 1, 3).reshape(sz.half, hidden)
        a = jnp.pad(a, ((0, 0), (0, spare)))
        return a.reshape(sz.half, 8, bw).transpose(1, 0, 2)

    def from_blocks(a):
        a = a.transpose(1, 0, 2).reshape(sz.half, padded)[:, :hidden]
        return a.reshape(steps, seqs, pieces, hidden).transpose(1, 2, 0, 3).reshape(1, seqs, sz.frames, hidden)

    def to_steps(flags):
        flags = flags.reshape(4, seqs, pieces, steps).transpose(0, 3, 1, 2).reshape(4, sz.half, 1)
        return jnp.broadcast_to(flags.astype(BF16), (4, sz.half, bw))

    masks = jnp.stack([to_steps(1 - resets), to_steps(valid_mask)])
    par = jnp.concatenate([recurrence, state_bias, norm_gain, norm_shift], axis=0)
    par = jnp.pad(par, ((0, 4), (0, spare))).reshape(8, 8, bw).transpose(1, 0, 2)
    w = jnp.pad(weights[0], ((0, spare), (0, spare))).reshape(2, 4 * bw, 2, 4, bw)
    w = jnp.stack([w[0], w[1, :, ::-1]]).transpose(0, 3, 1, 2, 4).reshape(2, 4, 4 * bw, 2 * bw)
    outg, ging, gout, smallg = run_kernel(sz, to_blocks(inputs), to_blocks(cotangent), par, masks, w)
    g = gout.reshape(2, sz.nz, 2, 2, sz.part, 2, bw)
    g = jnp.stack([g[:, :, 0], g[:, :, 1, :, :, ::-1]])
    g = g.transpose(0, 2, 4, 5, 3, 1, 6).reshape(padded, padded)[:hidden, :hidden].astype(F32)
    small = smallg.transpose(1, 0, 2).reshape(8, padded)[:, :hidden]
    return (
        from_blocks(outg),
        from_blocks(ging),
        g[None],
        small[2:3],
        small[3:4],
        small[0:1],
        small[1:2],
    )


def solution(mesh):
    def step(inputs, *rest):
        sz = Sizes(mesh.shape["rows"] // 2, inputs.shape[1], inputs.shape[2], inputs.shape[3])
        return local(sz, inputs, *rest)

    frames = P("section", None, "rows", None)
    flags = P(None, None, "rows")
    vectors = P("section", None)
    matrix = P("section", None, None)
    return jax.shard_map(
        step,
        mesh=mesh,
        in_specs=(frames, flags, flags, matrix, vectors, vectors, vectors, vectors, frames),
        out_specs=(frames, frames, matrix, vectors, vectors, vectors, vectors),
        check_vma=False,
    )
```

time: 2290 us -> 654 us (0.29)
  blocking collectives: 785 us -> 0 us
  Pallas kernels: 0 us -> 408 us
  waiting for transfers between devices: 403 us -> 0 us
  local copies, waits for them, and re-layouts: 508 us -> 195 us
  other arithmetic: 327 us -> 44 us
  matrix products: 147 us -> 0 us
  starting transfers between devices: 62.3 us -> 0 us
  between operations: 26.7 us -> 0.78 us
    pallas_call x0 -> x1, Pallas kernels: none -> 408 us  [run_kernel(): pl.pallas_call(functools.partial(kernel, sz), out_shape=(jax.ShapeDtypeSt...]
    all_gather x28 -> x0, blocking collectives: 394 us -> none  [carried_in(): pieces = jax.tree.map(lambda part: lax.all_gather(part, axis), value)]
    psum x21 -> x0, blocking collectives: 392 us -> none  [the longest x7 188 us: layer_backward(): lax.psum((jnp.sum(grad_state, axis=(0, 1)), jnp.sum(grad_state * normed,...]
    psum x1 -> x0, waiting for transfers between devices: 326 us -> none  [local(): lax.psum((grad_weight_sum, grad_bias_sum, grad_rate_sum), 'rows')]
    squeeze x217 -> x0, local copies, waits for them, and re-layouts: 204 us -> none  [the longest x216 198 us: block_recur(): lax.scan(advance, start, (decay_blocks, drive_blocks), reverse=reverse)]
    dot_general x21 -> x0, matrix products: 147 us -> none  [the longest x7 88.2 us: layer_backward(): jnp.einsum('sfh,sfk->hk', layer_input, grad_low, preferred_element_type=j...]
    select_n x118 -> x0, other arithmetic: 93.9 us -> none  [the longest x98 63.5 us: hop(): jnp.where(position < mine, new, old)]
    dynamic_update_slice x133 -> x0, local copies, waits for them, and re-layouts: 81.8 us -> none  [the longest x112 78.6 us: block_recur(): lax.scan(advance, start, (decay_blocks, drive_blocks), reverse=reverse)]
  transfers between devices with their start and end apart: 29 -> 0, of which waited for: 14 -> 0; matrix products, arithmetic and copies ran while one was open for 42% -> 0% of each run, Pallas kernels for 0% -> 0%
where the time goes in v1:
time: 654 us; the launch traced here: 647 us
  Pallas kernels  408 us (62%)
  local copies, waits for them, and re-layouts  195 us (30%)
  other arithmetic  44 us (7%)
    pallas_call x1, Pallas kernels, run_kernel(): pl.pallas_call(functools.partial(kernel, sz), out_shape=(jax.ShapeDtypeSt...  408 us
    rev x1, local copies, waits for them, and re-layouts, local(): w[1, :, ::-1]  37.7 us
    rev x1, local copies, waits for them, and re-layouts, local(): g = jnp.stack([g[:, :, 0], g[:, :, 1, :, :, ::-1]])  37.5 us
    slice x3, local copies, waits for them, and re-layouts, local(): w[0]  21.8 us
    transpose x1, local copies, waits for them, and re-layouts, local(): g.transpose(0, 2, 4, 5, 3, 1, 6).reshape(padded, padded)[:hidden, :hidden]  19.9 us
    slice x2, local copies, waits for them, and re-layouts, local(): w[1, :, ::-1]  15.2 us
    transpose x1, other arithmetic, local(): jnp.stack([w[0], w[1, :, ::-1]]).transpose(0, 3, 1, 2, 4)  14.8 us
    reshape x1, local copies, waits for them, and re-layouts, local(): g.transpose(0, 2, 4, 5, 3, 1, 6).reshape(padded, padded)[:hidden, :hidden]  14.4 us

profile of v1, /device:TPU:0, one launch (start us, length us, event | category | flops | bytes accessed | tf_op | source)
XLA Modules:
  0.0 647.2 jit_solution(2439630605096994988)
XLA Ops:
  0.6 0.7 subtract_convert_fusion
  1.3 0.7 convert_element_type.44
  2.0 0.1 convert_element_type.45
  2.1 0.1 convert_element_type.41
  2.2 0.1 copy.44
  2.3 0.1 convert_element_type.43
  2.4 0.1 copy.45
  2.6 0.1 convert_element_type.47
  2.7 1.4 select_maximum_fusion
  4.1 0.1 stack_broadcast_in_dim.5
  4.3 0.1 stack_broadcast_in_dim.4
  4.4 0.8 pad_maximum_fusion.mask_in
  5.2 1.4 copy.62
  6.7 0.2 reshape.86
  6.9 0.3 copy.57
  7.3 1.0 copy.40
  8.3 1.4 copy.61
  9.7 0.2 reshape.88
  10.0 0.3 copy.58
  10.3 1.0 copy.43
  11.3 6.6 %pad_slice_fusion.1 = (bf16[1024,2048]{1,0:T(8,128)(2,1)}, bf16[1024,2048]{1,0:T(8,128)(2,1)}) fusion(bf16[2000,2000]{1,0:T(8,128)(2,1)} %bitcast.46), kind=kLoop, calls=%fused_computation.5 | loop fusion | bytes 16388608 | tf_op jit(solution)/shard_map/slice | solution.py:905
  17.9 7.9 %slice.45 = bf16[1,1024,2,4,256]{4,3,2,1,0:T(4,128)(2,1)} reshape(bf16[1024,2048]{1,0:T(8,128)(2,1)} %get-tuple-element.17) | data formatting | bytes 8388608 | tf_op jit(solution)/shard_map/slice | solution.py:905
  25.8 7.4 %copy.47 = bf16[1,1024,2,4,256]{4,2,1,3,0:T(2,128)(2,1)} copy(bf16[1,1024,2,4,256]{4,3,2,1,0:T(4,128)(2,1)} %slice.45) | data formatting | bytes 8388608 | tf_op jit(solution)/shard_map/slice | solution.py:905
  33.2 7.8 %slice.47 = bf16[1,1024,2,4,256]{4,3,2,1,0:T(4,128)(2,1)} reshape(bf16[1024,2048]{1,0:T(8,128)(2,1)} %get-tuple-element.18) | data formatting | bytes 8388608 | tf_op jit(solution)/shard_map/slice | solution.py:905
  41.0 7.4 %copy.46 = bf16[1,1024,2,4,256]{4,2,1,3,0:T(2,128)(2,1)} copy(bf16[1,1024,2,4,256]{4,3,2,1,0:T(4,128)(2,1)} %slice.47) | data formatting | bytes 8388608 | tf_op jit(solution)/shard_map/slice | solution.py:905
  48.3 37.7 %rev.6 = bf16[1,1024,2,4,256]{4,2,1,3,0:T(2,128)(2,1)} reverse(bf16[1,1024,2,4,256]{4,2,1,3,0:T(2,128)(2,1)} %copy.46), dimensions={2} | reverse | bytes 8388608 | tf_op jit(solution)/shard_map/rev | solution.py:905
  86.0 14.8 %maximum_bitcast_fusion = bf16[2,4,1024,2,256]{4,3,2,1,0:T(2,128)(2,1)} fusion(bf16[1,1024,2,4,256]{4,2,1,3,0:T(2,128)(2,1)} %rev.6, bf16[1,1024,2,4,256]{4,2,1,3,0:T(2,128)(2,1)} %copy.47), kind=kLoop, calls=%fused_computation | loop fusion | flops 4194304 | bytes 16777216 | tf_op jit(solution)/shard_map/transpose | solution.py:905
  100.9 14.1 %reshape.91.w_in = bf16[2,4,1024,512]{3,2,1,0:T(8,128)(2,1)} reshape(bf16[2,4,1024,2,256]{4,3,2,1,0:T(2,128)(2,1)} %maximum_bitcast_fusion) | data formatting | bytes 16777216 | tf_op jit(solution)/shard_map/reshape | solution.py:905
  114.9 407.6 %shard_map.144 = (bf16[8,128,256]{2,1,0:T(8,128)(2,1)}, bf16[8,128,256]{2,1,0:T(8,128)(2,1)}, bf16[2,4,4,256,512]{4,3,2,1,0:T(8,128)(2,1)}, f32[8,8,256]{2,1,0:T(8,128)}) custom-call(bf16[8,128,256]{2,1,0:T(8,128)(2,1)} %bitcast.47, bf16[8,128,256]{2,1,0:T(8,128)(2,1)} %bitcast.48, f32[8,8,256]{2,1,0:T(8,128)} %bitcast.63, ...), custom_call_target="tpu_custom_call" | custom-call | tf_op jit(solution)/shard_map/pallas_call | solution.py:866
  522.5 0.0 copy-start
  522.5 1.3 copy.48
  523.9 1.3 copy.51
  525.3 0.2 copy.52
  525.5 0.2 reshape.96
  525.7 1.1 copy.53
  526.8 0.2 copy.49
  527.0 0.2 reshape.93
  527.2 1.1 copy.50
  528.3 0.0 copy-done
  528.3 0.6 fusion.1
  528.9 12.5 %reshape.98 = bf16[2,4,2,2,256,2,256]{6,5,4,3,2,1,0:T(2,128)(2,1)} reshape(bf16[2,4,4,256,512]{4,3,2,1,0:T(8,128)(2,1)} %get-tuple-element.13) | data formatting | bytes 16777216 | tf_op jit(solution)/shard_map/reshape | solution.py:907
  541.4 8.4 %slice_bitcast_fusion.1 = (bf16[1,2,4,2,256,2,256]{6,5,4,3,2,1,0:T(2,128)(2,1)}, bf16[2,4,1,2,256,2,256]{6,5,4,3,2,1,0:T(2,128)(2,1)}) fusion(bf16[2,4,2,2,256,2,256]{6,5,4,3,2,1,0:T(2,128)(2,1)} %reshape.98), kind=kLoop, calls=%fused_computation.6 | loop fusion | bytes 16777216 | tf_op jit(solution)/shard_map/stack;squeeze | solution.py:908
  549.8 37.5 %rev.7 = bf16[2,4,1,2,256,2,256]{6,5,4,3,2,1,0:T(2,128)(2,1)} reverse(bf16[2,4,1,2,256,2,256]{6,5,4,3,2,1,0:T(2,128)(2,1)} %get-tuple-element.16), dimensions={5} | reverse | bytes 8388608 | tf_op jit(solution)/shard_map/rev | solution.py:908
  587.4 14.1 %maximum_bitcast_fusion.1 = bf16[2,4,256,2,2,2,256]{6,3,2,4,1,5,0:T(2,128)(2,1)S(1)} fusion(bf16[1,2,4,2,256,2,256]{6,5,4,3,2,1,0:T(2,128)(2,1)} %bitcast.45, bf16[1,2,4,2,256,2,256]{6,5,4,3,2,1,0:T(2,128)(2,1)} %get-tuple-element.15), kind=kLoop, calls=%fused_computation.1 | loop fusion | flops 4194304 | bytes 16777216 | tf_op jit(solution)/shard_map/transpose | solution.py:909
  601.5 19.9 %copy.55 = bf16[2,4,256,2,2,2,256]{6,5,4,3,2,1,0:T(2,128)(2,1)} copy(bf16[2,4,256,2,2,2,256]{6,3,2,4,1,5,0:T(2,128)(2,1)S(1)} %maximum_bitcast_fusion.1) | data formatting | bytes 16777216 | tf_op jit(solution)/shard_map/transpose | solution.py:909
  621.4 14.4 %reshape.99 = bf16[2048,2048]{1,0:T(8,128)(2,1)} reshape(bf16[2,4,256,2,2,2,256]{6,5,4,3,2,1,0:T(2,128)(2,1)} %copy.55) | data formatting | bytes 16777216 | tf_op jit(solution)/shard_map/reshape | solution.py:909
  635.8 11.4 %fusion = f32[1,2000,2000]{2,1,0:T(8,128)} fusion(bf16[2048,2048]{1,0:T(8,128)(2,1)} %reshape.99), kind=kLoop, calls=%fused_computation.3 | loop fusion | flops 4000000 | bytes 24000000 | tf_op jit(solution)/shard_map/broadcast_in_dim | solution.py:914
  (4 shorter events, 0.2 us)
Async XLA Ops:
  522.5 5.8 copy-start

commit v2 on v1

--- a/solution.py
+++ b/solution.py
@@ -26,10 +26,16 @@
         self.padded = 8 * self.bw
         self.part = 4 * self.bw // nz
         self.items = 4 * SECTIONS
+        self.hidden = hidden
+        self.last = hidden - 7 * self.bw
 
 
 def wait_bytes(ref, sem):
     pltpu.make_async_copy(ref, ref, sem).wait()
+
+
+def local_copy(src, dst, sem):
+    pltpu.make_async_copy(src, dst, sem).start()
 
 
 def remote(src, dst, send, recv, device):
@@ -39,16 +45,16 @@
 
 
 def kernel(
-    sz, inp, cot, par_in, mask_in, w_in,
-    outg, ging, gout, smallg,
+    sz, inp_raw, cot_raw, w_raw, resets, valid_mask, recurrence, state_bias, norm_gain, norm_shift,
+    out, grad_inp, grad_rec, grad_bias, grad_gain, grad_shift, gout,
     mainbuf, wbuf, ysend, yrecv, own, xbuf, states, carry_in, chunk_a, chunk_aex, chunk_s0,
-    keepf, validf, maskbuf, par, pre_send, pre_recv, ex_send, ex_recv, e1_send, e1_recv, e2_send, e2_recv,
-    scal, s1ex, dbuf, dabuf, cex, aexr, dpbuf, pkeep, sibsend, sibrecv, xsend, xrecv, gw, gsend, grecv, gpiece,
-    small, outbuf,
-    in_ss, in_fs, in_rs, cot_ss, cot_rs, par_ss, par_rs, mask_ss, mask_rs, w_ls, w_ss, w_rs, w_up, w_dn,
+    keepf, validf, flagbuf, par, parblk, pre_send, pre_recv, ex_send, ex_recv, e1_send, e1_recv,
+    scal, slopes, s1ex, dbuf, cex, aexr, dpbuf, pkeep, sibsend, sibrecv, xsend, xrecv, gw, gsend, grecv,
+    gpiece, small, small_recv, outbuf, raw, blocks, wst, wx, outg, ging, smallg, blank,
+    raw_ls, wst_ls, in_ss, in_fs, in_rs, cot_ss, cot_rs, par_ss, par_rs, flag_ss, flag_rs, w_ss, w_rs, w_fs,
     pre_ss, pre_rs, mx_ss, mx_rs, ms_ss, ms_rs, mf_ss, mf_rs, y_ss, y_rs, ex_ss, ex_rs,
-    o_ss, o_rs, e1_ss, e1_rs, e2_ss, e2_rs, dp_ss, dp_rs, sb_ss, sb_rs, xp_ss, xp_rs,
-    gi_ss, gi_rs, gr_ss, gr_rs, gx_ss, gx_rs, gz_rs, gz_up, gz_dn, gz_sb, gs_rs, sm_ss, sm_rs,
+    o_ss, o_rs, e1_ss, e1_rs, dp_ss, dp_rs, sb_ss, sb_rs, xp_ss, xp_rs,
+    gi_ss, gi_rs, gr_ss, gr_rs, gx_ss, gx_rs, gz_rs, gz_up, gz_dn, gz_sb, gs_rs, st_ss, st_rs, sm_ss, sm_rs,
 ):
     nz, bw, items, groups, steps = sz.nz, sz.bw, sz.items, sz.groups, sz.steps
     pieces, seqs = sz.pieces, sz.seqs
@@ -59,7 +65,10 @@
     to_x, to_y, to_d, to_c = (s_x, r), (s_y, r), (s_d, r), (s, r_c)
     j_own, j_x, j_c, j_xc = 2 * x + c, 2 * (1 - x) + c, 2 * x + 1 - c, 2 * (1 - x) + 1 - c
     me = 2 * s + c
-    part = sz.part
+    part, half, last = sz.part, sz.half, sz.last
+    mine = SECTIONS - 1 - s
+    pair_half = z % 2
+    to_pair = (s, r + 2 - 4 * pair_half)
     sub = lax.broadcasted_iota(jnp.int32, (GROUP, bw), 0)
     place = sub % pieces
 
@@ -138,6 +147,11 @@
     def not_me(t, h):
         return jnp.logical_or(t != s, h != c)
 
+    blank[...] = jnp.zeros((GROUP, bw), F32)
+
+    def width(e):
+        return bw if e < 7 else last
+
     barrier = pltpu.get_barrier_semaphore()
     for t in (s, s_x, s_y, s_d):
         for q in (r, r_c):
@@ -149,43 +163,142 @@
         return 0
 
     lax.fori_loop(1, nz, greet, 0)
+
+    local_copy(inp_raw.at[0], raw.at[0], raw_ls.at[0])
+    local_copy(cot_raw.at[0], raw.at[1], raw_ls.at[1])
+    w_rows = [(1 - y, 2 * pair_half), (1 - y, 2 * pair_half + 1), (y, 2 * pair_half), (y, 2 * pair_half + 1)]
+    w_rows += [(y, 2 - 2 * pair_half), (y, 3 - 2 * pair_half)]
+
+    def w_load(n, wait):
+        yy, j = w_rows[n]
+        k, slot = 4 * yy + j, n % 3
+
+        def go(rows):
+            copy = pltpu.make_async_copy(
+                w_raw.at[0, pl.ds(pl.multiple_of(k * bw, bw), rows)], wst.at[slot, pl.ds(0, rows)], wst_ls.at[slot]
+            )
+            copy.wait() if wait else copy.start()
+
+        @pl.when(k < 7)
+        def _():
+            go(bw)
+
+        @pl.when(k == 7)
+        def _():
+            if not wait:
+                wst[slot, last:] = jnp.zeros((bw - last, sz.hidden), BF16)
+            go(last)
+
+    def w_cut(n, column, toward, dst):
+        slot = n % 3
+        for e in range(8):
+            @pl.when(column == e % 4)
+            def _(e=e):
+                place_of = jnp.where(toward == e // 4, 0, 1)
+                if e == 7:
+                    dst[place_of] = jnp.zeros((bw, bw), BF16)
+                dst[place_of, :, : width(e)] = wst[slot, :, e * bw : e * bw + width(e)]
+
+    for n in range(3):
+        w_load(n, False)
+
+    parblk[...] = jnp.zeros(parblk.shape, F32)
+    for n, ref in enumerate((recurrence, state_bias, norm_gain, norm_shift)):
+        for e in range(8):
+            parblk[e, n : n + 1, : width(e)] = ref[0:1, e * bw : e * bw + width(e)]
+    par[s] = parblk[me]
+    flagbuf[c] = jnp.zeros(flagbuf.shape[1:], F32)
+    for n, ref in enumerate((resets, valid_mask)):
+        for m in range(4):
+            row = seqs * (4 * n + m)
+            flagbuf[c, row : row + seqs, : sz.frames] = ref[SECTIONS - 1 - m].astype(F32)
+
+    for n in range(6):
+        w_load(n, True)
+        j = w_rows[n][1]
+        rows = pl.ds(pl.multiple_of(j * bw, bw), bw)
+        half_rows = pl.ds((n % 2) * bw, bw)
+        if n < 2:
+            w_cut(n, j_own, 1 - y, wx.at[1, :, half_rows])
+            w_cut(n, j_x, 1 - y, wx.at[2, :, half_rows])
+        elif n < 4:
+            w_cut(n, j_x, y, wx.at[0, :, half_rows])
+            w_cut(n, j_own, y, wbuf.at[s, :, rows])
+        else:
+            w_cut(n, j_own, y, wbuf.at[s, :, rows])
+        if n + 3 < 6:
+            w_load(n + 3, False)
+
+    row = lax.broadcasted_iota(jnp.int32, (half, half), 0)
+    col = lax.broadcasted_iota(jnp.int32, (half, half), 1)
+    frame_of = (row % GROUP // pieces) * sz.frames + (row % pieces) * steps + row // GROUP
+    permute = (col == frame_of).astype(BF16)
+    row_of = row
+    frame_at = (col % GROUP // pieces) * sz.frames + (col % pieces) * steps + col // GROUP
+
+    def cut_frames(n):
+        wait_bytes(raw.at[n], raw_ls.at[n])
+        for e in range(8):
+            value = raw[n, :, :, e * bw : e * bw + width(e)].reshape(half, width(e))
+            if e == 7:
+                blocks[n, e] = jnp.zeros((half, bw), BF16)
+            blocks[n, e, :, : width(e)] = jnp.dot(permute, value, preferred_element_type=F32).astype(BF16)
+
+    cut_frames(0)
     pl.semaphore_wait(barrier, 7 + nz - 1)
 
-    pltpu.make_async_copy(par_in.at[me], par.at[s], par_rs.at[s]).start()
     for n, t in enumerate((s_x, s_y, s_d)):
-        remote(par_in.at[2 * t + c], par.at[s], par_ss.at[n], par_rs.at[s], (t, r)).start()
-    pltpu.make_async_copy(mask_in, maskbuf.at[c], mask_rs.at[c]).start()
-    remote(mask_in, maskbuf.at[c], mask_ss.at[0], mask_rs.at[c], to_c).start()
-    pltpu.make_async_copy(w_in.at[y, j_own], wbuf.at[s], w_ls).start()
+        remote(parblk.at[2 * t + c], par.at[s], par_ss.at[n], par_rs.at[s], (t, r)).start()
+    remote(flagbuf.at[c], flagbuf.at[c], flag_ss.at[0], flag_rs.at[c], to_c).start()
 
     def w_cross():
-        for n, t in enumerate((s_x, s_y, s_d)):
-            src = w_in.at[t // 2, 2 * (t % 2) + c, pl.ds(z * part, part)]
-            remote(src, wbuf.at[s, pl.ds(z * part, part)], w_ss.at[n], w_rs.at[s, z], (t, r)).start()
+        for k in range(2):
+            j = 2 * pair_half + k
+            for n, t in enumerate((s_x, s_y, s_d)):
+                src = wx.at[n, :, pl.ds(k * bw, bw)]
+                dst = wbuf.at[s, :, pl.ds(pl.multiple_of(j * bw, bw), bw)]
+                remote(src, dst, w_ss.at[n, k], w_rs.at[s, j], (t, r)).start()
 
     @pl.when(s == 0)
     def _():
         w_cross()
 
-    in_dst = mainbuf.at[s, :, c]
-    pltpu.make_async_copy(inp.at[pl.ds(4 * y, 4)], in_dst, in_rs.at[s, c]).start()
-    remote(inp.at[pl.ds(4 * y, 4)], in_dst, in_ss.at[0], in_rs.at[s, c], to_x).start()
-    remote(inp.at[pl.ds(4 - 4 * y, 4)], in_dst, in_ss.at[1], in_rs.at[s, c], to_y).start()
-    remote(inp.at[pl.ds(4 - 4 * y, 4)], in_dst, in_ss.at[2], in_rs.at[s, c], to_d).start()
-    remote(inp.at[pl.ds(4 * y, 4)], in_dst, in_ss.at[3], in_rs.at[s, c], to_c).start()
-
-    wait_bytes(maskbuf.at[0], mask_rs.at[0])
-    wait_bytes(maskbuf.at[1], mask_rs.at[1])
+    in_dst = mainbuf.at[mine, :, c]
+    near, far = blocks.at[0, pl.ds(4 * y, 4)], blocks.at[0, pl.ds(4 - 4 * y, 4)]
+    remote(far, in_dst, in_ss.at[2], in_rs.at[mine, c], to_d).start()
+    remote(near, in_dst, in_ss.at[0], in_rs.at[mine, c], to_x).start()
+    remote(far, in_dst, in_ss.at[1], in_rs.at[mine, c], to_y).start()
+    remote(near, in_dst, in_ss.at[3], in_rs.at[mine, c], to_c).start()
+    local_copy(near, in_dst, in_rs.at[mine, c])
+
+    @pl.when(s != 0)
+    def _():
+        w_cross()
+
+    wait_bytes(flagbuf.at[1 - c], flag_rs.at[1 - c])
+    row = lax.broadcasted_iota(jnp.int32, (half, sz.frames), 0)
+    col = lax.broadcasted_iota(jnp.int32, (half, sz.frames), 1)
+    at_frame = col == (row % pieces) * steps + row // GROUP
+    of_seq = row % GROUP // pieces
+    ones = jnp.ones((sz.frames, bw), BF16)
 
     def masks_of(m, _):
         for h in range(2):
             lo, hi = h * steps, (h + 1) * steps
-            keepf[m, lo:hi] = maskbuf[h, 0, m].astype(F32).reshape(steps, GROUP, bw)
-            validf[m, lo:hi] = maskbuf[h, 1, m].astype(F32).reshape(steps, GROUP, bw)
+            for n in range(2):
+                flags = jnp.zeros((half, sz.frames), F32)
+                for q in range(seqs):
+                    line = flagbuf[h, pl.ds(seqs * (4 * n + m) + q, 1), : sz.frames]
+                    flags = jnp.where(jnp.logical_and(at_frame, of_seq == q), line, flags)
+                value = jnp.dot(flags.astype(BF16), ones, preferred_element_type=F32).reshape(steps, GROUP, bw)
+                if n == 0:
+                    keepf[m, lo:hi] = 1.0 - value
+                else:
+                    validf[m, lo:hi] = value
         return 0
 
     lax.fori_loop(0, 4, masks_of, 0)
-    for t in range(SECTIONS):
+    for t in (s_x, s_y, s_d):
         wait_bytes(par.at[t], par_rs.at[t])
 
     def decays_of(i, _):
@@ -215,67 +328,44 @@
     lax.fori_loop(0, items, decays_of, 0)
     send_z(pre_send, lambda k: pre_recv.at[k], pre_ss, pre_rs)
 
-    for n, t in enumerate((s_x, s_y, s_d)):
-        wait_bytes(mainbuf.at[t, :, c], in_rs.at[t, c])
-        remote(mainbuf.at[t, :, c], mainbuf.at[t, :, c], in_fs.at[n], in_rs.at[t, c], to_c).start()
-    wait_bytes(in_dst, in_rs.at[s, c])
-
-    def w_hop(l, d, finish):
-        def piece(p):
-            return wbuf.at[l, pl.ds(p * part, part)]
-
-        def move(p, up, down):
-            @pl.when(jnp.logical_and(p >= 0, p < nz))
-            def _():
-                if not finish:
-                    wait_bytes(piece(p), w_rs.at[l, p])
-                if up:
-                    @pl.when(z + 1 < nz)
-                    def _():
-                        copy = remote(piece(p), piece(p), w_up.at[l, p], w_rs.at[l, p], (s, r + 2))
-                        copy.wait_send() if finish else copy.start()
-                if down:
-                    @pl.when(z >= 1)
-                    def _():
-                        copy = remote(piece(p), piece(p), w_dn.at[l, p], w_rs.at[l, p], (s, r - 2))
-                        copy.wait_send() if finish else copy.start()
-
-        @pl.when(jnp.logical_and(l != s, jnp.logical_and(l < SECTIONS, d < nz)))
-        def _():
-            @pl.when(d == 0)
-            def _():
-                move(z, True, True)
-
-            @pl.when(d > 0)
-            def _():
-                move(z - d, True, False)
-                move(z + d, False, True)
-
-    def w_hops(l, first, count, finish=False):
-        def one(d, _):
-            w_hop(l, d, finish)
-            return 0
-
-        lax.fori_loop(first, first + count, one, 0)
-
-    w_hops(0, 0, nz)
-    wait_bytes(wbuf.at[s], w_ls)
-
-    @pl.when(s != 0)
-    def _():
-        w_cross()
-
+    for n, t in enumerate((s_d, s_x, s_y)):
+        slot = SECTIONS - 1 - t
+        wait_bytes(mainbuf.at[slot, :, c], in_rs.at[slot, c])
+        remote(mainbuf.at[slot, :, c], mainbuf.at[slot, :, c], in_fs.at[n], in_rs.at[slot, c], to_c).start()
+    wait_bytes(in_dst, in_rs.at[mine, c])
+
+    def w_rows_of(l, j):
+        return wbuf.at[l, :, pl.ds(pl.multiple_of(j * bw, bw), bw)]
+
+    def w_pass(l, k):
+        j = 2 * pair_half + k
+
+        @pl.when(l != s)
+        def _():
+            wait_bytes(w_rows_of(l, j), w_rs.at[l, j])
+            remote(w_rows_of(l, j), w_rows_of(l, j), w_fs.at[l, k], w_rs.at[l, j], to_pair).start()
+
+    def w_arrive(l):
+        @pl.when(l != s)
+        def _():
+            for k in range(2):
+                j = 2 - 2 * pair_half + k
+                wait_bytes(w_rows_of(l, j), w_rs.at[l, j])
+
+    w_pass(0, 0)
+    w_pass(0, 1)
+    cut_frames(1)
     for t in range(SECTIONS):
         for h in range(2):
-            src = cot.at[2 * t + h]
+            src = blocks.at[1, 2 * t + h]
 
             @pl.when(not_me(t, h))
             def _(src=src, t=t, h=h):
-                remote(src, dbuf.at[s, c], cot_ss.at[t, h], cot_rs.at[s, c], (t, 2 * z + h)).start()
+                remote(src, dbuf.at[mine, c], cot_ss.at[t, h], cot_rs.at[mine, c], (t, 2 * z + h)).start()
 
             @pl.when(jnp.logical_not(not_me(t, h)))
             def _(src=src):
-                pltpu.make_async_copy(src, dbuf.at[s, c], cot_rs.at[s, c]).start()
+                local_copy(src, dbuf.at[mine, c], cot_rs.at[mine, c])
 
     wait_bytes(pre_recv.at[pl.ds(0, nz - 1)], pre_rs)
 
@@ -287,6 +377,10 @@
     def project(i):
         l, m = i // 4, i % 4
 
+        @pl.when(m == 0)
+        def _():
+            w_arrive(l)
+
         @pl.when(l == 0)
         def _():
             wait_bytes(mainbuf.at[i, :, 1 - c], in_rs.at[m, 1 - c])
@@ -297,14 +391,17 @@
             wait_bytes(mainbuf.at[i, j_xc], mf_rs.at[i])
             wait_bytes(ysend.at[m], y_ss.at[m])
 
-        acc = jnp.zeros((sz.rows, 2 * bw), F32)
-        for j in range(4):
-            acc = acc + jnp.dot(
-                mainbuf[i, j].reshape(sz.rows, bw), wbuf[l, j * bw : (j + 1) * bw], preferred_element_type=F32
-            )
-        ysend[m] = acc[:, bw:].astype(BF16)
+        def to_half(n):
+            acc = jnp.zeros((sz.rows, bw), F32)
+            for j in range(4):
+                acc = acc + jnp.dot(
+                    mainbuf[i, j].reshape(sz.rows, bw), wbuf[l, n, j * bw : (j + 1) * bw], preferred_element_type=F32
+                )
+            return acc
+
+        ysend[m] = to_half(1).astype(BF16)
         remote(ysend.at[m], yrecv.at[i % 8], y_ss.at[m], y_rs.at[i % 8], to_y).start()
-        own[m] = acc[:, :bw].reshape(groups, GROUP, bw)
+        own[m] = to_half(0).reshape(groups, GROUP, bw)
 
     def moments(i):
         l, m = i // 4, i % 4
@@ -417,15 +514,34 @@
         @pl.when(jnp.logical_not(to_next))
         def _():
             for h in range(2):
-                @pl.when(not_me(m, h))
+                @pl.when(not_me(SECTIONS - 1 - m, h))
                 def _(h=h):
-                    remote(outbuf.at[m, h], outg.at[me], o_ss.at[m, h], o_rs.at[me], (m, 2 * z + h)).start()
-
-                @pl.when(jnp.logical_not(not_me(m, h)))
+                    remote(outbuf.at[m, h], outg.at[me], o_ss.at[m, h], o_rs.at[me], (SECTIONS - 1 - m, 2 * z + h)).start()
+
+                @pl.when(jnp.logical_not(not_me(SECTIONS - 1 - m, h)))
                 def _(h=h):
-                    pltpu.make_async_copy(outbuf.at[m, h], outg.at[me], o_rs.at[me]).start()
-
-    hop_count = -(-nz // 4)
+                    local_copy(outbuf.at[m, h], outg.at[me], o_rs.at[me])
+
+    def carry_slopes(i):
+        l, m = i // 4, i % 4
+        u = jnp.broadcast_to(par[l, 0:1], (GROUP, bw))
+        a_h = [chunk_a[i, 0], chunk_a[i, 1]]
+        xa, unused_b, unused_a, unused_t = entering(a_h, [jnp.zeros((GROUP, bw), F32)] * 2, True)
+        sum_one = jnp.zeros((GROUP, bw), F32)
+        sum_normed = jnp.zeros((GROUP, bw), F32)
+        for h in (1, 0):
+            v = xa[h]
+            for t in range(steps - 1, -1, -1):
+                g = h * steps + t
+                sum_one = sum_one + v
+                sum_normed = sum_normed + v * xbuf[i, g]
+                v = (u * keepf[m, g]) * v
+        rows = []
+        for value in (sum_one, sum_normed):
+            for q in range(seqs):
+                inside = jnp.logical_and(sub >= q * pieces, sub < (q + 1) * pieces)
+                rows.append(total(jnp.where(inside, value, 0.0)))
+        slopes[i] = pack(rows)
 
     def forward_tick(k, _):
         @pl.when(k < items)
@@ -435,6 +551,7 @@
         @pl.when(k >= 2)
         def _():
             finish_layer(k - 2)
+            carry_slopes(k - 2)
 
         @pl.when(jnp.logical_and(k >= 1, k < items + 1))
         def _():
@@ -446,7 +563,10 @@
 
         @pl.when(k < 12)
         def _():
-            w_hops(k // 4 + 1, (k % 4) * hop_count, hop_count)
+            for n in range(2):
+                @pl.when(k % 4 == n)
+                def _(n=n):
+                    w_pass(k // 4 + 1, n)
 
         return 0
 
@@ -476,7 +596,7 @@
                 w = states[i, g] + bias
                 sg = jax.nn.sigmoid(w)
                 da = grad[t] * validf[m, g] * (sg * (1.0 + w * (1.0 - sg)))
-                dabuf[m, g] = da
+                own[m, g] = da
                 sum_act = sum_act + da
                 v = (u * keepf[m, g]) * (da + v)
             ends[h] = v
@@ -484,7 +604,17 @@
         for h in range(2):
             aexr[m, h] = xa[h]
             cex[m, h] = xb[h]
-        value = pack(tb + [total(sum_act)])
+        sum_local = jnp.zeros((GROUP, bw), F32)
+        sum_normed = jnp.zeros((GROUP, bw), F32)
+        for h in (1, 0):
+            v = xb[h]
+            for t in range(steps - 1, -1, -1):
+                g = h * steps + t
+                ds = own[m, g] + v
+                sum_local = sum_local + ds
+                sum_normed = sum_normed + ds * xbuf[i, g]
+                v = (u * keepf[m, g]) * ds
+        value = pack(tb + [total(sum_local), total(sum_normed)] + [slopes[i, n : n + 1] for n in range(2 * seqs)])
 
         @pl.when(b >= 4)
         def _():
@@ -493,88 +623,80 @@
         e1_send[m] = value
         e1_recv[b % 8, nz - 1] = value
         send_z(e1_send.at[m], lambda k: e1_recv.at[b % 8, k], e1_ss.at[m], e1_rs.at[b % 8])
+        add_small(l, m, 3, sum_act)
+
+    def add_small(l, m, n, value):
+        added = jnp.where(sub == n, jnp.broadcast_to(total(value), (GROUP, bw)), 0.0)
+        if n == 3:
+            before = jnp.where(m == 0, 0.0, 1.0)
+            small[l] = jnp.where(before > 0.0, small[l], 0.0) + added
+        else:
+            small[l] = small[l] + added
 
     def state_back(b):
         l, m, i = back_index(b)
         wait_bytes(e1_recv.at[b % 8, pl.ds(0, nz - 1)], e1_rs.at[b % 8])
-        zero = jnp.zeros((1, bw), F32)
+        zero = blank[...]
+
+        def line(value):
+            return jnp.broadcast_to(value, (GROUP, bw))
 
         def hop_in(n, carry):
             p = nz - 1 - n
             slot = z_slot(p)
-            after = []
+            sum_shift, sum_gain = carry[0], carry[1]
+            flow, enter = carry[2 : 2 + seqs], carry[2 + seqs :]
+            sum_shift = sum_shift + line(e1_recv[b % 8, slot, seqs : seqs + 1])
+            sum_gain = sum_gain + line(e1_recv[b % 8, slot, seqs + 1 : seqs + 2])
+            after, inside = [], []
             for q in range(seqs):
-                value = e1_recv[b % 8, slot, q : q + 1] + pre_recv[slot, i, q : q + 1] * carry[q]
-                after.append(jnp.where(p > z, value, carry[q]))
-            return tuple(after) + (carry[seqs] + e1_recv[b % 8, slot, seqs : seqs + 1],)
-
-        *enter, sum_act = over_z(hop_in, (zero,) * (seqs + 1))
-        enter = by_seq(enter)
+                one = seqs + 2 + q
+                normed = one + seqs
+                sum_shift = sum_shift + flow[q] * line(e1_recv[b % 8, slot, one : one + 1])
+                sum_gain = sum_gain + flow[q] * line(e1_recv[b % 8, slot, normed : normed + 1])
+                inside.append(jnp.where(p == z, flow[q], enter[q]))
+                after.append(line(e1_recv[b % 8, slot, q : q + 1]) + line(pre_recv[slot, i, q : q + 1]) * flow[q])
+            return (sum_shift, sum_gain, *after, *inside)
+
+        sum_shift, sum_gain, *rest = over_z(hop_in, (zero,) * (2 + 2 * seqs))
+        enter = by_seq(rest[seqs:])
         u = jnp.broadcast_to(par[l, 0:1], (GROUP, bw))
-        sum_shift = jnp.zeros((GROUP, bw), F32)
-        sum_gain = jnp.zeros((GROUP, bw), F32)
+        alpha = jnp.broadcast_to(scal[i, 0:1], (GROUP, bw))
+        per_count = scal[i, 1:2]
+        gain_part, shift_part = sum_gain * per_count, sum_shift * per_count
         sum_rate = jnp.zeros((GROUP, bw), F32)
+        rows = [None] * groups
         for h in (1, 0):
             v = cex[m, h] + aexr[m, h] * enter
             for t in range(steps - 1, -1, -1):
                 g = h * steps + t
                 keep = keepf[m, g]
-                ds = dabuf[m, g] + v
-                dabuf[m, g] = ds
-                sum_shift = sum_shift + ds
-                sum_gain = sum_gain + ds * xbuf[i, g]
+                ds = own[m, g] + v
                 before = carry_in[i, h] if t == 0 else states[i, g - 1]
                 sum_rate = sum_rate + (ds * keep) * before
                 v = (u * keep) * ds
-        value = pack([total(sum_gain), total(sum_shift), total(sum_rate)])
-
-        @pl.when(b >= 4)
-        def _():
-            wait_bytes(e2_recv.at[b % 8, pl.ds(0, nz - 1)], e2_ss.at[m])
-
-        e2_send[m] = value
-        e2_recv[b % 8, nz - 1] = value
-        send_z(e2_send.at[m], lambda k: e2_recv.at[b % 8, k], e2_ss.at[m], e2_rs.at[b % 8])
-        added = pack([zero, zero, zero, sum_act])
-
-        @pl.when(m == 0)
-        def _():
-            small[l] = added
-
-        @pl.when(m > 0)
-        def _():
-            small[l] = small[l] + added
-
-    def norm_back(b):
-        l, m, i = back_index(b)
-        wait_bytes(e2_recv.at[b % 8, pl.ds(0, nz - 1)], e2_rs.at[b % 8])
-
-        def add(p, carry):
-            return carry + e2_recv[b % 8, z_slot(p)]
-
-        sums = over_z(add, jnp.zeros((8, bw), F32))
-        small[l] = small[l] + sums
-        alpha = jnp.broadcast_to(scal[i, 0:1], (GROUP, bw))
-        per_count = scal[i, 1:2]
-        gain_part = jnp.broadcast_to(sums[0:1] * per_count, (GROUP, bw))
-        shift_part = jnp.broadcast_to(sums[1:2] * per_count, (GROUP, bw))
-        rows = []
-        for g in range(groups):
-            rows.append(alpha * (dabuf[m, g] - validf[m, g] * (shift_part + xbuf[i, g] * gain_part)))
-        dpbuf[i, 0] = jnp.concatenate(rows, axis=0).astype(BF16)
-        remote(dpbuf.at[i, 0], dpbuf.at[i, 1], dp_ss.at[i], dp_rs.at[i], to_y).start()
+                rows[g] = alpha * (ds - validf[m, g] * (shift_part + xbuf[i, g] * gain_part))
+        @pl.when(b >= 8)
+        def _():
+            wait_bytes(dpbuf.at[b % 8, 0], dp_ss.at[b % 8])
+
+        dpbuf[b % 8, 0] = jnp.concatenate(rows, axis=0).astype(BF16)
+        remote(dpbuf.at[b % 8, 0], dpbuf.at[b % 8, 1], dp_ss.at[b % 8], dp_rs.at[b % 8], to_y).start()
+        add_small(l, m, 2, sum_rate)
+        small[l] = small[l] + pack([sum_gain[0:1], sum_shift[0:1]])
 
     nt = (((1,), (1,)), ((), ()))
     tn = (((0,), (0,)), ((), ()))
 
     def input_back(b):
         l, m, i = back_index(b)
-        wait_bytes(dpbuf.at[i, 1], dp_rs.at[i])
-        dp = jnp.concatenate([dpbuf[i, 0], dpbuf[i, 1]], axis=1)
+        wait_bytes(dpbuf.at[b % 8, 1], dp_rs.at[b % 8])
+        dp_own, dp_other = dpbuf[b % 8, 0], dpbuf[b % 8, 1]
 
         def toward(j):
-            w = wbuf[l, pl.ds(pl.multiple_of(j * bw, bw), bw), :]
-            return lax.dot_general(dp, w, nt, preferred_element_type=F32)
+            rows = pl.ds(pl.multiple_of(j * bw, bw), bw)
+            first = lax.dot_general(dp_own, wbuf[l, 0, rows], nt, preferred_element_type=F32)
+            return first + lax.dot_general(dp_other, wbuf[l, 1, rows], nt, preferred_element_type=F32)
 
         @pl.when(b >= 4)
         def _():
@@ -588,7 +710,12 @@
 
     def weight_back(b):
         l, m, i = back_index(b)
-        dp = jnp.concatenate([dpbuf[i, 0], dpbuf[i, 1]], axis=1)
+        dp = jnp.concatenate([dpbuf[b % 8, 0], dpbuf[b % 8, 1]], axis=1)
+
+        @pl.when(jnp.logical_and(m == 3, l < 2))
+        def _():
+            wait_bytes(grecv.at[l % 2], gr_ss.at[l % 2])
+
         for j in range(4):
             rows = pl.ds(j * bw, bw)
             new = lax.dot_general(mainbuf[i, j].reshape(sz.rows, bw), dp, tn, preferred_element_type=F32)
@@ -603,14 +730,14 @@
 
             @pl.when(m == 3)
             def _(new=new, rows=rows):
-                gsend[l, rows] = (gw[rows] + new).astype(BF16)
+                gsend[l % 2, rows] = (gw[rows] + new).astype(BF16)
 
         @pl.when(m == 3)
         def _():
             def one(k, _):
                 p = (z + k) % nz
-                src = gsend.at[l, pl.ds(p * part, part)]
-                remote(src, grecv.at[l, k - 1], gr_ss.at[l], gr_rs.at[l], z_peer(k)).start()
+                src = gsend.at[l % 2, pl.ds(p * part, part)]
+                remote(src, grecv.at[l % 2, k - 1], gr_ss.at[l % 2], gr_rs.at[l % 2], z_peer(k)).start()
                 return 0
 
             lax.fori_loop(1, nz, one, 0)
@@ -640,21 +767,21 @@
             for h in range(2):
                 src = dbuf.at[b + 4, h]
 
-                @pl.when(not_me(m, h))
+                @pl.when(not_me(SECTIONS - 1 - m, h))
                 def _(src=src, h=h):
-                    remote(src, ging.at[me], gi_ss.at[m, h], gi_rs.at[me], (m, 2 * z + h)).start()
-
-                @pl.when(jnp.logical_not(not_me(m, h)))
+                    remote(src, ging.at[me], gi_ss.at[m, h], gi_rs.at[me], (SECTIONS - 1 - m, 2 * z + h)).start()
+
+                @pl.when(jnp.logical_not(not_me(SECTIONS - 1 - m, h)))
                 def _(src=src):
-                    pltpu.make_async_copy(src, ging.at[me], gi_rs.at[me]).start()
+                    local_copy(src, ging.at[me], gi_rs.at[me])
 
     def gather_weights(l):
-        wait_bytes(grecv.at[l], gr_rs.at[l])
+        wait_bytes(grecv.at[l % 2], gr_rs.at[l % 2])
 
         def add(k, carry):
-            return carry + grecv[l, k].astype(F32)
-
-        start = gsend[l, pl.ds(pl.multiple_of(z * part, part), part), :].astype(F32)
+            return carry + grecv[l % 2, k].astype(F32)
+
+        start = gsend[l % 2, pl.ds(pl.multiple_of(z * part, part), part), :].astype(F32)
         gpiece[l] = lax.fori_loop(0, nz - 1, add, start).astype(BF16)
 
         @pl.when(l != s)
@@ -663,7 +790,7 @@
 
         @pl.when(l == s)
         def _():
-            pltpu.make_async_copy(gpiece.at[l], gout.at[c, z, s], gx_rs.at[s]).start()
+            local_copy(gpiece.at[l], gout.at[c, z, s], gx_rs.at[s])
 
     def backward_tick(k, _):
         @pl.when(k >= 4)
@@ -674,34 +801,34 @@
         def _():
             act_back(k)
 
-        @pl.when(jnp.logical_and(k >= 3, k < items + 3))
-        def _():
-            input_back(k - 3)
-
         @pl.when(jnp.logical_and(k >= 1, k < items + 1))
         def _():
             state_back(k - 1)
 
-        @pl.when(jnp.logical_and(k >= 3, k < items + 3))
-        def _():
-            cross_back(k - 3)
-
         @pl.when(jnp.logical_and(k >= 2, k < items + 2))
         def _():
-            norm_back(k - 2)
-
-        @pl.when(jnp.logical_and(k >= 3, k < items + 3))
-        def _():
-            weight_back(k - 3)
-
-        @pl.when(jnp.logical_and(k >= 10, k % 4 == 2))
-        def _():
-            gather_weights(SECTIONS - 1 - (k - 10) // 4)
+            input_back(k - 2)
+            weight_back(k - 2)
+            cross_back(k - 2)
+
+        @pl.when(jnp.logical_and(k >= 9, k % 4 == 1))
+        def _():
+            gather_weights(SECTIONS - 1 - (k - 9) // 4)
 
         return 0
 
     lax.fori_loop(0, items + 4, backward_tick, 0)
 
+    send_z(small, lambda k: small_recv.at[k], st_ss, st_rs)
+    wait_bytes(small_recv, st_rs)
+    wait_bytes(small_recv, st_ss)
+
+    def add_rest(k, _):
+        for l in range(SECTIONS):
+            small[l] = small[l] + jnp.where(sub >= 2, small_recv[k, l], 0.0)
+        return 0
+
+    lax.fori_loop(0, nz - 1, add_rest, 0)
     for t in range(SECTIONS):
         for h in range(2):
             @pl.when(not_me(t, h))
@@ -710,7 +837,7 @@
 
             @pl.when(jnp.logical_not(not_me(t, h)))
             def _(t=t):
-                pltpu.make_async_copy(small.at[t], smallg.at[me], sm_rs.at[me]).start()
+                local_copy(small.at[t], smallg.at[me], sm_rs.at[me])
 
     gather_weights(0)
     for t in range(SECTIONS):
@@ -749,40 +876,53 @@
 
     g_hops(False)
 
-    def drain_z(p, _):
-        wait_bytes(gout.at[1 - c, p], gs_rs.at[p])
-        return 0
-
-    lax.fori_loop(0, nz, drain_z, 0)
+    restore = (row_of == frame_at).astype(BF16)
     for e in range(8):
         wait_bytes(outg.at[e], o_rs.at[e])
         wait_bytes(ging.at[e], gi_rs.at[e])
         wait_bytes(smallg.at[e], sm_rs.at[e])
+        for src, dst in ((outg, out), (ging, grad_inp)):
+            value = jnp.dot(restore, src[e], preferred_element_type=F32).astype(BF16)
+            value = value.reshape(seqs, sz.frames, bw)
+            dst[0, :, :, e * bw : e * bw + width(e)] = value[:, :, : width(e)]
+        for n, dst in enumerate((grad_gain, grad_shift, grad_rec, grad_bias)):
+            dst[0:1, e * bw : e * bw + width(e)] = smallg[e, n : n + 1, : width(e)]
+
+    def drain_z(p, _):
+        wait_bytes(gout.at[1 - c, p], gs_rs.at[p])
+        return 0
+
+    lax.fori_loop(0, nz, drain_z, 0)
     g_hops(True)
+    for l in range(2):
+        wait_bytes(grecv.at[l], gr_ss.at[l])
     for l in range(SECTIONS):
-        w_hops(l, 0, nz, True)
-        wait_bytes(grecv.at[l], gr_ss.at[l])
-
         @pl.when(l != s)
         def _(l=l):
             wait_bytes(gpiece.at[l], gx_ss.at[l])
+            for k in range(2):
+                wait_bytes(w_rows_of(l, k), w_fs.at[l, k])
 
         wait_bytes(ysend.at[l], y_ss.at[l])
         wait_bytes(ex_recv.at[l, pl.ds(0, nz - 1)], ex_ss.at[l])
         wait_bytes(e1_recv.at[l, pl.ds(0, nz - 1)], e1_ss.at[l])
-        wait_bytes(e2_recv.at[l, pl.ds(0, nz - 1)], e2_ss.at[l])
         wait_bytes(sibsend.at[l], sb_ss.at[l])
         wait_bytes(xsend.at[l], xp_ss.at[l])
         for h in range(2):
             @pl.when(not_me(l, h))
             def _(l=l, h=h):
-                wait_bytes(dbuf.at[s, c], cot_ss.at[l, h])
+                wait_bytes(dbuf.at[mine, c], cot_ss.at[l, h])
+                wait_bytes(small.at[l], sm_ss.at[l, h])
+
+            @pl.when(not_me(SECTIONS - 1 - l, h))
+            def _(l=l, h=h):
                 wait_bytes(outbuf.at[l, h], o_ss.at[l, h])
                 wait_bytes(dbuf.at[items + l, h], gi_ss.at[l, h])
-                wait_bytes(small.at[l], sm_ss.at[l, h])
 
     def drain(i, _):
-        wait_bytes(dpbuf.at[i, 0], dp_ss.at[i])
+        @pl.when(i < 8)
+        def _():
+            wait_bytes(dpbuf.at[i, 0], dp_ss.at[i])
 
         @pl.when(i >= 4)
         def _():
@@ -795,15 +935,16 @@
     lax.fori_loop(0, items, drain, 0)
     for n in range(4):
         wait_bytes(in_dst, in_ss.at[n])
-    for n, t in enumerate((s_x, s_y, s_d)):
-        wait_bytes(mainbuf.at[t, :, c], in_fs.at[n])
+    for n in range(3):
+        wait_bytes(in_dst, in_fs.at[n])
         wait_bytes(par.at[s], par_ss.at[n])
-        wait_bytes(wbuf.at[s, pl.ds(z * part, part)], w_ss.at[n])
-    wait_bytes(maskbuf.at[c], mask_ss.at[0])
+        for k in range(2):
+            wait_bytes(wx.at[n, :, pl.ds(k * bw, bw)], w_ss.at[n, k])
+    wait_bytes(flagbuf.at[c], flag_ss.at[0])
     wait_bytes(pre_recv.at[pl.ds(0, nz - 1)], pre_ss)
 
 
-def run_kernel(sz, inp, cot, par, masks, weights):
+def run_kernel(sz, *args):
     nz, bw, items, groups = sz.nz, sz.bw, sz.items, sz.groups
     half, rows, part = sz.half, sz.rows, sz.part
     dma = pltpu.SemaphoreType.DMA
@@ -811,7 +952,7 @@
     step = (GROUP, bw)
     scratch = [
         vm((items, 4, 2, half, bw), BF16),
-        vm((SECTIONS, 4 * bw, 2 * bw), BF16),
+        vm((SECTIONS, 2, 4 * bw, bw), BF16),
         vm((4, rows, bw), BF16),
         vm((8, rows, bw), BF16),
         vm((4, groups) + step, F32),
@@ -823,100 +964,100 @@
         vm((items, 2) + step, F32),
         vm((4, groups) + step, F32),
         vm((4, groups) + step, F32),
-        vm((2, 2, 4, half, bw), BF16),
+        vm((2, 8 * sz.seqs, 128), F32),
         vm((SECTIONS,) + step, F32),
+        vm((8,) + step, F32),
         vm((items,) + step, F32),
         vm((nz, items) + step, F32),
         vm((4,) + step, F32),
         vm((8, nz) + step, F32),
         vm((4,) + step, F32),
         vm((8, nz) + step, F32),
-        vm((4,) + step, F32),
-        vm((8, nz) + step, F32),
+        vm((items,) + step, F32),
         vm((items,) + step, F32),
         vm((4, 2) + step, F32),
         vm((items + 4, 2, half, bw), BF16),
-        vm((4, groups) + step, F32),
         vm((4, 2) + step, F32),
         vm((4, 2) + step, F32),
-        vm((items, 2, rows, bw), BF16),
+        vm((8, 2, rows, bw), BF16),
         vm((4, 2, rows, bw), F32),
         vm((4, 2, rows, bw), BF16),
         vm((8, 2, rows, bw), BF16),
         vm((4, rows, bw), BF16),
         vm((8, rows, bw), BF16),
         vm((4 * bw, 2 * bw), F32),
-        vm((SECTIONS, 4 * bw, 2 * bw), BF16),
-        vm((SECTIONS, nz - 1, part, 2 * bw), BF16),
+        vm((2, 4 * bw, 2 * bw), BF16),
+        vm((2, nz - 1, part, 2 * bw), BF16),
         vm((SECTIONS, part, 2 * bw), BF16),
         vm((SECTIONS,) + step, F32),
+        vm((nz - 1, SECTIONS) + step, F32),
         vm((4, 2, half, bw), BF16),
+        vm((2, sz.seqs, sz.frames, sz.hidden), BF16),
+        vm((2, 8, half, bw), BF16),
+        vm((3, bw, sz.hidden), BF16),
+        vm((3, 2, 2 * bw, bw), BF16),
+        vm((8, half, bw), BF16),
+        vm((8, half, bw), BF16),
+        vm((8,) + step, F32),
+        vm(step, F32),
     ]
     sems = [
-        dma((4,)), dma((3,)), dma((4, 2)), dma((4, 2)), dma((4, 2)), dma((3,)), dma((4,)),
-        dma((1,)), dma((2,)), dma, dma((3,)), dma((4, nz)), dma((4, nz)), dma((4, nz)),
+        dma((2,)), dma((3,)), dma((4,)), dma((3,)), dma((4, 2)), dma((4, 2)), dma((4, 2)),
+        dma((3,)), dma((4,)), dma((1,)), dma((2,)), dma((3, 2)), dma((4, 4)), dma((4, 2)),
         dma, dma, dma((items,)), dma((items,)), dma((items,)), dma((items,)), dma((items,)), dma((items,)),
         dma((4,)), dma((8,)), dma((4,)), dma((8,)),
-        dma((4, 2)), dma((8,)), dma((4,)), dma((8,)), dma((4,)), dma((8,)),
-        dma((items,)), dma((items,)), dma((4,)), dma((8,)), dma((4,)), dma((8,)),
-        dma((4, 2)), dma((8,)), dma((4,)), dma((4,)), dma((4,)), dma((4,)),
-        dma((nz,)), dma((nz,)), dma((nz,)), dma((nz,)), dma((nz,)), dma((4, 2)), dma((8,)),
+        dma((4, 2)), dma((8,)), dma((4,)), dma((8,)),
+        dma((8,)), dma((8,)), dma((4,)), dma((8,)), dma((4,)), dma((8,)),
+        dma((4, 2)), dma((8,)), dma((2,)), dma((2,)), dma((4,)), dma((4,)),
+        dma((nz,)), dma((nz,)), dma((nz,)), dma((nz,)), dma((nz,)), dma, dma, dma((4, 2)), dma((8,)),
     ]
     anywhere = pl.BlockSpec(memory_space=pl.ANY)
+    inside = pl.BlockSpec(memory_space=pltpu.VMEM)
+    frames = jax.ShapeDtypeStruct((1, sz.seqs, sz.frames, sz.hidden), BF16)
+    vector = jax.ShapeDtypeStruct((1, sz.hidden), F32)
     return pl.pallas_call(
         functools.partial(kernel, sz),
-        out_shape=(
-            jax.ShapeDtypeStruct((8, half, bw), BF16),
-            jax.ShapeDtypeStruct((8, half, bw), BF16),
-            jax.ShapeDtypeStruct((2, nz, 4, part, 2 * bw), BF16),
-            jax.ShapeDtypeStruct((8, 8, bw), F32),
-        ),
-        in_specs=[anywhere] * 5,
-        out_specs=(anywhere,) * 4,
+        out_shape=(frames, frames) + (vector,) * 4 + (jax.ShapeDtypeStruct((2, nz, 4, part, 2 * bw), BF16),),
+        in_specs=[anywhere] * 3 + [inside] * 6,
+        out_specs=(inside,) * 6 + (anywhere,),
         scratch_shapes=scratch + sems,
         compiler_params=pltpu.CompilerParams(
             collective_id=0, has_side_effects=True, vmem_limit_bytes=63 * 2**20
         ),
-    )(inp, cot, par, masks, weights)
+    )(*args)
+
+
+def place_weights(sz, pieces):
+    bw, part, hidden = sz.bw, sz.part, sz.hidden
+    count = bw // part
+
+    def body(src, dst):
+        upper = pl.program_id(0) // 4
+        for yy in range(2):
+            @pl.when(upper == yy)
+            def _(yy=yy):
+                for p in range(count):
+                    for e in range(8):
+                        n, x, c = (0 if e // 4 == yy else 1), e % 4 // 2, e % 2
+                        wide = bw if e < 7 else sz.last
+                        value = src[c, p, x, :, n * bw : n * bw + wide].astype(F32)
+                        dst[p * part : (p + 1) * part, e * bw : e * bw + wide] = value
+
+    return pl.pallas_call(
+        body,
+        grid=(8,),
+        out_shape=jax.ShapeDtypeStruct((hidden, hidden), F32),
+        in_specs=[pl.BlockSpec((2, count, 2, part, 2 * bw), lambda q: (0, q % 4, q // 4, 0, 0))],
+        out_specs=pl.BlockSpec((bw, hidden), lambda q: (q, 0)),
+        compiler_params=pltpu.CompilerParams(vmem_limit_bytes=32 * 2**20),
+    )(pieces)
 
 
 def local(sz, inputs, resets, valid_mask, weights, recurrence, state_bias, norm_gain, norm_shift, cotangent):
-    hidden = inputs.shape[-1]
-    bw, padded, seqs, pieces, steps = sz.bw, sz.padded, sz.seqs, sz.pieces, sz.steps
-    spare = padded - hidden
-
-    def to_blocks(a):
-        a = a[0].reshape(seqs, pieces, steps, hidden).transpose(2, 0, 1, 3).reshape(sz.half, hidden)
-        a = jnp.pad(a, ((0, 0), (0, spare)))
-        return a.reshape(sz.half, 8, bw).transpose(1, 0, 2)
-
-    def from_blocks(a):
-        a = a.transpose(1, 0, 2).reshape(sz.half, padded)[:, :hidden]
-        return a.reshape(steps, seqs, pieces, hidden).transpose(1, 2, 0, 3).reshape(1, seqs, sz.frames, hidden)
-
-    def to_steps(flags):
-        flags = flags.reshape(4, seqs, pieces, steps).transpose(0, 3, 1, 2).reshape(4, sz.half, 1)
-        return jnp.broadcast_to(flags.astype(BF16), (4, sz.half, bw))
-
-    masks = jnp.stack([to_steps(1 - resets), to_steps(valid_mask)])
-    par = jnp.concatenate([recurrence, state_bias, norm_gain, norm_shift], axis=0)
-    par = jnp.pad(par, ((0, 4), (0, spare))).reshape(8, 8, bw).transpose(1, 0, 2)
-    w = jnp.pad(weights[0], ((0, spare), (0, spare))).reshape(2, 4 * bw, 2, 4, bw)
-    w = jnp.stack([w[0], w[1, :, ::-1]]).transpose(0, 3, 1, 2, 4).reshape(2, 4, 4 * bw, 2 * bw)
-    outg, ging, gout, smallg = run_kernel(sz, to_blocks(inputs), to_blocks(cotangent), par, masks, w)
-    g = gout.reshape(2, sz.nz, 2, 2, sz.part, 2, bw)
-    g = jnp.stack([g[:, :, 0], g[:, :, 1, :, :, ::-1]])
-    g = g.transpose(0, 2, 4, 5, 3, 1, 6).reshape(padded, padded)[:hidden, :hidden].astype(F32)
-    small = smallg.transpose(1, 0, 2).reshape(8, padded)[:, :hidden]
-    return (
-        from_blocks(outg),
-        from_blocks(ging),
-        g[None],
-        small[2:3],
-        small[3:4],
-        small[0:1],
-        small[1:2],
+    outputs, grad_inputs, rec, bias, gain, shift, pieces = run_kernel(
+        sz, inputs, cotangent, weights, resets, valid_mask, recurrence, state_bias, norm_gain, norm_shift
     )
+    return outputs, grad_inputs, place_weights(sz, pieces)[None], rec, bias, gain, shift
 
 
 def solution(mesh):

time: 654 us -> 385 us (0.59)
  local copies, waits for them, and re-layouts: 195 us -> 7.38 us
  other arithmetic: 44 us -> 0 us
  Pallas kernels: 408 us -> 376 us
    rev x2 -> x0, local copies, waits for them, and re-layouts: 75.2 us -> none  [the longest x1 37.7 us: local(): w[1, :, ::-1]]
    reshape x9 -> x0, local copies, waits for them, and re-layouts: 43.9 us -> none  [the longest x1 14.4 us: local(): g.transpose(0, 2, 4, 5, 3, 1, 6).reshape(padded, padded)[:hidden, :hidden]]
    slice x10 -> x0, local copies, waits for them, and re-layouts: 38.1 us -> none  [the longest x3 21.8 us: local(): w[0]]
    pallas_call x1 -> x2, Pallas kernels: 408 us -> 376 us  [the longest x1 370 us: run_kernel(): pl.pallas_call(functools.partial(kernel, sz), out_shape=(frames, frames)...]
    transpose x2 -> x0, other arithmetic: 28.9 us -> none  [the longest x1 14.8 us: local(): jnp.stack([w[0], w[1, :, ::-1]]).transpose(0, 3, 1, 2, 4)]
    transpose x5 -> x0, local copies, waits for them, and re-layouts: 24.7 us -> none  [the longest x1 19.9 us: local(): g.transpose(0, 2, 4, 5, 3, 1, 6).reshape(padded, padded)[:hidden, :hidden]]
    another operation x5 -> x0, local copies, waits for them, and re-layouts: 11.6 us -> none  [the longest x1 8.45 us: local(): g = jnp.stack([g[:, :, 0], g[:, :, 1, :, :, ::-1]])]
    broadcast_in_dim x1 -> x0, other arithmetic: 11.4 us -> none  [local(): g[None]]
where the time goes in v2:
time: 385 us
  Pallas kernels  376 us (98%)
  local copies, waits for them, and re-layouts  7.38 us (2%)
    pallas_call x1, Pallas kernels, run_kernel(): pl.pallas_call(functools.partial(kernel, sz), out_shape=(frames, frames)...  370 us

profile of v2, /device:TPU:0, one launch (start us, length us, event | category | flops | bytes accessed | tf_op | source)
XLA Modules:
  0.0 384.5 jit_solution(10799278784488259442)
XLA Ops:
  0.6 369.7 %shard_map.144 = (bf16[1,2,64,2000]{3,2,1,0:T(8,128)(2,1)}, bf16[1,2,64,2000]{3,2,1,0:T(8,128)(2,1)}, f32[1,2000]{1,0:T(1,128)}, f32[1,2000]{1,0:T(1,128)}, f32[...) custom-call(bf16[1,2,64,2000]{3,2,1,0:T(8,128)(2,1)} %inp_raw.1, ...), custom_call_target="tpu_custom_call" | custom-call | tf_op jit(solution)/shard_map/pallas_call | solution.py:1018
  370.3 0.0 copy-start
  370.4 3.4 copy-done
  373.7 0.0 copy-start.2
  373.7 0.0 copy-start.1
  373.7 0.0 copy-start.6
  373.7 0.0 copy-start.5
  373.7 0.0 copy-start.4
  373.7 0.0 copy-start.3
  373.8 6.8 %shard_map.145 = f32[2000,2000]{1,0:T(8,128)} custom-call(bf16[2,4,4,256,512]{4,3,2,1,0:T(8,128)(2,1)S(1)} %copy-done), custom_call_target="tpu_custom_call" | custom-call | tf_op jit(solution)/shard_map/pallas_call | solution.py:1046
  380.5 0.0 copy-done.2
  380.5 0.8 copy.22
  381.3 0.0 copy-done.1
  381.3 0.8 copy.23
  382.1 0.0 copy-done.6
  382.1 0.6 copy.24
  382.7 0.0 copy-done.5
  382.7 0.6 copy.25
  383.3 0.0 copy-done.4
  383.3 0.6 copy.26
  383.9 0.0 copy-done.3
  383.9 0.6 copy.27
Async XLA Ops:
  370.3 3.4 copy-start
  373.7 6.8 %copy-start.2 = (bf16[1,2,64,2000]{3,2,1,0:T(8,128)(2,1)S(1)}, bf16[1,2,64,2000]{3,2,1,0:T(8,128)(2,1)}, u32[]{:S(2)}) copy-start(bf16[1,2,64,2000]{3,2,1,0:T(8,128)(2,1)} %get-tuple-element.28) | copy-start | bytes 1536004
  373.7 7.6 %copy-start.1 = (bf16[1,2,64,2000]{3,2,1,0:T(8,128)(2,1)S(1)}, bf16[1,2,64,2000]{3,2,1,0:T(8,128)(2,1)}, u32[]{:S(2)}) copy-start(bf16[1,2,64,2000]{3,2,1,0:T(8,128)(2,1)} %get-tuple-element.29) | copy-start | bytes 1536004
  373.7 8.4 %copy-start.6 = (f32[1,2000]{1,0:T(1,128)S(1)}, f32[1,2000]{1,0:T(1,128)}, u32[]{:S(2)}) copy-start(f32[1,2000]{1,0:T(1,128)} %get-tuple-element.31) | copy-start | bytes 24004
  373.7 9.0 %copy-start.5 = (f32[1,2000]{1,0:T(1,128)S(1)}, f32[1,2000]{1,0:T(1,128)}, u32[]{:S(2)}) copy-start(f32[1,2000]{1,0:T(1,128)} %get-tuple-element.32) | copy-start | bytes 24004
  373.7 9.6 %copy-start.4 = (f32[1,2000]{1,0:T(1,128)S(1)}, f32[1,2000]{1,0:T(1,128)}, u32[]{:S(2)}) copy-start(f32[1,2000]{1,0:T(1,128)} %get-tuple-element.33) | copy-start | bytes 24004
  373.7 10.2 %copy-start.3 = (f32[1,2000]{1,0:T(1,128)S(1)}, f32[1,2000]{1,0:T(1,128)}, u32[]{:S(2)}) copy-start(f32[1,2000]{1,0:T(1,128)} %get-tuple-element.34) | copy-start | bytes 24004

commit v3 on v2

--- a/solution.py
+++ b/solution.py
@@ -49,12 +49,12 @@
     out, grad_inp, grad_rec, grad_bias, grad_gain, grad_shift, gout,
     mainbuf, wbuf, ysend, yrecv, own, xbuf, states, carry_in, chunk_a, chunk_aex, chunk_s0,
     keepf, validf, flagbuf, par, parblk, pre_send, pre_recv, ex_send, ex_recv, e1_send, e1_recv,
-    scal, slopes, s1ex, dbuf, cex, aexr, dpbuf, pkeep, sibsend, sibrecv, xsend, xrecv, gw, gsend, grecv,
-    gpiece, small, small_recv, outbuf, raw, blocks, wst, wx, outg, ging, smallg, blank,
-    raw_ls, wst_ls, in_ss, in_fs, in_rs, cot_ss, cot_rs, par_ss, par_rs, flag_ss, flag_rs, w_ss, w_rs, w_fs,
+    scal, slopes, s1ex, dbuf, cex, aexr, dpbuf, pkeep, sibsend, sibrecv, xrecv, gw, gall, gpart, gleave,
+    small, small_recv, outbuf, raw, blocks, wst, wx, outg, ging, smallg, blank,
+    raw_ls, wst_ls, in_ss, in_fs, in_rs, cot_ss, cot_rs, par_ss, par_rs, flag_ss, flag_rs, w_ss, w_rs, w_fs, w_ps,
     pre_ss, pre_rs, mx_ss, mx_rs, ms_ss, ms_rs, mf_ss, mf_rs, y_ss, y_rs, ex_ss, ex_rs,
     o_ss, o_rs, e1_ss, e1_rs, dp_ss, dp_rs, sb_ss, sb_rs, xp_ss, xp_rs,
-    gi_ss, gi_rs, gr_ss, gr_rs, gx_ss, gx_rs, gz_rs, gz_up, gz_dn, gz_sb, gs_rs, st_ss, st_rs, sm_ss, sm_rs,
+    gi_ss, gi_rs, ga_ss, ga_rs, go_ss, gr_rs, gx_ss, gx_rs, gs_ss, gs_rs, st_ss, st_rs, sm_ss, sm_rs,
 ):
     nz, bw, items, groups, steps = sz.nz, sz.bw, sz.items, sz.groups, sz.steps
     pieces, seqs = sz.pieces, sz.seqs
@@ -171,7 +171,7 @@
 
     def w_load(n, wait):
         yy, j = w_rows[n]
-        k, slot = 4 * yy + j, n % 3
+        k, slot = 4 * yy + j, n % 2
 
         def go(rows):
             copy = pltpu.make_async_copy(
@@ -190,7 +190,7 @@
             go(last)
 
     def w_cut(n, column, toward, dst):
-        slot = n % 3
+        slot = n % 2
         for e in range(8):
             @pl.when(column == e % 4)
             def _(e=e):
@@ -199,7 +199,7 @@
                     dst[place_of] = jnp.zeros((bw, bw), BF16)
                 dst[place_of, :, : width(e)] = wst[slot, :, e * bw : e * bw + width(e)]
 
-    for n in range(3):
+    for n in range(2):
         w_load(n, False)
 
     parblk[...] = jnp.zeros(parblk.shape, F32)
@@ -213,7 +213,22 @@
             row = seqs * (4 * n + m)
             flagbuf[c, row : row + seqs, : sz.frames] = ref[SECTIONS - 1 - m].astype(F32)
 
+    def w_cross():
+        for k in range(2):
+            j = 2 * pair_half + k
+            for n, t in enumerate((s_x, s_y, s_d)):
+                src = wx.at[n, :, pl.ds(k * bw, bw)]
+                dst = wbuf.at[s, :, pl.ds(pl.multiple_of(j * bw, bw), bw)]
+                remote(src, dst, w_ss.at[n, k], w_rs.at[s, j], (t, r)).start()
+
     for n in range(6):
+        if n == 4:
+            pl.semaphore_wait(barrier, 7 + nz - 1)
+
+            @pl.when(s == 0)
+            def _():
+                w_cross()
+
         w_load(n, True)
         j = w_rows[n][1]
         rows = pl.ds(pl.multiple_of(j * bw, bw), bw)
@@ -226,8 +241,8 @@
             w_cut(n, j_own, y, wbuf.at[s, :, rows])
         else:
             w_cut(n, j_own, y, wbuf.at[s, :, rows])
-        if n + 3 < 6:
-            w_load(n + 3, False)
+        if n + 2 < 6:
+            w_load(n + 2, False)
 
     row = lax.broadcasted_iota(jnp.int32, (half, half), 0)
     col = lax.broadcasted_iota(jnp.int32, (half, half), 1)
@@ -245,23 +260,10 @@
             blocks[n, e, :, : width(e)] = jnp.dot(permute, value, preferred_element_type=F32).astype(BF16)
 
     cut_frames(0)
-    pl.semaphore_wait(barrier, 7 + nz - 1)
 
     for n, t in enumerate((s_x, s_y, s_d)):
         remote(parblk.at[2 * t + c], par.at[s], par_ss.at[n], par_rs.at[s], (t, r)).start()
     remote(flagbuf.at[c], flagbuf.at[c], flag_ss.at[0], flag_rs.at[c], to_c).start()
-
-    def w_cross():
-        for k in range(2):
-            j = 2 * pair_half + k
-            for n, t in enumerate((s_x, s_y, s_d)):
-                src = wx.at[n, :, pl.ds(k * bw, bw)]
-                dst = wbuf.at[s, :, pl.ds(pl.multiple_of(j * bw, bw), bw)]
-                remote(src, dst, w_ss.at[n, k], w_rs.at[s, j], (t, r)).start()
-
-    @pl.when(s == 0)
-    def _():
-        w_cross()
 
     in_dst = mainbuf.at[mine, :, c]
     near, far = blocks.at[0, pl.ds(4 * y, 4)], blocks.at[0, pl.ds(4 - 4 * y, 4)]
@@ -326,34 +328,53 @@
         return 0
 
     lax.fori_loop(0, items, decays_of, 0)
-    send_z(pre_send, lambda k: pre_recv.at[k], pre_ss, pre_rs)
-
-    for n, t in enumerate((s_d, s_x, s_y)):
-        slot = SECTIONS - 1 - t
-        wait_bytes(mainbuf.at[slot, :, c], in_rs.at[slot, c])
-        remote(mainbuf.at[slot, :, c], mainbuf.at[slot, :, c], in_fs.at[n], in_rs.at[slot, c], to_c).start()
-    wait_bytes(in_dst, in_rs.at[mine, c])
+
+    def send_decays(l):
+        some = pl.ds(4 * l, 4)
+        send_z(pre_send.at[some], lambda k: pre_recv.at[k, some], pre_ss.at[l], pre_rs.at[l])
+
+    send_decays(0)
+
+    def inputs_on(slot):
+        block = mainbuf.at[slot, :, c]
+
+        @pl.when(slot != mine)
+        def _():
+            wait_bytes(block, in_rs.at[slot, c])
+            remote(block, block, in_fs.at[slot], in_rs.at[slot, c], to_c).start()
+
+        @pl.when(slot == mine)
+        def _():
+            wait_bytes(block, in_rs.at[slot, c])
+
+    for slot in range(3):
+        inputs_on(slot)
 
     def w_rows_of(l, j):
         return wbuf.at[l, :, pl.ds(pl.multiple_of(j * bw, bw), bw)]
 
-    def w_pass(l, k):
+    def w_unit(l, j, n):
+        return wbuf.at[l, n, pl.ds(pl.multiple_of(j * bw, bw), bw)]
+
+    def w_pass(l, k, n):
         j = 2 * pair_half + k
 
         @pl.when(l != s)
         def _():
-            wait_bytes(w_rows_of(l, j), w_rs.at[l, j])
-            remote(w_rows_of(l, j), w_rows_of(l, j), w_fs.at[l, k], w_rs.at[l, j], to_pair).start()
+            if n == 0:
+                wait_bytes(w_rows_of(l, j), w_rs.at[l, j])
+            remote(w_unit(l, j, n), w_unit(l, j, n), w_fs.at[l, k, n], w_ps.at[l, k, n], to_pair).start()
 
     def w_arrive(l):
         @pl.when(l != s)
         def _():
             for k in range(2):
-                j = 2 - 2 * pair_half + k
-                wait_bytes(w_rows_of(l, j), w_rs.at[l, j])
-
-    w_pass(0, 0)
-    w_pass(0, 1)
+                for n in range(2):
+                    wait_bytes(w_unit(l, 2 - 2 * pair_half + k, n), w_ps.at[l, k, n])
+
+    for k in range(2):
+        for n in range(2):
+            w_pass(0, k, n)
     cut_frames(1)
     for t in range(SECTIONS):
         for h in range(2):
@@ -366,8 +387,6 @@
             @pl.when(jnp.logical_not(not_me(t, h)))
             def _(src=src):
                 local_copy(src, dbuf.at[mine, c], cot_rs.at[mine, c])
-
-    wait_bytes(pre_recv.at[pl.ds(0, nz - 1)], pre_rs)
 
     def arrived(i):
         block = mainbuf.at[i, j_x]
@@ -436,6 +455,11 @@
 
     def finish_layer(i):
         l, m = i // 4, i % 4
+
+        @pl.when(m == 0)
+        def _():
+            wait_bytes(pre_recv.at[pl.ds(0, nz - 1), pl.ds(4 * l, 4)], pre_rs.at[l])
+
         wait_bytes(ex_recv.at[i % 8, pl.ds(0, nz - 1)], ex_rs.at[i % 8])
         u, bias = par[l, 0:1], par[l, 1:2]
         gain, shift = par[l, 2:3], par[l, 3:4]
@@ -548,6 +572,10 @@
         def _():
             project(k)
 
+        @pl.when(k == 1)
+        def _():
+            inputs_on(3)
+
         @pl.when(k >= 2)
         def _():
             finish_layer(k - 2)
@@ -563,14 +591,21 @@
 
         @pl.when(k < 12)
         def _():
-            for n in range(2):
+            for n in range(4):
                 @pl.when(k % 4 == n)
                 def _(n=n):
-                    w_pass(k // 4 + 1, n)
+                    w_pass(k // 4 + 1, n // 2, n % 2)
+
+            @pl.when(k % 4 == 1)
+            def _():
+                send_decays(k // 4 + 1)
 
         return 0
 
     lax.fori_loop(0, items + 2, forward_tick, 0)
+
+    for m in range(4):
+        wait_bytes(ysend.at[m], y_ss.at[m])
 
     def back_index(b):
         l, m = SECTIONS - 1 - b // 4, b % 4
@@ -711,11 +746,7 @@
     def weight_back(b):
         l, m, i = back_index(b)
         dp = jnp.concatenate([dpbuf[b % 8, 0], dpbuf[b % 8, 1]], axis=1)
-
-        @pl.when(jnp.logical_and(m == 3, l < 2))
-        def _():
-            wait_bytes(grecv.at[l % 2], gr_ss.at[l % 2])
-
+        count = nz // 4
         for j in range(4):
             rows = pl.ds(j * bw, bw)
             new = lax.dot_general(mainbuf[i, j].reshape(sz.rows, bw), dp, tn, preferred_element_type=F32)
@@ -729,18 +760,99 @@
                 gw[rows] = gw[rows] + new
 
             @pl.when(m == 3)
-            def _(new=new, rows=rows):
-                gsend[l % 2, rows] = (gw[rows] + new).astype(BF16)
-
-        @pl.when(m == 3)
-        def _():
-            def one(k, _):
-                p = (z + k) % nz
-                src = gsend.at[l % 2, pl.ds(p * part, part)]
-                remote(src, grecv.at[l % 2, k - 1], gr_ss.at[l % 2], gr_rs.at[l % 2], z_peer(k)).start()
-                return 0
-
-            lax.fori_loop(1, nz, one, 0)
+            def _(new=new, rows=rows, j=j):
+                all_items = (gw[rows] + new).astype(BF16)
+                for n in range(2):
+                    value = all_items[:, n * bw : (n + 1) * bw].reshape(count, part, bw)
+                    gall[l, j * count : (j + 1) * count, n] = value
+
+    period = 2 * nz
+    to_end, to_start = (s, r + 2), (s, r - 2)
+
+    def g_from(p, n, up):
+        return gpart.at[p + 1 if up else p, n], gr_rs.at[p + 1 if up else p, n]
+
+    def g_ready(l, p, n, cross):
+        unit = gall.at[l, p, n]
+        if cross:
+            to_section(l, unit, gout.at[c, s, p, n], gx_ss.at[l, p, n], gx_rs.at[s, p, n], gs_ss.at[s, p, n], gs_rs.at[s, p, n])
+
+    def to_section(l, src, dst, cross_ss, cross_rs, other_ss, other_rs):
+        @pl.when(l != s)
+        def _():
+            remote(src, dst, cross_ss, cross_rs, (l, r)).start()
+
+        @pl.when(l == s)
+        def _():
+            local_copy(src, dst, cross_rs)
+            remote(src, dst, other_ss, other_rs, to_c).start()
+
+    def g_step(g, cross):
+        for up in (True, False):
+            place_z = z if up else nz - 1 - z
+            ahead = nz - 1 - place_z
+            t = g - 2 * place_z
+            q = t // period
+            k = t % period
+            l = SECTIONS - 1 - q
+            n = k % 2
+            inside = jnp.logical_and(t >= 0, q < SECTIONS)
+
+            @pl.when(jnp.logical_and(inside, k < 2 * ahead))
+            def _(up=up, place_z=place_z, q=q, k=k, l=l, n=n):
+                far = nz - 1 - k // 2
+                p = far if up else nz - 1 - far
+                unit = gall.at[l, p, n]
+
+                buf, sem = g_from(p, n, up)
+                way, slot = 0 if up else 1, k % 4
+                leaving = gleave.at[way, slot]
+
+                @pl.when(jnp.logical_or(q > 0, k >= 4))
+                def _():
+                    wait_bytes(leaving, ga_ss.at[way, slot])
+
+                @pl.when(place_z > 0)
+                def _():
+                    wait_bytes(buf, sem)
+                    leaving[...] = (unit[...].astype(F32) + buf[...].astype(F32)).astype(BF16)
+
+                @pl.when(place_z == 0)
+                def _():
+                    leaving[...] = unit[...]
+
+                remote(leaving, buf, ga_ss.at[way, slot], sem, to_end if up else to_start).start()
+
+            @pl.when(jnp.logical_and(inside, k >= 2 * ahead))
+            def _(up=up, place_z=place_z, ahead=ahead, k=k, l=l, n=n):
+                back = (k - 2 * ahead) // 2
+                p = z - back if up else z + back
+                unit = gall.at[l, p, n]
+
+                @pl.when(back == 0)
+                def _():
+                    if up:
+                        whole = unit[...].astype(F32)
+                        for way, there in ((True, z > 0), (False, z < nz - 1)):
+                            buf, sem = g_from(p, n, way)
+
+                            @pl.when(there)
+                            def _(buf=buf, sem=sem):
+                                wait_bytes(buf, sem)
+
+                            whole = whole + jnp.where(there, buf[...].astype(F32), 0.0)
+                        unit[...] = whole.astype(BF16)
+                        g_ready(l, p, n, cross)
+
+                @pl.when(back > 0)
+                def _():
+                    wait_bytes(unit, ga_rs.at[l, p, n])
+                    g_ready(l, p, n, cross)
+
+                @pl.when(ahead > 0)
+                def _():
+                    way = 0 if up else 1
+                    remote(unit, unit, go_ss.at[l, p, n, way], ga_rs.at[l, p, n], to_end if up else to_start).start()
 
     def cross_back(b):
         m = b % 4
@@ -748,10 +860,10 @@
 
         @pl.when(b >= 4)
         def _():
-            wait_bytes(xsend.at[m], xp_ss.at[m])
-
-        xsend[m] = (pkeep[m, 1] + sibrecv[b % 8, 1].astype(F32)).astype(BF16)
-        remote(xsend.at[m], xrecv.at[b % 8], xp_ss.at[m], xp_rs.at[b % 8], to_x).start()
+            wait_bytes(ysend.at[m], xp_ss.at[m])
+
+        ysend[m] = (pkeep[m, 1] + sibrecv[b % 8, 1].astype(F32)).astype(BF16)
+        remote(ysend.at[m], xrecv.at[b % 8], xp_ss.at[m], xp_rs.at[b % 8], to_x).start()
         pkeep[m, 0] = pkeep[m, 0] + sibrecv[b % 8, 0].astype(F32)
 
     def join_back(b):
@@ -775,22 +887,7 @@
                 def _(src=src):
                     local_copy(src, ging.at[me], gi_rs.at[me])
 
-    def gather_weights(l):
-        wait_bytes(grecv.at[l % 2], gr_rs.at[l % 2])
-
-        def add(k, carry):
-            return carry + grecv[l % 2, k].astype(F32)
-
-        start = gsend[l % 2, pl.ds(pl.multiple_of(z * part, part), part), :].astype(F32)
-        gpiece[l] = lax.fori_loop(0, nz - 1, add, start).astype(BF16)
-
-        @pl.when(l != s)
-        def _():
-            remote(gpiece.at[l], gout.at[c, z, s], gx_ss.at[l], gx_rs.at[s], (l, r)).start()
-
-        @pl.when(l == s)
-        def _():
-            local_copy(gpiece.at[l], gout.at[c, z, s], gx_rs.at[s])
+    first_step = 6
 
     def backward_tick(k, _):
         @pl.when(k >= 4)
@@ -800,6 +897,10 @@
         @pl.when(k < items)
         def _():
             act_back(k)
+
+        @pl.when(k >= first_step)
+        def _():
+            g_step(k - first_step, False)
 
         @pl.when(jnp.logical_and(k >= 1, k < items + 1))
         def _():
@@ -810,10 +911,6 @@
             input_back(k - 2)
             weight_back(k - 2)
             cross_back(k - 2)
-
-        @pl.when(jnp.logical_and(k >= 9, k % 4 == 1))
-        def _():
-            gather_weights(SECTIONS - 1 - (k - 9) // 4)
 
         return 0
 
@@ -839,42 +936,39 @@
             def _(t=t):
                 local_copy(small.at[t], smallg.at[me], sm_rs.at[me])
 
-    gather_weights(0)
-    for t in range(SECTIONS):
-        wait_bytes(gout.at[c, z, t], gx_rs.at[t])
-
-    def g_move(p, up, down, finish):
-        @pl.when(jnp.logical_and(p >= 0, p < nz))
-        def _():
-            block = gout.at[c, p]
-            if not finish:
-                @pl.when(p != z)
-                def _():
-                    wait_bytes(block, gz_rs.at[p])
-            if up:
-                @pl.when(z + 1 < nz)
-                def _():
-                    copy = remote(block, block, gz_up.at[p], gz_rs.at[p], (s, r + 2))
-                    copy.wait_send() if finish else copy.start()
-            if down:
-                @pl.when(z >= 1)
-                def _():
-                    copy = remote(block, block, gz_dn.at[p], gz_rs.at[p], (s, r - 2))
-                    copy.wait_send() if finish else copy.start()
-            copy = remote(block, block, gz_sb.at[p], gs_rs.at[p], to_c)
-            copy.wait_send() if finish else copy.start()
-
-    def g_hops(finish):
-        g_move(z, True, True, finish)
-
-        def one(d, _):
-            g_move(z - d, True, False, finish)
-            g_move(z + d, False, True, finish)
-            return 0
-
-        lax.fori_loop(1, nz, one, 0)
-
-    g_hops(False)
+    steps_done = items + 4 - first_step
+    steps_all = SECTIONS * period + 2 * (nz - 1)
+
+    def whole_at(q, p, n):
+        return q * period + 2 * (nz - 1) + 2 * jnp.abs(z - p) + n
+
+    def cross_early(k, _):
+        q, p, n = k // period, k % period // 2, k % 2
+        l = SECTIONS - 1 - q
+
+        @pl.when(whole_at(q, p, n) < steps_done)
+        def _():
+            g_ready(l, p, n, True)
+
+        return 0
+
+    lax.fori_loop(0, SECTIONS * period, cross_early, 0)
+
+    def late_step(g, _):
+        g_step(g, True)
+        return 0
+
+    lax.fori_loop(steps_done, steps_all, late_step, 0)
+
+    def to_other_core(k, _):
+        p, n = k // 2, k % 2
+        for t in (s_x, s_y, s_d):
+            unit = gout.at[c, t, p, n]
+            wait_bytes(unit, gx_rs.at[t, p, n])
+            remote(unit, unit, gs_ss.at[t, p, n], gs_rs.at[t, p, n], to_c).start()
+        return 0
+
+    lax.fori_loop(0, period, to_other_core, 0)
 
     restore = (row_of == frame_at).astype(BF16)
     for e in range(8):
@@ -888,26 +982,51 @@
         for n, dst in enumerate((grad_gain, grad_shift, grad_rec, grad_bias)):
             dst[0:1, e * bw : e * bw + width(e)] = smallg[e, n : n + 1, : width(e)]
 
-    def drain_z(p, _):
-        wait_bytes(gout.at[1 - c, p], gs_rs.at[p])
+    def drain_units(k, _):
+        p, n = k // 2, k % 2
+        unit = gall.at[0, p, n]
+        for t in range(SECTIONS):
+            wait_bytes(unit, gs_rs.at[t, p, n])
+            wait_bytes(unit, gs_ss.at[t, p, n])
+
+            @pl.when(t != s)
+            def _(t=t):
+                wait_bytes(unit, gx_ss.at[t, p, n])
+
+            @pl.when(t == s)
+            def _(t=t):
+                wait_bytes(unit, gx_rs.at[t, p, n])
+
+            @pl.when(jnp.logical_and(p <= z, z < nz - 1))
+            def _(t=t):
+                wait_bytes(unit, go_ss.at[t, p, n, 0])
+
+            @pl.when(jnp.logical_and(p >= z, z > 0))
+            def _(t=t):
+                wait_bytes(unit, go_ss.at[t, p, n, 1])
+
         return 0
 
-    lax.fori_loop(0, nz, drain_z, 0)
-    g_hops(True)
-    for l in range(2):
-        wait_bytes(grecv.at[l], gr_ss.at[l])
+    lax.fori_loop(0, period, drain_units, 0)
+    for way in range(2):
+        ahead = nz - 1 - z if way == 0 else z
+        for slot in range(4):
+            @pl.when(slot < 2 * ahead)
+            def _(way=way, slot=slot):
+                wait_bytes(gleave.at[way, slot], ga_ss.at[way, slot])
+
     for l in range(SECTIONS):
         @pl.when(l != s)
         def _(l=l):
-            wait_bytes(gpiece.at[l], gx_ss.at[l])
             for k in range(2):
-                wait_bytes(w_rows_of(l, k), w_fs.at[l, k])
-
-        wait_bytes(ysend.at[l], y_ss.at[l])
+                for n in range(2):
+                    wait_bytes(w_unit(l, k, n), w_fs.at[l, k, n])
+
+        wait_bytes(pre_recv.at[pl.ds(0, nz - 1), pl.ds(4 * l, 4)], pre_ss.at[l])
         wait_bytes(ex_recv.at[l, pl.ds(0, nz - 1)], ex_ss.at[l])
         wait_bytes(e1_recv.at[l, pl.ds(0, nz - 1)], e1_ss.at[l])
         wait_bytes(sibsend.at[l], sb_ss.at[l])
-        wait_bytes(xsend.at[l], xp_ss.at[l])
+        wait_bytes(ysend.at[l], xp_ss.at[l])
         for h in range(2):
             @pl.when(not_me(l, h))
             def _(l=l, h=h):
@@ -935,13 +1054,16 @@
     lax.fori_loop(0, items, drain, 0)
     for n in range(4):
         wait_bytes(in_dst, in_ss.at[n])
+    for slot in range(4):
+        @pl.when(slot != mine)
+        def _(slot=slot):
+            wait_bytes(in_dst, in_fs.at[slot])
+
     for n in range(3):
-        wait_bytes(in_dst, in_fs.at[n])
         wait_bytes(par.at[s], par_ss.at[n])
         for k in range(2):
             wait_bytes(wx.at[n, :, pl.ds(k * bw, bw)], w_ss.at[n, k])
     wait_bytes(flagbuf.at[c], flag_ss.at[0])
-    wait_bytes(pre_recv.at[pl.ds(0, nz - 1)], pre_ss)
 
 
 def run_kernel(sz, *args):
@@ -983,18 +1105,17 @@
         vm((4, 2, rows, bw), F32),
         vm((4, 2, rows, bw), BF16),
         vm((8, 2, rows, bw), BF16),
-        vm((4, rows, bw), BF16),
         vm((8, rows, bw), BF16),
         vm((4 * bw, 2 * bw), F32),
-        vm((2, 4 * bw, 2 * bw), BF16),
-        vm((2, nz - 1, part, 2 * bw), BF16),
-        vm((SECTIONS, part, 2 * bw), BF16),
+        vm((SECTIONS, nz, 2, part, bw), BF16),
+        vm((nz + 1, 2, part, bw), BF16),
+        vm((2, 4, part, bw), BF16),
         vm((SECTIONS,) + step, F32),
         vm((nz - 1, SECTIONS) + step, F32),
         vm((4, 2, half, bw), BF16),
         vm((2, sz.seqs, sz.frames, sz.hidden), BF16),
         vm((2, 8, half, bw), BF16),
-        vm((3, bw, sz.hidden), BF16),
+        vm((2, bw, sz.hidden), BF16),
         vm((3, 2, 2 * bw, bw), BF16),
         vm((8, half, bw), BF16),
         vm((8, half, bw), BF16),
@@ -1002,14 +1123,18 @@
         vm(step, F32),
     ]
     sems = [
-        dma((2,)), dma((3,)), dma((4,)), dma((3,)), dma((4, 2)), dma((4, 2)), dma((4, 2)),
-        dma((3,)), dma((4,)), dma((1,)), dma((2,)), dma((3, 2)), dma((4, 4)), dma((4, 2)),
-        dma, dma, dma((items,)), dma((items,)), dma((items,)), dma((items,)), dma((items,)), dma((items,)),
+        dma((2,)), dma((2,)), dma((4,)), dma((4,)), dma((4, 2)), dma((4, 2)), dma((4, 2)),
+        dma((3,)), dma((4,)), dma((1,)), dma((2,)),
+        dma((3, 2)), dma((4, 4)), dma((4, 2, 2)), dma((4, 2, 2)),
+        dma((4,)), dma((4,)),
+        dma((items,)), dma((items,)), dma((items,)), dma((items,)), dma((items,)), dma((items,)),
         dma((4,)), dma((8,)), dma((4,)), dma((8,)),
         dma((4, 2)), dma((8,)), dma((4,)), dma((8,)),
         dma((8,)), dma((8,)), dma((4,)), dma((8,)), dma((4,)), dma((8,)),
-        dma((4, 2)), dma((8,)), dma((2,)), dma((2,)), dma((4,)), dma((4,)),
-        dma((nz,)), dma((nz,)), dma((nz,)), dma((nz,)), dma((nz,)), dma, dma, dma((4, 2)), dma((8,)),
+        dma((4, 2)), dma((8,)),
+        dma((2, 4)), dma((4, nz, 2)), dma((4, nz, 2, 2)), dma((nz + 1, 2)),
+        dma((4, nz, 2)), dma((4, nz, 2)), dma((4, nz, 2)), dma((4, nz, 2)),
+        dma, dma, dma((4, 2)), dma((8,)),
     ]
     anywhere = pl.BlockSpec(memory_space=pl.ANY)
     inside = pl.BlockSpec(memory_space=pltpu.VMEM)
@@ -1017,7 +1142,7 @@
     vector = jax.ShapeDtypeStruct((1, sz.hidden), F32)
     return pl.pallas_call(
         functools.partial(kernel, sz),
-        out_shape=(frames, frames) + (vector,) * 4 + (jax.ShapeDtypeStruct((2, nz, 4, part, 2 * bw), BF16),),
+        out_shape=(frames, frames) + (vector,) * 4 + (jax.ShapeDtypeStruct((2, SECTIONS, nz, 2, part, bw), BF16),),
         in_specs=[anywhere] * 3 + [inside] * 6,
         out_specs=(inside,) * 6 + (anywhere,),
         scratch_shapes=scratch + sems,
@@ -1040,14 +1165,14 @@
                     for e in range(8):
                         n, x, c = (0 if e // 4 == yy else 1), e % 4 // 2, e % 2
                         wide = bw if e < 7 else sz.last
-                        value = src[c, p, x, :, n * bw : n * bw + wide].astype(F32)
+                        value = src[c, x, p, n, :, :wide].astype(F32)
                         dst[p * part : (p + 1) * part, e * bw : e * bw + wide] = value
 
     return pl.pallas_call(
         body,
         grid=(8,),
         out_shape=jax.ShapeDtypeStruct((hidden, hidden), F32),
-        in_specs=[pl.BlockSpec((2, count, 2, part, 2 * bw), lambda q: (0, q % 4, q // 4, 0, 0))],
+        in_specs=[pl.BlockSpec((2, 2, count, 2, part, bw), lambda q: (0, q // 4, q % 4, 0, 0, 0))],
         out_specs=pl.BlockSpec((bw, hidden), lambda q: (q, 0)),
         compiler_params=pltpu.CompilerParams(vmem_limit_bytes=32 * 2**20),
     )(pieces)

time: 385 us -> 326 us (0.85)
  Pallas kernels: 376 us -> 315 us
    pallas_call x1, Pallas kernels: 370 us -> 309 us  [run_kernel(): pl.pallas_call(functools.partial(kernel, sz), out_shape=(frames, frames)...]
where the time goes in v3:
time: 326 us; the launch traced here: 323 us
  Pallas kernels  315 us (97%)
  local copies, waits for them, and re-layouts  7.38 us (2%)
    pallas_call x1, Pallas kernels, run_kernel(): pl.pallas_call(functools.partial(kernel, sz), out_shape=(frames, frames)...  309 us
    unnamed x20, local copies, waits for them, and re-layouts  7.38 us
    pallas_call x1, Pallas kernels, place_weights(): pl.pallas_call(body, grid=(8,), out_shape=jax.ShapeDtypeStruct((hidden, h...  6.78 us

profile of v3, /device:TPU:0, one launch (start us, length us, event | category | flops | bytes accessed | tf_op | source)
XLA Modules:
  0.0 323.5 jit_solution(9331303912291335721)
XLA Ops:
  0.6 308.6 %shard_map.144 = (bf16[1,2,64,2000]{3,2,1,0:T(8,128)(2,1)}, bf16[1,2,64,2000]{3,2,1,0:T(8,128)(2,1)}, f32[1,2000]{1,0:T(1,128)}, f32[1,2000]{1,0:T(1,128)}, f32[...) custom-call(bf16[1,2,64,2000]{3,2,1,0:T(8,128)(2,1)} %inp_raw.1, ...), custom_call_target="tpu_custom_call" | custom-call | tf_op jit(solution)/shard_map/pallas_call | solution.py:1143
  309.3 0.0 copy-start
  309.3 3.4 %copy-done = bf16[2,4,4,2,256,256]{5,4,3,2,1,0:T(8,128)(2,1)S(1)} copy-done((bf16[2,4,4,2,256,256]{5,4,3,2,1,0:T(8,128)(2,1)S(1)}, bf16[2,4,4,2,256,256]{5,4,3,2,1,0:T(8,128)(2,1)}, u32[]{:S(2)}) %copy-start) | copy-done | bytes 8388632
  312.7 0.0 copy-start.2
  312.7 0.0 copy-start.1
  312.7 0.0 copy-start.6
  312.7 0.0 copy-start.5
  312.7 0.0 copy-start.4
  312.7 0.0 copy-start.3
  312.7 6.8 %shard_map.145 = f32[2000,2000]{1,0:T(8,128)} custom-call(bf16[2,4,4,2,256,256]{5,4,3,2,1,0:T(8,128)(2,1)S(1)} %copy-done), custom_call_target="tpu_custom_call" | custom-call | tf_op jit(solution)/shard_map/pallas_call | solution.py:1171
  319.5 0.0 copy-done.2
  319.5 0.8 copy.22
  320.3 0.0 copy-done.1
  320.3 0.8 copy.23
  321.1 0.0 copy-done.6
  321.1 0.6 copy.24
  321.7 0.0 copy-done.5
  321.7 0.6 copy.25
  322.3 0.0 copy-done.4
  322.3 0.6 copy.26
  322.9 0.0 copy-done.3
  322.9 0.6 copy.27
Async XLA Ops:
  309.3 3.4 %copy-start = (bf16[2,4,4,2,256,256]{5,4,3,2,1,0:T(8,128)(2,1)S(1)}, bf16[2,4,4,2,256,256]{5,4,3,2,1,0:T(8,128)(2,1)}, u32[]{:S(2)}) copy-start(bf16[2,4,4,2,256,256]{5,4,3,2,1,0:T(8,128)(2,1)} %get-tuple-element.16.src) | copy-start | bytes 25165828
  312.7 6.8 %copy-start.2 = (bf16[1,2,64,2000]{3,2,1,0:T(8,128)(2,1)S(1)}, bf16[1,2,64,2000]{3,2,1,0:T(8,128)(2,1)}, u32[]{:S(2)}) copy-start(bf16[1,2,64,2000]{3,2,1,0:T(8,128)(2,1)} %get-tuple-element.28) | copy-start | bytes 1536004
  312.7 7.6 %copy-start.1 = (bf16[1,2,64,2000]{3,2,1,0:T(8,128)(2,1)S(1)}, bf16[1,2,64,2000]{3,2,1,0:T(8,128)(2,1)}, u32[]{:S(2)}) copy-start(bf16[1,2,64,2000]{3,2,1,0:T(8,128)(2,1)} %get-tuple-element.29) | copy-start | bytes 1536004
  312.7 8.4 %copy-start.6 = (f32[1,2000]{1,0:T(1,128)S(1)}, f32[1,2000]{1,0:T(1,128)}, u32[]{:S(2)}) copy-start(f32[1,2000]{1,0:T(1,128)} %get-tuple-element.31) | copy-start | bytes 24004
  312.7 9.0 %copy-start.5 = (f32[1,2000]{1,0:T(1,128)S(1)}, f32[1,2000]{1,0:T(1,128)}, u32[]{:S(2)}) copy-start(f32[1,2000]{1,0:T(1,128)} %get-tuple-element.32) | copy-start | bytes 24004
  312.7 9.6 %copy-start.4 = (f32[1,2000]{1,0:T(1,128)S(1)}, f32[1,2000]{1,0:T(1,128)}, u32[]{:S(2)}) copy-start(f32[1,2000]{1,0:T(1,128)} %get-tuple-element.33) | copy-start | bytes 24004
  312.7 10.2 %copy-start.3 = (f32[1,2000]{1,0:T(1,128)S(1)}, f32[1,2000]{1,0:T(1,128)}, u32[]{:S(2)}) copy-start(f32[1,2000]{1,0:T(1,128)} %get-tuple-element.34) | copy-start | bytes 24004

commit v4 on v3

--- a/solution.py
+++ b/solution.py
@@ -49,12 +49,12 @@
     out, grad_inp, grad_rec, grad_bias, grad_gain, grad_shift, gout,
     mainbuf, wbuf, ysend, yrecv, own, xbuf, states, carry_in, chunk_a, chunk_aex, chunk_s0,
     keepf, validf, flagbuf, par, parblk, pre_send, pre_recv, ex_send, ex_recv, e1_send, e1_recv,
-    scal, slopes, s1ex, dbuf, cex, aexr, dpbuf, pkeep, sibsend, sibrecv, xrecv, gw, gall, gpart, gleave,
+    scal, slopes, s1ex, dbuf, cex, aexr, dpbuf, pkeep, sibsend, sibrecv, xrecv, gw, gall, gpart, gleave, grelay,
     small, small_recv, outbuf, raw, blocks, wst, wx, outg, ging, smallg, blank,
     raw_ls, wst_ls, in_ss, in_fs, in_rs, cot_ss, cot_rs, par_ss, par_rs, flag_ss, flag_rs, w_ss, w_rs, w_fs, w_ps,
     pre_ss, pre_rs, mx_ss, mx_rs, ms_ss, ms_rs, mf_ss, mf_rs, y_ss, y_rs, ex_ss, ex_rs,
     o_ss, o_rs, e1_ss, e1_rs, dp_ss, dp_rs, sb_ss, sb_rs, xp_ss, xp_rs,
-    gi_ss, gi_rs, ga_ss, ga_rs, go_ss, gr_rs, gx_ss, gx_rs, gs_ss, gs_rs, st_ss, st_rs, sm_ss, sm_rs,
+    gi_ss, gi_rs, ga_ss, ga_rs, go_ss, gr_rs, gx_ss, gx_rs, gl_ss, gl_rs, gs_ss, gs_rs, st_ss, st_rs, sm_ss, sm_rs,
 ):
     nz, bw, items, groups, steps = sz.nz, sz.bw, sz.items, sz.groups, sz.steps
     pieces, seqs = sz.pieces, sz.seqs
@@ -567,46 +567,6 @@
                 rows.append(total(jnp.where(inside, value, 0.0)))
         slopes[i] = pack(rows)
 
-    def forward_tick(k, _):
-        @pl.when(k < items)
-        def _():
-            project(k)
-
-        @pl.when(k == 1)
-        def _():
-            inputs_on(3)
-
-        @pl.when(k >= 2)
-        def _():
-            finish_layer(k - 2)
-            carry_slopes(k - 2)
-
-        @pl.when(jnp.logical_and(k >= 1, k < items + 1))
-        def _():
-            moments(k - 1)
-
-        @pl.when(jnp.logical_and(k + 1 >= 4, k + 1 < items))
-        def _():
-            arrived(k + 1)
-
-        @pl.when(k < 12)
-        def _():
-            for n in range(4):
-                @pl.when(k % 4 == n)
-                def _(n=n):
-                    w_pass(k // 4 + 1, n // 2, n % 2)
-
-            @pl.when(k % 4 == 1)
-            def _():
-                send_decays(k // 4 + 1)
-
-        return 0
-
-    lax.fori_loop(0, items + 2, forward_tick, 0)
-
-    for m in range(4):
-        wait_bytes(ysend.at[m], y_ss.at[m])
-
     def back_index(b):
         l, m = SECTIONS - 1 - b // 4, b % 4
         return l, m, l * 4 + m
@@ -773,19 +733,23 @@
         return gpart.at[p + 1 if up else p, n], gr_rs.at[p + 1 if up else p, n]
 
     def g_ready(l, p, n, cross):
-        unit = gall.at[l, p, n]
-        if cross:
-            to_section(l, unit, gout.at[c, s, p, n], gx_ss.at[l, p, n], gx_rs.at[s, p, n], gs_ss.at[s, p, n], gs_rs.at[s, p, n])
-
-    def to_section(l, src, dst, cross_ss, cross_rs, other_ss, other_rs):
-        @pl.when(l != s)
-        def _():
-            remote(src, dst, cross_ss, cross_rs, (l, r)).start()
+        if not cross:
+            return
+        unit, place_out = gall.at[l, p, n], gout.at[c, s, p, n]
+        by_relay = jnp.logical_and(l == s_d, n == 1)
+
+        @pl.when(jnp.logical_and(l != s, jnp.logical_not(by_relay)))
+        def _():
+            remote(unit, place_out, gx_ss.at[l, p, n], gx_rs.at[s, p, n], (l, r)).start()
+
+        @pl.when(by_relay)
+        def _():
+            remote(unit, grelay.at[p], gx_ss.at[l, p, n], gl_rs.at[p], to_y).start()
 
         @pl.when(l == s)
         def _():
-            local_copy(src, dst, cross_rs)
-            remote(src, dst, other_ss, other_rs, to_c).start()
+            local_copy(unit, place_out, gx_rs.at[s, p, n])
+            remote(unit, place_out, gs_ss.at[s, p, n], gs_rs.at[s, p, n], to_c).start()
 
     def g_step(g, cross):
         for up in (True, False):
@@ -858,6 +822,10 @@
         m = b % 4
         wait_bytes(sibrecv.at[b % 8], sb_rs.at[b % 8])
 
+        @pl.when(b < 4)
+        def _():
+            wait_bytes(ysend.at[m], y_ss.at[m])
+
         @pl.when(b >= 4)
         def _():
             wait_bytes(ysend.at[m], xp_ss.at[m])
@@ -889,12 +857,45 @@
 
     first_step = 6
 
-    def backward_tick(k, _):
+    def forward_tick(k):
+        @pl.when(k < items)
+        def _():
+            project(k)
+
+        @pl.when(k == 1)
+        def _():
+            inputs_on(3)
+
+        @pl.when(jnp.logical_and(k >= 2, k < items + 2))
+        def _():
+            finish_layer(k - 2)
+            carry_slopes(k - 2)
+
+        @pl.when(jnp.logical_and(k >= 1, k < items + 1))
+        def _():
+            moments(k - 1)
+
+        @pl.when(jnp.logical_and(k + 1 >= 4, k + 1 < items))
+        def _():
+            arrived(k + 1)
+
+        @pl.when(k < 12)
+        def _():
+            for n in range(4):
+                @pl.when(k % 4 == n)
+                def _(n=n):
+                    w_pass(k // 4 + 1, n // 2, n % 2)
+
+            @pl.when(k % 4 == 1)
+            def _():
+                send_decays(k // 4 + 1)
+
+    def backward_tick(k):
         @pl.when(k >= 4)
         def _():
             join_back(k - 4)
 
-        @pl.when(k < items)
+        @pl.when(jnp.logical_and(k >= 0, k < items))
         def _():
             act_back(k)
 
@@ -912,11 +913,91 @@
             weight_back(k - 2)
             cross_back(k - 2)
 
+    start = items - 2
+
+    def tick(k, _):
+        forward_tick(k)
+        backward_tick(k - start)
         return 0
 
-    lax.fori_loop(0, items + 4, backward_tick, 0)
+    lax.fori_loop(0, start + items + 4, tick, 0)
 
     send_z(small, lambda k: small_recv.at[k], st_ss, st_rs)
+    steps_done = items + 4 - first_step
+    steps_all = SECTIONS * period + 2 * (nz - 1)
+
+    def whole_at(q, p, n):
+        return q * period + 2 * (nz - 1) + 2 * jnp.abs(z - p) + n
+
+    def crosses_at(q, p, n):
+        early = whole_at(q, p, n) < steps_done
+        return jnp.where(early, steps_done + 2 * p + n, whole_at(q, p, n))
+
+    def cross_early(g):
+        p, n = (g - steps_done) // 2, (g - steps_done) % 2
+
+        @pl.when(p < nz)
+        def _():
+            for q in range(SECTIONS):
+                @pl.when(whole_at(q, p, n) < steps_done)
+                def _(q=q):
+                    g_ready(SECTIONS - 1 - q, p, n, True)
+
+    def relay_lag(q):
+        return jnp.where(q < 2, 12, 4)
+
+    def g_relay(g):
+        q = SECTIONS - 1 - s_x
+
+        def one(p, _):
+            @pl.when(crosses_at(q, p, 1) + relay_lag(q) == g)
+            def _():
+                wait_bytes(grelay.at[p], gl_rs.at[p])
+                remote(grelay.at[p], gout.at[c, s_y, p, 1], gl_ss.at[p], gx_rs.at[s_y, p, 1], to_x).start()
+
+            return 0
+
+        lax.fori_loop(0, nz, one, 0)
+
+    def g_to_other_core(g):
+        q = SECTIONS - 1 - s
+        lag = jnp.where(q < 2, 14, 6)
+
+        def one(p, _):
+            for n in range(2):
+                sent = crosses_at(q, p, n) + lag
+
+                def onward(t, n=n):
+                    unit = gout.at[c, t, p, n]
+                    wait_bytes(unit, gx_rs.at[t, p, n])
+                    remote(unit, unit, gs_ss.at[t, p, n], gs_rs.at[t, p, n], to_c).start()
+
+                @pl.when(sent == g)
+                def _(n=n):
+                    onward(s_x)
+                    onward(s_y)
+                    if n == 0:
+                        onward(s_d)
+
+                if n == 1:
+                    @pl.when(sent + relay_lag(q) == g)
+                    def _():
+                        onward(s_d)
+            return 0
+
+        lax.fori_loop(0, nz, one, 0)
+
+    def late_step(g, _):
+        g_step(g, True)
+        cross_early(g)
+        g_relay(g)
+        g_to_other_core(g)
+        return 0
+
+    def late_steps(first, last_step):
+        lax.fori_loop(first, last_step, late_step, 0)
+
+    late_steps(steps_done, steps_done + 3)
     wait_bytes(small_recv, st_rs)
     wait_bytes(small_recv, st_ss)
 
@@ -936,39 +1017,7 @@
             def _(t=t):
                 local_copy(small.at[t], smallg.at[me], sm_rs.at[me])
 
-    steps_done = items + 4 - first_step
-    steps_all = SECTIONS * period + 2 * (nz - 1)
-
-    def whole_at(q, p, n):
-        return q * period + 2 * (nz - 1) + 2 * jnp.abs(z - p) + n
-
-    def cross_early(k, _):
-        q, p, n = k // period, k % period // 2, k % 2
-        l = SECTIONS - 1 - q
-
-        @pl.when(whole_at(q, p, n) < steps_done)
-        def _():
-            g_ready(l, p, n, True)
-
-        return 0
-
-    lax.fori_loop(0, SECTIONS * period, cross_early, 0)
-
-    def late_step(g, _):
-        g_step(g, True)
-        return 0
-
-    lax.fori_loop(steps_done, steps_all, late_step, 0)
-
-    def to_other_core(k, _):
-        p, n = k // 2, k % 2
-        for t in (s_x, s_y, s_d):
-            unit = gout.at[c, t, p, n]
-            wait_bytes(unit, gx_rs.at[t, p, n])
-            remote(unit, unit, gs_ss.at[t, p, n], gs_rs.at[t, p, n], to_c).start()
-        return 0
-
-    lax.fori_loop(0, period, to_other_core, 0)
+    late_steps(steps_done + 3, steps_done + 9)
 
     restore = (row_of == frame_at).astype(BF16)
     for e in range(8):
@@ -982,6 +1031,8 @@
         for n, dst in enumerate((grad_gain, grad_shift, grad_rec, grad_bias)):
             dst[0:1, e * bw : e * bw + width(e)] = smallg[e, n : n + 1, : width(e)]
 
+    late_steps(steps_done + 9, steps_all + 10)
+
     def drain_units(k, _):
         p, n = k // 2, k % 2
         unit = gall.at[0, p, n]
@@ -1008,6 +1059,12 @@
         return 0
 
     lax.fori_loop(0, period, drain_units, 0)
+
+    def drain_relay(p, _):
+        wait_bytes(grelay.at[p], gl_ss.at[p])
+        return 0
+
+    lax.fori_loop(0, nz, drain_relay, 0)
     for way in range(2):
         ahead = nz - 1 - z if way == 0 else z
         for slot in range(4):
@@ -1110,6 +1167,7 @@
         vm((SECTIONS, nz, 2, part, bw), BF16),
         vm((nz + 1, 2, part, bw), BF16),
         vm((2, 4, part, bw), BF16),
+        vm((nz, part, bw), BF16),
         vm((SECTIONS,) + step, F32),
         vm((nz - 1, SECTIONS) + step, F32),
         vm((4, 2, half, bw), BF16),
@@ -1133,7 +1191,7 @@
         dma((8,)), dma((8,)), dma((4,)), dma((8,)), dma((4,)), dma((8,)),
         dma((4, 2)), dma((8,)),
         dma((2, 4)), dma((4, nz, 2)), dma((4, nz, 2, 2)), dma((nz + 1, 2)),
-        dma((4, nz, 2)), dma((4, nz, 2)), dma((4, nz, 2)), dma((4, nz, 2)),
+        dma((4, nz, 2)), dma((4, nz, 2)), dma((nz,)), dma((nz,)), dma((4, nz, 2)), dma((4, nz, 2)),
         dma, dma, dma((4, 2)), dma((8,)),
     ]
     anywhere = pl.BlockSpec(memory_space=pl.ANY)
@@ -1152,12 +1210,19 @@
     )(*args)
 
 
-def place_weights(sz, pieces):
+def place_weights(sz, pieces, *others):
     bw, part, hidden = sz.bw, sz.part, sz.hidden
     count = bw // part
 
-    def body(src, dst):
+    def body(*refs):
+        src, dst = refs[0], refs[1 + len(others)]
         upper = pl.program_id(0) // 4
+
+        @pl.when(pl.program_id(0) == 0)
+        def _():
+            for n in range(len(others)):
+                refs[2 + len(others) + n][...] = refs[1 + n][...]
+
         for yy in range(2):
             @pl.when(upper == yy)
             def _(yy=yy):
@@ -1168,21 +1233,23 @@
                         value = src[c, x, p, n, :, :wide].astype(F32)
                         dst[p * part : (p + 1) * part, e * bw : e * bw + wide] = value
 
+    whole = [pl.BlockSpec(v.shape, lambda q, rank=v.ndim: (0,) * rank) for v in others]
     return pl.pallas_call(
         body,
         grid=(8,),
-        out_shape=jax.ShapeDtypeStruct((hidden, hidden), F32),
-        in_specs=[pl.BlockSpec((2, 2, count, 2, part, bw), lambda q: (0, q // 4, q % 4, 0, 0, 0))],
-        out_specs=pl.BlockSpec((bw, hidden), lambda q: (q, 0)),
-        compiler_params=pltpu.CompilerParams(vmem_limit_bytes=32 * 2**20),
-    )(pieces)
+        out_shape=[jax.ShapeDtypeStruct((hidden, hidden), F32)] + [jax.ShapeDtypeStruct(v.shape, v.dtype) for v in others],
+        in_specs=[pl.BlockSpec((2, 2, count, 2, part, bw), lambda q: (0, q // 4, q % 4, 0, 0, 0))] + whole,
+        out_specs=[pl.BlockSpec((bw, hidden), lambda q: (q, 0))] + whole,
+        compiler_params=pltpu.CompilerParams(vmem_limit_bytes=60 * 2**20),
+    )(pieces, *others)
 
 
 def local(sz, inputs, resets, valid_mask, weights, recurrence, state_bias, norm_gain, norm_shift, cotangent):
-    outputs, grad_inputs, rec, bias, gain, shift, pieces = run_kernel(
+    *others, pieces = run_kernel(
         sz, inputs, cotangent, weights, resets, valid_mask, recurrence, state_bias, norm_gain, norm_shift
     )
-    return outputs, grad_inputs, place_weights(sz, pieces)[None], rec, bias, gain, shift
+    grad_weights, outputs, grad_inputs, *vectors = place_weights(sz, pieces, *others)
+    return outputs, grad_inputs, grad_weights[None], *vectors
 
 
 def solution(mesh):

time: 326 us -> 306 us (0.939)
  Pallas kernels: 315 us -> 305 us
  local copies, waits for them, and re-layouts: 7.38 us -> 0 us
    pallas_call x1, Pallas kernels: 309 us -> 294 us  [run_kernel(): pl.pallas_call(functools.partial(kernel, sz), out_shape=(frames, frames)...]
    unnamed x20 -> x0, local copies, waits for them, and re-layouts: 7.38 us -> none
    pallas_call x1, Pallas kernels: 6.78 us -> 11.2 us  [place_weights(): pl.pallas_call(body, grid=(8,), out_shape=[jax.ShapeDtypeStruct((hidden,...]
where the time goes in v4:
time: 306 us
  Pallas kernels  305 us (100%)
    pallas_call x1, Pallas kernels, run_kernel(): pl.pallas_call(functools.partial(kernel, sz), out_shape=(frames, frames)...  294 us
    pallas_call x1, Pallas kernels, place_weights(): pl.pallas_call(body, grid=(8,), out_shape=[jax.ShapeDtypeStruct((hidden,...  11.2 us

profile of v4, /device:TPU:0, one launch (start us, length us, event | category | flops | bytes accessed | tf_op | source)
XLA Modules:
  0.0 305.8 jit_solution(3334455765816874379)
XLA Ops:
  0.6 293.9 %shard_map.144 = (bf16[1,2,64,2000]{3,2,1,0:T(8,128)(2,1)}, bf16[1,2,64,2000]{3,2,1,0:T(8,128)(2,1)}, f32[1,2000]{1,0:T(1,128)}, f32[1,2000]{1,0:T(1,128)}, f32[...) custom-call(bf16[1,2,64,2000]{3,2,1,0:T(8,128)(2,1)} %inp_raw.1, ...), custom_call_target="tpu_custom_call" | custom-call | tf_op jit(solution)/shard_map/pallas_call | solution.py:1201
  294.5 11.2 %shard_map.145 = (f32[2000,2000]{1,0:T(8,128)}, bf16[1,2,64,2000]{3,2,1,0:T(8,128)(2,1)}, bf16[1,2,64,2000]{3,2,1,0:T(8,128)(2,1)}, f32[1,2000]{1,0:T(1,128)}, f...) custom-call(bf16[2,4,4,2,256,256]{5,4,3,2,1,0:T(8,128)(2,1)} %get-tuple-element.21.refs_0_, ...), custom_call_target="tpu_custom_call" | custom-call | tf_op jit(solution)/shard_map/pallas_call | solution.py:1237

commit v5 on v4

--- a/solution.py
+++ b/solution.py
@@ -171,7 +171,7 @@
 
     def w_load(n, wait):
         yy, j = w_rows[n]
-        k, slot = 4 * yy + j, n % 2
+        k, slot = 4 * yy + j, n % 3
 
         def go(rows):
             copy = pltpu.make_async_copy(
@@ -190,7 +190,7 @@
             go(last)
 
     def w_cut(n, column, toward, dst):
-        slot = n % 2
+        slot = n % 3
         for e in range(8):
             @pl.when(column == e % 4)
             def _(e=e):
@@ -199,7 +199,7 @@
                     dst[place_of] = jnp.zeros((bw, bw), BF16)
                 dst[place_of, :, : width(e)] = wst[slot, :, e * bw : e * bw + width(e)]
 
-    for n in range(2):
+    for n in range(3):
         w_load(n, False)
 
     parblk[...] = jnp.zeros(parblk.shape, F32)
@@ -213,13 +213,16 @@
             row = seqs * (4 * n + m)
             flagbuf[c, row : row + seqs, : sz.frames] = ref[SECTIONS - 1 - m].astype(F32)
 
+    def w_unit(l, j, n):
+        return wbuf.at[l, n, pl.ds(pl.multiple_of(j * bw, bw), bw)]
+
     def w_cross():
         for k in range(2):
             j = 2 * pair_half + k
-            for n, t in enumerate((s_x, s_y, s_d)):
-                src = wx.at[n, :, pl.ds(k * bw, bw)]
-                dst = wbuf.at[s, :, pl.ds(pl.multiple_of(j * bw, bw), bw)]
-                remote(src, dst, w_ss.at[n, k], w_rs.at[s, j], (t, r)).start()
+            for m, t in enumerate((s_x, s_y, s_d)):
+                for n in range(2):
+                    src = wx.at[m, n, pl.ds(k * bw, bw)]
+                    remote(src, w_unit(s, j, n), w_ss.at[m, k, n], w_rs.at[s, j, n], (t, r)).start()
 
     for n in range(6):
         if n == 4:
@@ -241,8 +244,8 @@
             w_cut(n, j_own, y, wbuf.at[s, :, rows])
         else:
             w_cut(n, j_own, y, wbuf.at[s, :, rows])
-        if n + 2 < 6:
-            w_load(n + 2, False)
+        if n + 3 < 6:
+            w_load(n + 3, False)
 
     row = lax.broadcasted_iota(jnp.int32, (half, half), 0)
     col = lax.broadcasted_iota(jnp.int32, (half, half), 1)
@@ -350,19 +353,12 @@
     for slot in range(3):
         inputs_on(slot)
 
-    def w_rows_of(l, j):
-        return wbuf.at[l, :, pl.ds(pl.multiple_of(j * bw, bw), bw)]
-
-    def w_unit(l, j, n):
-        return wbuf.at[l, n, pl.ds(pl.multiple_of(j * bw, bw), bw)]
-
     def w_pass(l, k, n):
         j = 2 * pair_half + k
 
         @pl.when(l != s)
         def _():
-            if n == 0:
-                wait_bytes(w_rows_of(l, j), w_rs.at[l, j])
+            wait_bytes(w_unit(l, j, n), w_rs.at[l, j, n])
             remote(w_unit(l, j, n), w_unit(l, j, n), w_fs.at[l, k, n], w_ps.at[l, k, n], to_pair).start()
 
     def w_arrive(l):
@@ -372,9 +368,11 @@
                 for n in range(2):
                     wait_bytes(w_unit(l, 2 - 2 * pair_half + k, n), w_ps.at[l, k, n])
 
-    for k in range(2):
-        for n in range(2):
-            w_pass(0, k, n)
+    for n in range(2):
+        w_pass(0, 0, n)
+
+    for n in range(2):
+        w_pass(0, 1, n)
     cut_frames(1)
     for t in range(SECTIONS):
         for h in range(2):
@@ -584,7 +582,7 @@
         ends = [None, None]
         sum_act = jnp.zeros((GROUP, bw), F32)
         for h in (1, 0):
-            grad = dbuf[b, h].astype(F32).reshape(steps, GROUP, bw)
+            grad = dbuf[b % 12, h].astype(F32).reshape(steps, GROUP, bw)
             v = jnp.zeros((GROUP, bw), F32)
             for t in range(steps - 1, -1, -1):
                 g = h * steps + t
@@ -727,16 +725,26 @@
                     gall[l, j * count : (j + 1) * count, n] = value
 
     period = 2 * nz
+
+    def unit_of(q, v):
+        return jnp.where(q < 2, SECTIONS - 1 - q, 1 - v), jnp.where(q < 2, v, q - 2)
+
+    def round_of(l, n):
+        return jnp.where(l < 2, 2 + n, SECTIONS - 1 - l), jnp.where(l < 2, 1 - l, n)
+
     to_end, to_start = (s, r + 2), (s, r - 2)
 
-    def g_from(p, n, up):
-        return gpart.at[p + 1 if up else p, n], gr_rs.at[p + 1 if up else p, n]
+    def g_from(p, v, up):
+        return gpart.at[p + 1 if up else p, v], gr_rs.at[p + 1 if up else p, v]
+
+    def relayed(p):
+        return jnp.abs(z - p) % 2 == 0
 
     def g_ready(l, p, n, cross):
         if not cross:
             return
         unit, place_out = gall.at[l, p, n], gout.at[c, s, p, n]
-        by_relay = jnp.logical_and(l == s_d, n == 1)
+        by_relay = jnp.logical_and(l == s_d, relayed(p))
 
         @pl.when(jnp.logical_and(l != s, jnp.logical_not(by_relay)))
         def _():
@@ -744,7 +752,7 @@
 
         @pl.when(by_relay)
         def _():
-            remote(unit, grelay.at[p], gx_ss.at[l, p, n], gl_rs.at[p], to_y).start()
+            remote(unit, grelay.at[p, n], gx_ss.at[l, p, n], gl_rs.at[p, n], to_y).start()
 
         @pl.when(l == s)
         def _():
@@ -758,17 +766,17 @@
             t = g - 2 * place_z
             q = t // period
             k = t % period
-            l = SECTIONS - 1 - q
-            n = k % 2
+            v = k % 2
+            l, n = unit_of(q, v)
             inside = jnp.logical_and(t >= 0, q < SECTIONS)
 
             @pl.when(jnp.logical_and(inside, k < 2 * ahead))
-            def _(up=up, place_z=place_z, q=q, k=k, l=l, n=n):
+            def _(up=up, place_z=place_z, q=q, k=k, l=l, n=n, v=v):
                 far = nz - 1 - k // 2
                 p = far if up else nz - 1 - far
                 unit = gall.at[l, p, n]
 
-                buf, sem = g_from(p, n, up)
+                buf, sem = g_from(p, v, up)
                 way, slot = 0 if up else 1, k % 4
                 leaving = gleave.at[way, slot]
 
@@ -788,7 +796,7 @@
                 remote(leaving, buf, ga_ss.at[way, slot], sem, to_end if up else to_start).start()
 
             @pl.when(jnp.logical_and(inside, k >= 2 * ahead))
-            def _(up=up, place_z=place_z, ahead=ahead, k=k, l=l, n=n):
+            def _(up=up, ahead=ahead, k=k, l=l, n=n, v=v):
                 back = (k - 2 * ahead) // 2
                 p = z - back if up else z + back
                 unit = gall.at[l, p, n]
@@ -798,7 +806,7 @@
                     if up:
                         whole = unit[...].astype(F32)
                         for way, there in ((True, z > 0), (False, z < nz - 1)):
-                            buf, sem = g_from(p, n, way)
+                            buf, sem = g_from(p, v, way)
 
                             @pl.when(there)
                             def _(buf=buf, sem=sem):
@@ -838,14 +846,14 @@
         l, m, i = back_index(b)
         wait_bytes(xrecv.at[b % 8], xp_rs.at[b % 8])
         even = (1 - l % 2).astype(F32)
-        side = dbuf[jnp.maximum(b - 4, 0)].astype(F32).reshape(sz.rows, bw)
+        side = dbuf[jnp.maximum(b - 4, 0) % 12].astype(F32).reshape(sz.rows, bw)
         value = pkeep[m, 0] + xrecv[b % 8].astype(F32) + even * side
-        dbuf[b + 4] = value.astype(BF16).reshape(2, sz.half, bw)
+        dbuf[(b + 4) % 12] = value.astype(BF16).reshape(2, sz.half, bw)
 
         @pl.when(l == 0)
         def _():
             for h in range(2):
-                src = dbuf.at[b + 4, h]
+                src = dbuf.at[(b + 4) % 12, h]
 
                 @pl.when(not_me(SECTIONS - 1 - m, h))
                 def _(src=src, h=h):
@@ -866,25 +874,33 @@
         def _():
             inputs_on(3)
 
+        @pl.when(jnp.logical_and(k >= 1, k < items + 1))
+        def _():
+            moments(k - 1)
+
         @pl.when(jnp.logical_and(k >= 2, k < items + 2))
         def _():
             finish_layer(k - 2)
+
+        @pl.when(jnp.logical_and(k >= 2, k < items + 2))
+        def _():
             carry_slopes(k - 2)
 
-        @pl.when(jnp.logical_and(k >= 1, k < items + 1))
-        def _():
-            moments(k - 1)
-
         @pl.when(jnp.logical_and(k + 1 >= 4, k + 1 < items))
         def _():
             arrived(k + 1)
 
-        @pl.when(k < 12)
-        def _():
+        @pl.when(k < 11)
+        def _():
+            @pl.when(k == 0)
+            def _():
+                w_pass(1, 0, 0)
+
+            unit = k + 1
             for n in range(4):
-                @pl.when(k % 4 == n)
+                @pl.when(unit % 4 == n)
                 def _(n=n):
-                    w_pass(k // 4 + 1, n // 2, n % 2)
+                    w_pass(unit // 4 + 1, n // 2, n % 2)
 
             @pl.when(k % 4 == 1)
             def _():
@@ -926,46 +942,45 @@
     steps_done = items + 4 - first_step
     steps_all = SECTIONS * period + 2 * (nz - 1)
 
-    def whole_at(q, p, n):
-        return q * period + 2 * (nz - 1) + 2 * jnp.abs(z - p) + n
-
-    def crosses_at(q, p, n):
-        early = whole_at(q, p, n) < steps_done
-        return jnp.where(early, steps_done + 2 * p + n, whole_at(q, p, n))
+    def whole_at(l, p, n):
+        q, v = round_of(l, n)
+        return q * period + 2 * (nz - 1) + 2 * jnp.abs(z - p) + v
+
+    def crosses_at(l, p, n):
+        early = whole_at(l, p, n) < steps_done
+        return jnp.where(early, steps_done + 2 * p + n, whole_at(l, p, n))
 
     def cross_early(g):
         p, n = (g - steps_done) // 2, (g - steps_done) % 2
 
         @pl.when(p < nz)
         def _():
-            for q in range(SECTIONS):
-                @pl.when(whole_at(q, p, n) < steps_done)
-                def _(q=q):
-                    g_ready(SECTIONS - 1 - q, p, n, True)
-
-    def relay_lag(q):
-        return jnp.where(q < 2, 12, 4)
+            for l in range(SECTIONS):
+                @pl.when(whole_at(l, p, n) < steps_done)
+                def _(l=l):
+                    g_ready(l, p, n, True)
+
+    def relay_lag(l):
+        return jnp.where(l < 2, 4, 12)
 
     def g_relay(g):
-        q = SECTIONS - 1 - s_x
-
-        def one(p, _):
-            @pl.when(crosses_at(q, p, 1) + relay_lag(q) == g)
-            def _():
-                wait_bytes(grelay.at[p], gl_rs.at[p])
-                remote(grelay.at[p], gout.at[c, s_y, p, 1], gl_ss.at[p], gx_rs.at[s_y, p, 1], to_x).start()
-
-            return 0
-
-        lax.fori_loop(0, nz, one, 0)
-
-    def g_to_other_core(g):
-        q = SECTIONS - 1 - s
-        lag = jnp.where(q < 2, 14, 6)
-
         def one(p, _):
             for n in range(2):
-                sent = crosses_at(q, p, n) + lag
+                @pl.when(jnp.logical_and(relayed(p), crosses_at(s_x, p, n) + relay_lag(s_x) == g))
+                def _(n=n):
+                    wait_bytes(grelay.at[p, n], gl_rs.at[p, n])
+                    remote(grelay.at[p, n], gout.at[c, s_y, p, n], gl_ss.at[p, n], gx_rs.at[s_y, p, n], to_x).start()
+
+            return 0
+
+        lax.fori_loop(0, nz, one, 0)
+
+    def g_to_other_core(g):
+        lag = jnp.where(s < 2, 6, 14)
+
+        def one(p, _):
+            for n in range(2):
+                sent = crosses_at(s, p, n) + lag
 
                 def onward(t, n=n):
                     unit = gout.at[c, t, p, n]
@@ -973,16 +988,14 @@
                     remote(unit, unit, gs_ss.at[t, p, n], gs_rs.at[t, p, n], to_c).start()
 
                 @pl.when(sent == g)
-                def _(n=n):
+                def _(onward=onward):
                     onward(s_x)
                     onward(s_y)
-                    if n == 0:
-                        onward(s_d)
-
-                if n == 1:
-                    @pl.when(sent + relay_lag(q) == g)
-                    def _():
-                        onward(s_d)
+
+                @pl.when(sent + jnp.where(relayed(p), relay_lag(s), 0) == g)
+                def _(onward=onward):
+                    onward(s_d)
+
             return 0
 
         lax.fori_loop(0, nz, one, 0)
@@ -1061,7 +1074,11 @@
     lax.fori_loop(0, period, drain_units, 0)
 
     def drain_relay(p, _):
-        wait_bytes(grelay.at[p], gl_ss.at[p])
+        @pl.when(relayed(p))
+        def _():
+            for n in range(2):
+                wait_bytes(grelay.at[p, n], gl_ss.at[p, n])
+
         return 0
 
     lax.fori_loop(0, nz, drain_relay, 0)
@@ -1093,7 +1110,7 @@
             @pl.when(not_me(SECTIONS - 1 - l, h))
             def _(l=l, h=h):
                 wait_bytes(outbuf.at[l, h], o_ss.at[l, h])
-                wait_bytes(dbuf.at[items + l, h], gi_ss.at[l, h])
+                wait_bytes(dbuf.at[(items + l) % 12, h], gi_ss.at[l, h])
 
     def drain(i, _):
         @pl.when(i < 8)
@@ -1119,7 +1136,9 @@
     for n in range(3):
         wait_bytes(par.at[s], par_ss.at[n])
         for k in range(2):
-            wait_bytes(wx.at[n, :, pl.ds(k * bw, bw)], w_ss.at[n, k])
+            for m in range(2):
+                wait_bytes(wx.at[n, m, pl.ds(k * bw, bw)], w_ss.at[n, k, m])
+
     wait_bytes(flagbuf.at[c], flag_ss.at[0])
 
 
@@ -1155,7 +1174,7 @@
         vm((items,) + step, F32),
         vm((items,) + step, F32),
         vm((4, 2) + step, F32),
-        vm((items + 4, 2, half, bw), BF16),
+        vm((12, 2, half, bw), BF16),
         vm((4, 2) + step, F32),
         vm((4, 2) + step, F32),
         vm((8, 2, rows, bw), BF16),
@@ -1167,13 +1186,13 @@
         vm((SECTIONS, nz, 2, part, bw), BF16),
         vm((nz + 1, 2, part, bw), BF16),
         vm((2, 4, part, bw), BF16),
-        vm((nz, part, bw), BF16),
+        vm((nz, 2, part, bw), BF16),
         vm((SECTIONS,) + step, F32),
         vm((nz - 1, SECTIONS) + step, F32),
         vm((4, 2, half, bw), BF16),
         vm((2, sz.seqs, sz.frames, sz.hidden), BF16),
         vm((2, 8, half, bw), BF16),
-        vm((2, bw, sz.hidden), BF16),
+        vm((3, bw, sz.hidden), BF16),
         vm((3, 2, 2 * bw, bw), BF16),
         vm((8, half, bw), BF16),
         vm((8, half, bw), BF16),
@@ -1181,9 +1200,9 @@
         vm(step, F32),
     ]
     sems = [
-        dma((2,)), dma((2,)), dma((4,)), dma((4,)), dma((4, 2)), dma((4, 2)), dma((4, 2)),
+        dma((2,)), dma((4,)), dma((4,)), dma((4,)), dma((4, 2)), dma((4, 2)), dma((4, 2)),
         dma((3,)), dma((4,)), dma((1,)), dma((2,)),
-        dma((3, 2)), dma((4, 4)), dma((4, 2, 2)), dma((4, 2, 2)),
+        dma((3, 2, 2)), dma((4, 4, 2)), dma((4, 2, 2)), dma((4, 2, 2)),
         dma((4,)), dma((4,)),
         dma((items,)), dma((items,)), dma((items,)), dma((items,)), dma((items,)), dma((items,)),
         dma((4,)), dma((8,)), dma((4,)), dma((8,)),
@@ -1191,7 +1210,7 @@
         dma((8,)), dma((8,)), dma((4,)), dma((8,)), dma((4,)), dma((8,)),
         dma((4, 2)), dma((8,)),
         dma((2, 4)), dma((4, nz, 2)), dma((4, nz, 2, 2)), dma((nz + 1, 2)),
-        dma((4, nz, 2)), dma((4, nz, 2)), dma((nz,)), dma((nz,)), dma((4, nz, 2)), dma((4, nz, 2)),
+        dma((4, nz, 2)), dma((4, nz, 2)), dma((nz, 2)), dma((nz, 2)), dma((4, nz, 2)), dma((4, nz, 2)),
         dma, dma, dma((4, 2)), dma((8,)),
     ]
     anywhere = pl.BlockSpec(memory_space=pl.ANY)
@@ -1217,11 +1236,8 @@
     def body(*refs):
         src, dst = refs[0], refs[1 + len(others)]
         upper = pl.program_id(0) // 4
-
-        @pl.when(pl.program_id(0) == 0)
-        def _():
-            for n in range(len(others)):
-                refs[2 + len(others) + n][...] = refs[1 + n][...]
+        for n in range(len(others)):
+            refs[2 + len(others) + n][...] = refs[1 + n][...]
 
         for yy in range(2):
             @pl.when(upper == yy)
@@ -1233,13 +1249,20 @@
                         value = src[c, x, p, n, :, :wide].astype(F32)
                         dst[p * part : (p + 1) * part, e * bw : e * bw + wide] = value
 
-    whole = [pl.BlockSpec(v.shape, lambda q, rank=v.ndim: (0,) * rank) for v in others]
+    def spec(value):
+        if value.ndim < 4:
+            return pl.BlockSpec(value.shape, lambda q: (0,) * value.ndim)
+        eighth = sz.seqs * sz.frames // 8
+        per_seq = sz.frames // eighth
+        return pl.BlockSpec((1, 1, eighth, hidden), lambda q: (0, q // per_seq, q % per_seq, 0))
+
+    specs = [spec(v) for v in others]
     return pl.pallas_call(
         body,
         grid=(8,),
         out_shape=[jax.ShapeDtypeStruct((hidden, hidden), F32)] + [jax.ShapeDtypeStruct(v.shape, v.dtype) for v in others],
-        in_specs=[pl.BlockSpec((2, 2, count, 2, part, bw), lambda q: (0, q // 4, q % 4, 0, 0, 0))] + whole,
-        out_specs=[pl.BlockSpec((bw, hidden), lambda q: (q, 0))] + whole,
+        in_specs=[pl.BlockSpec((2, 2, count, 2, part, bw), lambda q: (0, q // 4, q % 4, 0, 0, 0))] + specs,
+        out_specs=[pl.BlockSpec((bw, hidden), lambda q: (q, 0))] + specs,
         compiler_params=pltpu.CompilerParams(vmem_limit_bytes=60 * 2**20),
     )(pieces, *others)
 

time: 306 us -> 289 us (0.944)
  Pallas kernels: 305 us -> 288 us
    pallas_call x1, Pallas kernels: 294 us -> 277 us  [run_kernel(): pl.pallas_call(functools.partial(kernel, sz), out_shape=(frames, frames)...]
where the time goes in v5:
time: 289 us
  Pallas kernels  288 us (100%)
    pallas_call x1, Pallas kernels, run_kernel(): pl.pallas_call(functools.partial(kernel, sz), out_shape=(frames, frames)...  277 us
    pallas_call x1, Pallas kernels, place_weights(): pl.pallas_call(body, grid=(8,), out_shape=[jax.ShapeDtypeStruct((hidden,...  10.7 us

profile of v5, /device:TPU:0, one launch (start us, length us, event | category | flops | bytes accessed | tf_op | source)
XLA Modules:
  0.0 288.7 jit_solution(670411891168291412)
XLA Ops:
  0.6 277.3 %shard_map.144 = (bf16[1,2,64,2000]{3,2,1,0:T(8,128)(2,1)}, bf16[1,2,64,2000]{3,2,1,0:T(8,128)(2,1)}, f32[1,2000]{1,0:T(1,128)}, f32[1,2000]{1,0:T(1,128)}, f32[...) custom-call(bf16[1,2,64,2000]{3,2,1,0:T(8,128)(2,1)} %inp_raw.1, ...), custom_call_target="tpu_custom_call" | custom-call | tf_op jit(solution)/shard_map/pallas_call | solution.py:1220
  278.0 10.7 %shard_map.145 = (f32[2000,2000]{1,0:T(8,128)}, bf16[1,2,64,2000]{3,2,1,0:T(8,128)(2,1)}, bf16[1,2,64,2000]{3,2,1,0:T(8,128)(2,1)}, f32[1,2000]{1,0:T(1,128)}, f...) custom-call(bf16[2,4,4,2,256,256]{5,4,3,2,1,0:T(8,128)(2,1)} %get-tuple-element.21.refs_0_, ...), custom_call_target="tpu_custom_call" | custom-call | tf_op jit(solution)/shard_map/pallas_call | solution.py:1260

commit v6 on v5

--- a/solution.py
+++ b/solution.py
@@ -50,7 +50,7 @@
     mainbuf, wbuf, ysend, yrecv, own, xbuf, states, carry_in, chunk_a, chunk_aex, chunk_s0,
     keepf, validf, flagbuf, par, parblk, pre_send, pre_recv, ex_send, ex_recv, e1_send, e1_recv,
     scal, slopes, s1ex, dbuf, cex, aexr, dpbuf, pkeep, sibsend, sibrecv, xrecv, gw, gall, gpart, gleave, grelay,
-    small, small_recv, outbuf, raw, blocks, wst, wx, outg, ging, smallg, blank,
+    small, small_send, small_recv, outbuf, raw, blocks, wst, wx, outg, ging, smallg, blank,
     raw_ls, wst_ls, in_ss, in_fs, in_rs, cot_ss, cot_rs, par_ss, par_rs, flag_ss, flag_rs, w_ss, w_rs, w_fs, w_ps,
     pre_ss, pre_rs, mx_ss, mx_rs, ms_ss, ms_rs, mf_ss, mf_rs, y_ss, y_rs, ex_ss, ex_rs,
     o_ss, o_rs, e1_ss, e1_rs, dp_ss, dp_rs, sb_ss, sb_rs, xp_ss, xp_rs,
@@ -374,17 +374,17 @@
     for n in range(2):
         w_pass(0, 1, n)
     cut_frames(1)
-    for t in range(SECTIONS):
-        for h in range(2):
-            src = blocks.at[1, 2 * t + h]
-
-            @pl.when(not_me(t, h))
-            def _(src=src, t=t, h=h):
-                remote(src, dbuf.at[mine, c], cot_ss.at[t, h], cot_rs.at[mine, c], (t, 2 * z + h)).start()
-
-            @pl.when(jnp.logical_not(not_me(t, h)))
-            def _(src=src):
-                local_copy(src, dbuf.at[mine, c], cot_rs.at[mine, c])
+    def cotangent_out(e):
+        t, h = (s, s_x, s_y, s_d)[e // 2], e % 2
+        src = blocks.at[1, 2 * t + h]
+
+        @pl.when(not_me(t, h))
+        def _():
+            remote(src, dbuf.at[mine, c], cot_ss.at[t, h], cot_rs.at[mine, c], (t, 2 * z + h)).start()
+
+        @pl.when(jnp.logical_not(not_me(t, h)))
+        def _():
+            local_copy(src, dbuf.at[mine, c], cot_rs.at[mine, c])
 
     def arrived(i):
         block = mainbuf.at[i, j_x]
@@ -532,17 +532,6 @@
             block[...] = outbuf[m]
             remote(block, block, mx_ss.at[target], mx_rs.at[target], to_x).start()
             remote(block, block, ms_ss.at[target], ms_rs.at[target], to_c).start()
-
-        @pl.when(jnp.logical_not(to_next))
-        def _():
-            for h in range(2):
-                @pl.when(not_me(SECTIONS - 1 - m, h))
-                def _(h=h):
-                    remote(outbuf.at[m, h], outg.at[me], o_ss.at[m, h], o_rs.at[me], (SECTIONS - 1 - m, 2 * z + h)).start()
-
-                @pl.when(jnp.logical_not(not_me(SECTIONS - 1 - m, h)))
-                def _(h=h):
-                    local_copy(outbuf.at[m, h], outg.at[me], o_rs.at[me])
 
     def carry_slopes(i):
         l, m = i // 4, i % 4
@@ -850,20 +839,23 @@
         value = pkeep[m, 0] + xrecv[b % 8].astype(F32) + even * side
         dbuf[(b + 4) % 12] = value.astype(BF16).reshape(2, sz.half, bw)
 
-        @pl.when(l == 0)
-        def _():
-            for h in range(2):
-                src = dbuf.at[(b + 4) % 12, h]
-
-                @pl.when(not_me(SECTIONS - 1 - m, h))
-                def _(src=src, h=h):
-                    remote(src, ging.at[me], gi_ss.at[m, h], gi_rs.at[me], (SECTIONS - 1 - m, 2 * z + h)).start()
-
-                @pl.when(jnp.logical_not(not_me(SECTIONS - 1 - m, h)))
-                def _(src=src):
-                    local_copy(src, ging.at[me], gi_rs.at[me])
+    def frames_out(m):
+        t = SECTIONS - 1 - m
+        for h in range(2):
+            grads = dbuf.at[(items + m) % 12, h]
+
+            @pl.when(not_me(t, h))
+            def _(h=h, grads=grads):
+                remote(outbuf.at[m, h], outg.at[me], o_ss.at[m, h], o_rs.at[me], (t, 2 * z + h)).start()
+                remote(grads, ging.at[me], gi_ss.at[m, h], gi_rs.at[me], (t, 2 * z + h)).start()
+
+            @pl.when(jnp.logical_not(not_me(t, h)))
+            def _(h=h, grads=grads):
+                local_copy(outbuf.at[m, h], outg.at[me], o_rs.at[me])
+                local_copy(grads, ging.at[me], gi_rs.at[me])
 
     first_step = 6
+
 
     def forward_tick(k):
         @pl.when(k < items)
@@ -889,6 +881,11 @@
         @pl.when(jnp.logical_and(k + 1 >= 4, k + 1 < items))
         def _():
             arrived(k + 1)
+
+        for e in range(8):
+            @pl.when(k == 3 + e)
+            def _(e=e):
+                cotangent_out(e)
 
         @pl.when(k < 11)
         def _():
@@ -938,7 +935,8 @@
 
     lax.fori_loop(0, start + items + 4, tick, 0)
 
-    send_z(small, lambda k: small_recv.at[k], st_ss, st_rs)
+    small_send[...] = pack([small[l, n : n + 1] for l in range(SECTIONS) for n in (2, 3)])
+    send_z(small_send, lambda k: small_recv.at[k], st_ss, st_rs)
     steps_done = items + 4 - first_step
     steps_all = SECTIONS * period + 2 * (nz - 1)
 
@@ -1000,51 +998,123 @@
 
         lax.fori_loop(0, nz, one, 0)
 
+    def sum_small():
+        wait_bytes(small_recv, st_rs)
+        wait_bytes(small_recv, st_ss)
+
+        def add_rest(k, carry):
+            return carry + small_recv[k]
+
+        sums = lax.fori_loop(0, nz - 1, add_rest, small_send[...])
+        for l in range(SECTIONS):
+            rate = jnp.broadcast_to(sums[2 * l : 2 * l + 1], (GROUP, bw))
+            bias = jnp.broadcast_to(sums[2 * l + 1 : 2 * l + 2], (GROUP, bw))
+            small[l] = jnp.where(sub == 2, rate, jnp.where(sub == 3, bias, small[l]))
+        for t in range(SECTIONS):
+            for h in range(2):
+                @pl.when(not_me(t, h))
+                def _(t=t, h=h):
+                    remote(small.at[t], smallg.at[me], sm_ss.at[t, h], sm_rs.at[me], (t, 2 * z + h)).start()
+
+                @pl.when(jnp.logical_not(not_me(t, h)))
+                def _(t=t):
+                    local_copy(small.at[t], smallg.at[me], sm_rs.at[me])
+
+    restore = (row_of == frame_at).astype(BF16)
+
+    def place_block(e):
+        wait_bytes(outg.at[e], o_rs.at[e])
+        wait_bytes(ging.at[e], gi_rs.at[e])
+        for src, dst in ((outg, out), (ging, grad_inp)):
+            value = jnp.dot(restore, src[e], preferred_element_type=F32).astype(BF16)
+            value = value.reshape(seqs, sz.frames, bw)
+            dst[0, :, :, e * bw : e * bw + width(e)] = value[:, :, : width(e)]
+
+    def drain_layers():
+        for l in range(SECTIONS):
+            @pl.when(l != s)
+            def _(l=l):
+                for k in range(2):
+                    for n in range(2):
+                        wait_bytes(w_unit(l, k, n), w_fs.at[l, k, n])
+
+            wait_bytes(pre_recv.at[pl.ds(0, nz - 1), pl.ds(4 * l, 4)], pre_ss.at[l])
+            wait_bytes(ex_recv.at[l, pl.ds(0, nz - 1)], ex_ss.at[l])
+            wait_bytes(e1_recv.at[l, pl.ds(0, nz - 1)], e1_ss.at[l])
+            wait_bytes(sibsend.at[l], sb_ss.at[l])
+            wait_bytes(ysend.at[l], xp_ss.at[l])
+            for h in range(2):
+                @pl.when(not_me(l, h))
+                def _(l=l, h=h):
+                    wait_bytes(dbuf.at[mine, c], cot_ss.at[l, h])
+                    wait_bytes(small.at[l], sm_ss.at[l, h])
+
+                @pl.when(not_me(SECTIONS - 1 - l, h))
+                def _(l=l, h=h):
+                    wait_bytes(outbuf.at[l, h], o_ss.at[l, h])
+                    wait_bytes(dbuf.at[(items + l) % 12, h], gi_ss.at[l, h])
+
+        def drain(i, _):
+            @pl.when(i < 8)
+            def _():
+                wait_bytes(dpbuf.at[i, 0], dp_ss.at[i])
+
+            @pl.when(i >= 4)
+            def _():
+                wait_bytes(mainbuf.at[i, j_own], mx_ss.at[i])
+                wait_bytes(mainbuf.at[i, j_own], ms_ss.at[i])
+                wait_bytes(mainbuf.at[i, j_x], mf_ss.at[i])
+
+            return 0
+
+        lax.fori_loop(0, items, drain, 0)
+        for n in range(4):
+            wait_bytes(in_dst, in_ss.at[n])
+        for slot in range(4):
+            @pl.when(slot != mine)
+            def _(slot=slot):
+                wait_bytes(in_dst, in_fs.at[slot])
+
+        for n in range(3):
+            wait_bytes(par.at[s], par_ss.at[n])
+            for k in range(2):
+                for m in range(2):
+                    wait_bytes(wx.at[n, m, pl.ds(k * bw, bw)], w_ss.at[n, k, m])
+
+        wait_bytes(flagbuf.at[c], flag_ss.at[0])
+
     def late_step(g, _):
         g_step(g, True)
         cross_early(g)
         g_relay(g)
         g_to_other_core(g)
+
+        @pl.when(g == steps_done)
+        def _():
+            for m in range(4):
+                frames_out(m)
+
+        @pl.when(g == steps_done + 5)
+        def _():
+            sum_small()
+
+        for e in range(8):
+            @pl.when(g == steps_done + 16 + e)
+            def _(e=e):
+                place_block(e)
+
+        @pl.when(g == steps_done + 24)
+        def _():
+            drain_layers()
+
         return 0
 
-    def late_steps(first, last_step):
-        lax.fori_loop(first, last_step, late_step, 0)
-
-    late_steps(steps_done, steps_done + 3)
-    wait_bytes(small_recv, st_rs)
-    wait_bytes(small_recv, st_ss)
-
-    def add_rest(k, _):
-        for l in range(SECTIONS):
-            small[l] = small[l] + jnp.where(sub >= 2, small_recv[k, l], 0.0)
-        return 0
-
-    lax.fori_loop(0, nz - 1, add_rest, 0)
-    for t in range(SECTIONS):
-        for h in range(2):
-            @pl.when(not_me(t, h))
-            def _(t=t, h=h):
-                remote(small.at[t], smallg.at[me], sm_ss.at[t, h], sm_rs.at[me], (t, 2 * z + h)).start()
-
-            @pl.when(jnp.logical_not(not_me(t, h)))
-            def _(t=t):
-                local_copy(small.at[t], smallg.at[me], sm_rs.at[me])
-
-    late_steps(steps_done + 3, steps_done + 9)
-
-    restore = (row_of == frame_at).astype(BF16)
+    lax.fori_loop(steps_done, max(steps_all + 10, steps_done + period + 26), late_step, 0)
+
     for e in range(8):
-        wait_bytes(outg.at[e], o_rs.at[e])
-        wait_bytes(ging.at[e], gi_rs.at[e])
         wait_bytes(smallg.at[e], sm_rs.at[e])
-        for src, dst in ((outg, out), (ging, grad_inp)):
-            value = jnp.dot(restore, src[e], preferred_element_type=F32).astype(BF16)
-            value = value.reshape(seqs, sz.frames, bw)
-            dst[0, :, :, e * bw : e * bw + width(e)] = value[:, :, : width(e)]
         for n, dst in enumerate((grad_gain, grad_shift, grad_rec, grad_bias)):
             dst[0:1, e * bw : e * bw + width(e)] = smallg[e, n : n + 1, : width(e)]
-
-    late_steps(steps_done + 9, steps_all + 10)
 
     def drain_units(k, _):
         p, n = k // 2, k % 2
@@ -1088,58 +1158,6 @@
             @pl.when(slot < 2 * ahead)
             def _(way=way, slot=slot):
                 wait_bytes(gleave.at[way, slot], ga_ss.at[way, slot])
-
-    for l in range(SECTIONS):
-        @pl.when(l != s)
-        def _(l=l):
-            for k in range(2):
-                for n in range(2):
-                    wait_bytes(w_unit(l, k, n), w_fs.at[l, k, n])
-
-        wait_bytes(pre_recv.at[pl.ds(0, nz - 1), pl.ds(4 * l, 4)], pre_ss.at[l])
-        wait_bytes(ex_recv.at[l, pl.ds(0, nz - 1)], ex_ss.at[l])
-        wait_bytes(e1_recv.at[l, pl.ds(0, nz - 1)], e1_ss.at[l])
-        wait_bytes(sibsend.at[l], sb_ss.at[l])
-        wait_bytes(ysend.at[l], xp_ss.at[l])
-        for h in range(2):
-            @pl.when(not_me(l, h))
-            def _(l=l, h=h):
-                wait_bytes(dbuf.at[mine, c], cot_ss.at[l, h])
-                wait_bytes(small.at[l], sm_ss.at[l, h])
-
-            @pl.when(not_me(SECTIONS - 1 - l, h))
-            def _(l=l, h=h):
-                wait_bytes(outbuf.at[l, h], o_ss.at[l, h])
-                wait_bytes(dbuf.at[(items + l) % 12, h], gi_ss.at[l, h])
-
-    def drain(i, _):
-        @pl.when(i < 8)
-        def _():
-            wait_bytes(dpbuf.at[i, 0], dp_ss.at[i])
-
-        @pl.when(i >= 4)
-        def _():
-            wait_bytes(mainbuf.at[i, j_own], mx_ss.at[i])
-            wait_bytes(mainbuf.at[i, j_own], ms_ss.at[i])
-            wait_bytes(mainbuf.at[i, j_x], mf_ss.at[i])
-
-        return 0
-
-    lax.fori_loop(0, items, drain, 0)
-    for n in range(4):
-        wait_bytes(in_dst, in_ss.at[n])
-    for slot in range(4):
-        @pl.when(slot != mine)
-        def _(slot=slot):
-            wait_bytes(in_dst, in_fs.at[slot])
-
-    for n in range(3):
-        wait_bytes(par.at[s], par_ss.at[n])
-        for k in range(2):
-            for m in range(2):
-                wait_bytes(wx.at[n, m, pl.ds(k * bw, bw)], w_ss.at[n, k, m])
-
-    wait_bytes(flagbuf.at[c], flag_ss.at[0])
 
 
 def run_kernel(sz, *args):
@@ -1188,7 +1206,8 @@
         vm((2, 4, part, bw), BF16),
         vm((nz, 2, part, bw), BF16),
         vm((SECTIONS,) + step, F32),
-        vm((nz - 1, SECTIONS) + step, F32),
+        vm(step, F32),
+        vm((nz - 1,) + step, F32),
         vm((4, 2, half, bw), BF16),
         vm((2, sz.seqs, sz.frames, sz.hidden), BF16),
         vm((2, 8, half, bw), BF16),
@@ -1231,38 +1250,64 @@
 
 def place_weights(sz, pieces, *others):
     bw, part, hidden = sz.bw, sz.part, sz.hidden
-    count = bw // part
+    count, strips, ring = bw // part, 8, 3
 
     def body(*refs):
-        src, dst = refs[0], refs[1 + len(others)]
-        upper = pl.program_id(0) // 4
+        src, rest = refs[0], refs[1 : 1 + len(others)]
+        dst, rest_out = refs[1 + len(others)], refs[2 + len(others) : 2 + 2 * len(others)]
+        arrived, leaving, in_sem, out_sem, rest_in, rest_sem = refs[2 + 2 * len(others) :][:6]
+        held = refs[8 + 2 * len(others) :]
+
+        def load(q):
+            some = src.at[:, pl.ds(2 * (q // 4), 2), pl.ds(q % 4 * count, count)]
+            return pltpu.make_async_copy(some, arrived.at[q], in_sem.at[q])
+
+        def store(q):
+            rows = bw if q < 7 else sz.last
+            some = dst.at[pl.ds(q * bw, rows)]
+            return pltpu.make_async_copy(leaving.at[q % ring, pl.ds(0, rows)], some, out_sem.at[q % ring])
+
+        def through(n, out):
+            if out:
+                return pltpu.make_async_copy(held[n], rest_out[n], rest_sem.at[n])
+            return pltpu.make_async_copy(rest[n], held[n], rest_in.at[n])
+
+        for q in range(strips):
+            load(q).start()
         for n in range(len(others)):
-            refs[2 + len(others) + n][...] = refs[1 + n][...]
-
-        for yy in range(2):
-            @pl.when(upper == yy)
-            def _(yy=yy):
-                for p in range(count):
-                    for e in range(8):
-                        n, x, c = (0 if e // 4 == yy else 1), e % 4 // 2, e % 2
-                        wide = bw if e < 7 else sz.last
-                        value = src[c, x, p, n, :, :wide].astype(F32)
-                        dst[p * part : (p + 1) * part, e * bw : e * bw + wide] = value
-
-    def spec(value):
-        if value.ndim < 4:
-            return pl.BlockSpec(value.shape, lambda q: (0,) * value.ndim)
-        eighth = sz.seqs * sz.frames // 8
-        per_seq = sz.frames // eighth
-        return pl.BlockSpec((1, 1, eighth, hidden), lambda q: (0, q // per_seq, q % per_seq, 0))
-
-    specs = [spec(v) for v in others]
+            through(n, False).start()
+        for q in range(strips):
+            load(q).wait()
+            if q >= ring:
+                store(q - ring).wait()
+            for p in range(count):
+                for e in range(8):
+                    n, x, c = (0 if e // 4 == q // 4 else 1), e % 4 // 2, e % 2
+                    wide = bw if e < 7 else sz.last
+                    value = arrived[q, c, x, p, n, :, :wide].astype(F32)
+                    leaving[q % ring, p * part : (p + 1) * part, e * bw : e * bw + wide] = value
+            store(q).start()
+            if q == 1:
+                for n in range(len(others)):
+                    through(n, False).wait()
+                    through(n, True).start()
+        for q in range(strips - ring, strips):
+            store(q).wait()
+        for n in range(len(others)):
+            through(n, True).wait()
+
+    anywhere = pl.BlockSpec(memory_space=pl.ANY)
+    dma = pltpu.SemaphoreType.DMA
     return pl.pallas_call(
         body,
-        grid=(8,),
         out_shape=[jax.ShapeDtypeStruct((hidden, hidden), F32)] + [jax.ShapeDtypeStruct(v.shape, v.dtype) for v in others],
-        in_specs=[pl.BlockSpec((2, 2, count, 2, part, bw), lambda q: (0, q // 4, q % 4, 0, 0, 0))] + specs,
-        out_specs=[pl.BlockSpec((bw, hidden), lambda q: (q, 0))] + specs,
+        in_specs=[anywhere] * (1 + len(others)),
+        out_specs=[anywhere] * (1 + len(others)),
+        scratch_shapes=[
+            pltpu.VMEM((strips, 2, 2, count, 2, part, bw), BF16),
+            pltpu.VMEM((ring, bw, hidden), F32),
+            dma((strips,)), dma((ring,)), dma((len(others),)), dma((len(others),)),
+        ] + [pltpu.VMEM(v.shape, v.dtype) for v in others],
         compiler_params=pltpu.CompilerParams(vmem_limit_bytes=60 * 2**20),
     )(pieces, *others)
 

time: 289 us -> 277 us (0.958); the launches traced: 289 us -> 274 us
  Pallas kernels: 288 us -> 273 us
    pallas_call x1, Pallas kernels: 277 us -> 263 us  [run_kernel(): pl.pallas_call(functools.partial(kernel, sz), out_shape=(frames, frames)...]
where the time goes in v6:
time: 277 us; the launch traced here: 274 us
  Pallas kernels  273 us (99%)
    pallas_call x1, Pallas kernels, run_kernel(): pl.pallas_call(functools.partial(kernel, sz), out_shape=(frames, frames)...  263 us
    pallas_call x1, Pallas kernels, place_weights(): pl.pallas_call(body, out_shape=[jax.ShapeDtypeStruct((hidden, hidden), F3...  10.1 us

profile of v6, /device:TPU:0, one launch (start us, length us, event | category | flops | bytes accessed | tf_op | source)
XLA Modules:
  0.0 273.8 jit_solution(15212346974932336509)
XLA Ops:
  0.6 263.0 %shard_map.144 = (bf16[1,2,64,2000]{3,2,1,0:T(8,128)(2,1)}, bf16[1,2,64,2000]{3,2,1,0:T(8,128)(2,1)}, f32[1,2000]{1,0:T(1,128)}, f32[1,2000]{1,0:T(1,128)}, f32[...) custom-call(bf16[1,2,64,2000]{3,2,1,0:T(8,128)(2,1)} %inp_raw.1, ...), custom_call_target="tpu_custom_call" | custom-call | tf_op jit(solution)/shard_map/pallas_call | solution.py:1239
  263.7 10.1 %shard_map.145 = (f32[2000,2000]{1,0:T(8,128)}, bf16[1,2,64,2000]{3,2,1,0:T(8,128)(2,1)}, bf16[1,2,64,2000]{3,2,1,0:T(8,128)(2,1)}, f32[1,2000]{1,0:T(1,128)}, f...) custom-call(bf16[2,4,4,2,256,256]{5,4,3,2,1,0:T(8,128)(2,1)} %get-tuple-element.21.refs_0_, ...), custom_call_target="tpu_custom_call" | custom-call | tf_op jit(solution)/shard_map/pallas_call | solution.py:1301

commit v7 on v6

--- a/solution.py
+++ b/solution.py
@@ -912,13 +912,13 @@
         def _():
             act_back(k)
 
+        @pl.when(jnp.logical_and(k >= 1, k < items + 1))
+        def _():
+            state_back(k - 1)
+
         @pl.when(k >= first_step)
         def _():
             g_step(k - first_step, False)
-
-        @pl.when(jnp.logical_and(k >= 1, k < items + 1))
-        def _():
-            state_back(k - 1)
 
         @pl.when(jnp.logical_and(k >= 2, k < items + 2))
         def _():

time: 277 us -> 276 us (level)
  no operation moved by 1% of the time
where the time goes in v7:
time: 276 us; the launch traced here: 273 us
  Pallas kernels  272 us (99%)
    pallas_call x1, Pallas kernels, run_kernel(): pl.pallas_call(functools.partial(kernel, sz), out_shape=(frames, frames)...  262 us
    pallas_call x1, Pallas kernels, place_weights(): pl.pallas_call(body, out_shape=[jax.ShapeDtypeStruct((hidden, hidden), F3...  10.1 us

profile of v7, /device:TPU:0, one launch (start us, length us, event | category | flops | bytes accessed | tf_op | source)
XLA Modules:
  0.0 273.1 jit_solution(8158442233163770624)
XLA Ops:
  0.6 262.4 %shard_map.144 = (bf16[1,2,64,2000]{3,2,1,0:T(8,128)(2,1)}, bf16[1,2,64,2000]{3,2,1,0:T(8,128)(2,1)}, f32[1,2000]{1,0:T(1,128)}, f32[1,2000]{1,0:T(1,128)}, f32[...) custom-call(bf16[1,2,64,2000]{3,2,1,0:T(8,128)(2,1)} %inp_raw.1, ...), custom_call_target="tpu_custom_call" | custom-call | tf_op jit(solution)/shard_map/pallas_call | solution.py:1239
  263.0 10.1 %shard_map.145 = (f32[2000,2000]{1,0:T(8,128)}, bf16[1,2,64,2000]{3,2,1,0:T(8,128)(2,1)}, bf16[1,2,64,2000]{3,2,1,0:T(8,128)(2,1)}, f32[1,2000]{1,0:T(1,128)}, f...) custom-call(bf16[2,4,4,2,256,256]{5,4,3,2,1,0:T(8,128)(2,1)} %get-tuple-element.21.refs_0_, ...), custom_call_target="tpu_custom_call" | custom-call | tf_op jit(solution)/shard_map/pallas_call | solution.py:1301

commit v8 on v7

--- a/solution.py
+++ b/solution.py
@@ -946,12 +946,12 @@
 
     def crosses_at(l, p, n):
         early = whole_at(l, p, n) < steps_done
-        return jnp.where(early, steps_done + 2 * p + n, whole_at(l, p, n))
+        return jnp.where(early, steps_done + 2 + 2 * p + n, whole_at(l, p, n))
 
     def cross_early(g):
-        p, n = (g - steps_done) // 2, (g - steps_done) % 2
-
-        @pl.when(p < nz)
+        p, n = (g - steps_done - 2) // 2, (g - steps_done - 2) % 2
+
+        @pl.when(jnp.logical_and(g >= steps_done + 2, p < nz))
         def _():
             for l in range(SECTIONS):
                 @pl.when(whole_at(l, p, n) < steps_done)
@@ -1109,7 +1109,7 @@
 
         return 0
 
-    lax.fori_loop(steps_done, max(steps_all + 10, steps_done + period + 26), late_step, 0)
+    lax.fori_loop(steps_done, max(steps_all + 10, steps_done + period + 28), late_step, 0)
 
     for e in range(8):
         wait_bytes(smallg.at[e], sm_rs.at[e])

time: 276 us -> 275 us (level)
  no operation moved by 1% of the time
where the time goes in v8:
time: 275 us
  Pallas kernels  274 us (100%)
    pallas_call x1, Pallas kernels, run_kernel(): pl.pallas_call(functools.partial(kernel, sz), out_shape=(frames, frames)...  264 us
    pallas_call x1, Pallas kernels, place_weights(): pl.pallas_call(body, out_shape=[jax.ShapeDtypeStruct((hidden, hidden), F3...  10.1 us

profile of v8, /device:TPU:0, one launch (start us, length us, event | category | flops | bytes accessed | tf_op | source)
XLA Modules:
  0.0 274.6 jit_solution(1864645514927418531)
XLA Ops:
  0.6 263.9 %shard_map.144 = (bf16[1,2,64,2000]{3,2,1,0:T(8,128)(2,1)}, bf16[1,2,64,2000]{3,2,1,0:T(8,128)(2,1)}, f32[1,2000]{1,0:T(1,128)}, f32[1,2000]{1,0:T(1,128)}, f32[...) custom-call(bf16[1,2,64,2000]{3,2,1,0:T(8,128)(2,1)} %inp_raw.1, ...), custom_call_target="tpu_custom_call" | custom-call | tf_op jit(solution)/shard_map/pallas_call | solution.py:1239
  264.5 10.1 %shard_map.145 = (f32[2000,2000]{1,0:T(8,128)}, bf16[1,2,64,2000]{3,2,1,0:T(8,128)(2,1)}, bf16[1,2,64,2000]{3,2,1,0:T(8,128)(2,1)}, f32[1,2000]{1,0:T(1,128)}, f...) custom-call(bf16[2,4,4,2,256,256]{5,4,3,2,1,0:T(8,128)(2,1)} %get-tuple-element.21.refs_0_, ...), custom_call_target="tpu_custom_call" | custom-call | tf_op jit(solution)/shard_map/pallas_call | solution.py:1301
